TPU v7x, 32 devices: a whole 2x2x4 slice. The times are simulated.
32 devices in a mesh: batch: 4 (over x, core), group: 8 (over z, y).
Axes of the slice: x: 2, y: 2, z: 4, core: 2. Of those that a mesh axis runs over, the one named last changes fastest.
Arguments:
- block_input: bfloat16 [2048, 50176], P('group', 'batch'), may hold values from -6 to 6
- reduce_weight: bfloat16 [2048, 1024], P('group'), may hold values from -0.1875 to 0.1875
- reduce_gain: float32 [1024], P('group'), may hold values from 0.5 to 1.5
- reduce_bias: float32 [1024], P('group'), may hold values from -3 to 3
- group_weight: bfloat16 [32, 3, 3, 32, 32], P('group'), may hold values from -0.375 to 0.375
- group_gain: float32 [1024], P('group'), may hold values from 0.5 to 1.5
- group_bias: float32 [1024], P('group'), may hold values from -3 to 3
- expand_weight: bfloat16 [2048, 1024], P('group'), may hold values from -0.25 to 0.25
- expand_gain: float32 [2048], P('group'), may hold values from 0.5 to 1.5
- expand_bias: float32 [2048], P('group'), may hold values from -3 to 3
- out_grad: bfloat16 [2048, 50176], P('group', 'batch'), may hold values from -6 to 6
Outputs:
- block_output: bfloat16 [2048, 50176], P('group', 'batch')
- input_grad: float32 [2048, 50176], P('group', 'batch')
- reduce_weight_grad: float32 [2048, 1024], P('group')
- group_weight_grad: float32 [32, 3, 3, 32, 32], P('group')
- expand_weight_grad: float32 [2048, 1024], P('group')
- reduce_gain_grad: float32 [1024], P('group')
- reduce_bias_grad: float32 [1024], P('group')
- group_gain_grad: float32 [1024], P('group')
- group_bias_grad: float32 [1024], P('group')
- expand_gain_grad: float32 [2048], P('group')
- expand_bias_grad: float32 [2048], P('group')
All inputs are finite; a program needn't handle non-finite values.
Results may differ from a plain program's by a relative error of at most 0.013.
Values may be sent and summed in bfloat16 or wider, within the bound.
A program may use at most 512 MiB of HBM per device.

v0:
```python
import jax
import jax.numpy as jnp
from jax import lax
from jax.sharding import PartitionSpec as P

GW = 32
SIDE = 14


EPS = 1e-05


def silu_slope(values):
    sigma = jax.nn.sigmoid(values)
    return sigma * (1.0 + values * (1.0 - sigma))


def normalize(values, first_sum, second_sum, count, norm_gain, norm_bias):
    center = first_sum / count
    spread = second_sum / count - center * center
    inverse = lax.rsqrt(spread + EPS)
    standard = (values - center) * inverse
    return (standard, inverse, standard * norm_gain + norm_bias)


def norm_back(upstream, standard, inverse, norm_gain, bias_sum, gain_sum, count):
    return norm_gain * inverse * (upstream - bias_sum / count - standard * (gain_sum / count))


def patch_stack(feature, groups):
    images = feature.shape[0] // (SIDE * SIDE)
    lattice = feature.reshape(images, SIDE, SIDE, groups, GW)
    padded = jnp.pad(lattice, ((0, 0), (1, 1), (1, 1), (0, 0), (0, 0)))
    return jnp.stack(
        [
            padded[:, row_off : row_off + SIDE, col_off : col_off + SIDE]
            for row_off in range(3)
            for col_off in range(3)
        ],
        axis=3,
    )


def patch_scatter(patch_grad):
    images = patch_grad.shape[0]
    groups = patch_grad.shape[4]
    padded = jnp.zeros((images, SIDE + 2, SIDE + 2, groups, GW), jnp.float32)
    for row_off in range(3):
        for col_off in range(3):
            padded = padded.at[:, row_off : row_off + SIDE, col_off : col_off + SIDE].add(
                patch_grad[:, :, :, row_off * 3 + col_off]
            )
    return padded[:, 1 : SIDE + 1, 1 : SIDE + 1].reshape(images * SIDE * SIDE, groups * GW)


def local(
    block_input,
    reduce_weight,
    reduce_gain,
    reduce_bias,
    group_weight,
    group_gain,
    group_bias,
    expand_weight,
    expand_gain,
    expand_bias,
    out_grad,
):
    pixels = block_input.shape[1]
    count = pixels * lax.axis_size("batch")
    local_mid = reduce_gain.shape[0]
    groups = group_weight.shape[0]
    reduced = lax.psum_scatter(
        lax.dot_general(
            reduce_weight, block_input, (((0,), (0,)), ((), ())), preferred_element_type=jnp.float32
        ),
        "group",
        scatter_dimension=0,
        tiled=True,
    ).T
    reduce_sums = lax.psum((jnp.sum(reduced, 0), jnp.sum(reduced * reduced, 0)), "batch")
    reduce_std, reduce_inv, reduce_norm = normalize(
        reduced, reduce_sums[0], reduce_sums[1], count, reduce_gain, reduce_bias
    )
    entered = jax.nn.silu(reduce_norm).astype(jnp.bfloat16)
    patches = patch_stack(entered, groups)
    kernel = group_weight.reshape(groups, 9, GW, GW)
    grouped = jnp.einsum(
        "nhwtgi,gtio->nhwgo", patches, kernel, preferred_element_type=jnp.float32
    ).reshape(pixels, local_mid)
    group_sums = lax.psum((jnp.sum(grouped, 0), jnp.sum(grouped * grouped, 0)), "batch")
    group_std, group_inv, group_norm = normalize(
        grouped, group_sums[0], group_sums[1], count, group_gain, group_bias
    )
    activated = jax.nn.silu(group_norm).astype(jnp.bfloat16)
    gathered = lax.all_gather(activated, "group", axis=1, tiled=True)
    expanded = lax.dot_general(
        expand_weight, gathered, (((1,), (1,)), ((), ())), preferred_element_type=jnp.float32
    )
    expand_sums = lax.psum((jnp.sum(expanded, 1), jnp.sum(expanded * expanded, 1)), "batch")
    expand_std, expand_inv, expand_norm = normalize(
        expanded,
        expand_sums[0][:, None],
        expand_sums[1][:, None],
        count,
        expand_gain[:, None],
        expand_bias[:, None],
    )
    summed_pre = expand_norm + block_input.astype(jnp.float32)
    block_output = jax.nn.silu(summed_pre).astype(jnp.bfloat16)
    upstream = out_grad.astype(jnp.float32) * silu_slope(summed_pre)
    expand_stats = lax.psum((jnp.sum(upstream, 1), jnp.sum(upstream * expand_std, 1)), "batch")
    expand_back = norm_back(
        upstream,
        expand_std,
        expand_inv,
        expand_gain[:, None],
        expand_stats[0][:, None],
        expand_stats[1][:, None],
        count,
    ).astype(jnp.bfloat16)
    expand_weight_part = jnp.dot(expand_back, gathered, preferred_element_type=jnp.float32)
    activated_grad = lax.psum_scatter(
        lax.dot_general(
            expand_weight, expand_back, (((0,), (0,)), ((), ())), preferred_element_type=jnp.float32
        ),
        "group",
        scatter_dimension=0,
        tiled=True,
    ).T
    group_up = activated_grad * silu_slope(group_norm)
    group_stats = lax.psum(
        (jnp.sum(group_up, 0), jnp.sum(group_up * group_std, 0), expand_weight_part), "batch"
    )
    group_back = norm_back(
        group_up, group_std, group_inv, group_gain, group_stats[0], group_stats[1], count
    ).astype(jnp.bfloat16)
    back_grid = group_back.reshape(patches.shape[0], SIDE, SIDE, groups, GW)
    kernel_part = jnp.einsum(
        "nhwtgi,nhwgo->gtio", patches, back_grid, preferred_element_type=jnp.float32
    )
    patch_grad = jnp.einsum(
        "nhwgo,gtio->nhwtgi", back_grid, kernel, preferred_element_type=jnp.float32
    )
    entered_grad = patch_scatter(patch_grad)
    reduce_up = entered_grad * silu_slope(reduce_norm)
    reduce_stats = lax.psum(
        (jnp.sum(reduce_up, 0), jnp.sum(reduce_up * reduce_std, 0), kernel_part), "batch"
    )
    reduce_back = norm_back(
        reduce_up, reduce_std, reduce_inv, reduce_gain, reduce_stats[0], reduce_stats[1], count
    ).astype(jnp.bfloat16)
    whole_grad = lax.all_gather(reduce_back, "group", axis=1, tiled=True)
    input_grad = upstream + lax.dot_general(
        reduce_weight, whole_grad, (((1,), (1,)), ((), ())), preferred_element_type=jnp.float32
    )
    reduce_weight_part = jnp.dot(block_input, whole_grad, preferred_element_type=jnp.float32)
    reduce_weight_grad = lax.psum(reduce_weight_part.astype(jnp.bfloat16), "batch").astype(
        jnp.float32
    )
    return (
        block_output,
        input_grad,
        reduce_weight_grad,
        reduce_stats[2].reshape(group_weight.shape),
        group_stats[2],
        reduce_stats[1],
        reduce_stats[0],
        group_stats[1],
        group_stats[0],
        expand_stats[1],
        expand_stats[0],
    )


def solution(mesh):
    in_specs = (
        P("group", "batch"),
        P("group", None),
        P("group"),
        P("group"),
        P("group", None, None, None, None),
        P("group"),
        P("group"),
        P("group", None),
        P("group"),
        P("group"),
        P("group", "batch"),
    )
    out_specs = (
        P("group", "batch"),
        P("group", "batch"),
        P("group", None),
        P("group", None, None, None, None),
        P("group", None),
        P("group"),
        P("group"),
        P("group"),
        P("group"),
        P("group"),
        P("group"),
    )
    return jax.shard_map(local, mesh=mesh, in_specs=in_specs, out_specs=out_specs, check_vma=False)
```

profile of v0, /device:TPU:25, one launch (start us, length us, event | category | flops | bytes accessed | tf_op | source)
XLA Modules:
  0.0 3353.6 jit_solution(8610833158973118400)
XLA Ops:
  7.2 22.7 fusion.59
  30.0 804.8 %reduce-scatter.3.cloned.1.call-done = f32[128,12544]{1,0:T(8,128)} async-done(((f32[1024,12544]{1,0:T(8,128)}), f32[128,12544]{1,0:T(8,128)}) %reduce-scatter.3.cloned.1.call-update) | async-done | bytes 6422544 | tf_op jit(solution)/shard_map/reduce_scatter | solution.py:73
  838.4 5.8 all-reduce.7
  845.2 5.3 multiply_convert_fusion.3
  850.5 5.6 copy.51
  856.1 17.0 reshape.495
  873.1 17.1 stack.34
  890.2 20.0 copy.52
  910.2 7.3 fusion.27
  922.0 4.6 fusion.31
  926.6 4.6 fusion.33
  931.2 20.5 copy.58
  951.7 6.9 constant_dynamic-update-slice_fusion
  958.6 7.5 fusion.35
  966.1 4.6 fusion.37
  970.7 4.8 fusion.39
  975.5 4.7 fusion.41
  980.2 26.8 fusion.53
  1007.1 24.1 copy.63
  1031.2 19.9 reshape.497
  1051.1 8.0 copy.64
  1059.1 7.0 all-reduce.6
  1066.1 5.3 multiply_convert_fusion.2
  1071.5 10.0 copy.65
  1081.5 9.8 copy.66
  1091.2 471.2 %all-gather.3.cloned.1.call-done = bf16[12544,1024]{0,1:T(8,128)(2,1)} async-done(((bf16[12544,128]{0,1:T(8,128)(2,1)}), bf16[12544,1024]{0,1:T(8,128)(2,1)}) %all-gather.3.cloned.1.call-update) | async-done | bytes 25690128 | tf_op jit(solution)/shard_map/all_gather | solution.py:96
  1562.4 14.6 fusion.52
  1577.0 5.4 all-reduce.5
  1582.5 20.1 fusion.51
  1602.7 6.8 all-reduce.4
  1609.5 9.6 fusion.25
  1621.7 18.7 convolution_bitcast_fusion.1
  1642.4 801.2 %reduce-scatter.5.cloned.1.call-done = f32[128,12544]{1,0:T(8,128)} async-done(((f32[1024,12544]{1,0:T(8,128)}), f32[128,12544]{1,0:T(8,128)}) %reduce-scatter.5.cloned.1.call-update) | async-done | bytes 6422544 | tf_op jit(solution)/shard_map/reduce_scatter | solution.py:123
  2443.6 8.4 fusion.55
  2452.0 5.7 all-reduce.3
  2457.6 8.4 multiply_convert_fusion.1
  2466.0 5.6 copy.68
  2471.6 17.0 reshape.498
  2488.6 43.4 %convolution_bitcast_fusion = f32[64,14,14,9,4,32]{0,5,3,2,1,4:T(8,128)} fusion(bf16[4,9,32,32,1,1]{3,2,1,5,4,0:T(8,128)(2,1)S(1)} %bitcast.207, bf16[64,14,14,4,32,1]{4,3,2,1,0,5:T(4,128)(2,1)} %bitcast.203), kind=kOutput, calls=%fused_computation.2 | convolution fusion | flops 924844032 | bytes 61087744 | tf_op jit(solution)/shard_map/nhwgo,gtio->nhwtgi/dot_general | solution.py:142
  2532.0 12.0 slice_bitcast_fusion.8
  2544.1 13.9 scatter-add.30
  2557.9 14.7 fusion.17
  2572.6 15.8 fusion.3
  2588.4 13.4 fusion.15
  2601.8 13.4 fusion.13
  2615.2 13.4 fusion.11
  2628.6 13.4 fusion.9
  2642.0 13.4 fusion.7
  2655.4 13.4 fusion.5
  2668.8 12.1 slice.452
  2680.9 24.1 copy.78
  2704.9 19.9 reshape.511
  2724.8 8.1 copy.79
  2732.9 8.4 fusion.54
  2741.3 7.1 all-reduce.2
  2748.5 8.5 fusion.46
  2757.1 9.7 copy.82
  2766.8 14.8 fusion.60
  2781.5 466.5 %all-gather.5.cloned.1.call-done = bf16[12544,1024]{0,1:T(8,128)(2,1)} async-done(((bf16[12544,128]{0,1:T(8,128)(2,1)}), bf16[12544,1024]{0,1:T(8,128)(2,1)}) %all-gather.5.cloned.1.call-update) | async-done | bytes 25690128 | tf_op jit(solution)/shard_map/all_gather | solution.py:153
  3248.0 14.3 fusion.47
  3262.4 25.0 fusion
  3288.3 20.7 fusion.2
  3309.0 14.2 copy.83
  3325.5 16.8 all-reduce.14.cloned.1.call-done
  (91 shorter events, 21.6 us)
Async XLA Ops:
  7.2 1555.2 %copy-start = (bf16[256,1024]{1,0:T(8,128)(2,1)S(1)}, bf16[256,1024]{1,0:T(8,128)(2,1)}, u32[]{:S(2)}) copy-start(bf16[256,1024]{1,0:T(8,128)(2,1)} %param.36) | copy-start | bytes 1572868
  7.2 827.6 %reduce-scatter.3.cloned.1.call-start = ((), (), s32[]{:S(2)}) async-start(), calls=%async_computation.2 | async-start | bytes 57802752 | tf_op jit(solution)/shard_map/reduce_scatter | solution.py:73
  30.0 814.2 %copy-start.11 = (f32[128]{0:T(128)S(1)}, f32[128]{0:T(128)}, u32[]{:S(2)}) copy-start(f32[128]{0:T(128)} %param.31) | copy-start | bytes 1540
  30.0 815.3 %copy-start.16 = (f32[128]{0:T(128)S(1)}, f32[128]{0:T(128)}, u32[]{:S(2)}) copy-start(f32[128]{0:T(128)} %param.32) | copy-start | bytes 1540
  30.0 1532.4 %all-gather.3.cloned.1.call-start = ((), (), s32[]{:S(2)}) async-start(), calls=%async_computation.3 | async-start | bytes 28901376 | tf_op jit(solution)/shard_map/all_gather | solution.py:96
  844.7 0.5 copy-start.6
  844.7 0.5 copy-start.8
  910.2 7.3 copy-start.2
  951.7 14.4 slice-start
  958.6 7.5 slice-start.1
  970.7 9.5 copy-start.5
  1051.1 15.0 copy-start.10
  1051.1 15.0 copy-start.15
  1071.4 1372.1 %reduce-scatter.5.cloned.1.call-start = ((), (), s32[]{:S(2)}) async-start(), calls=%async_computation.4 | async-start | bytes 57802752 | tf_op jit(solution)/shard_map/reduce_scatter | solution.py:123
  1091.2 491.3 %copy-start.13 = (f32[256]{0:T(256)S(1)}, f32[256]{0:T(256)}, u32[]{:S(2)}) copy-start(f32[256]{0:T(256)} %param.37) | copy-start | bytes 3076
  1091.2 491.3 %copy-start.18 = (f32[256]{0:T(256)S(1)}, f32[256]{0:T(256)}, u32[]{:S(2)}) copy-start(f32[256]{0:T(256)} %param.38) | copy-start | bytes 3076
  1609.5 9.6 copy-start.19
  1609.5 9.6 copy-start.20
  1619.1 2.6 copy-start.3
  1640.4 1.3 copy-start.21
  1640.4 1607.6 %all-gather.5.cloned.1.call-start = ((), (), s32[]{:S(2)}) async-start(), calls=%async_computation.5 | async-start | bytes 28901376 | tf_op jit(solution)/shard_map/all_gather | solution.py:153
  2457.6 31.0 copy-start.22
  2457.6 31.0 copy-start.23
  2724.8 8.1 copy-start.7
  2724.8 8.1 copy-start.9
  2724.8 8.1 copy-start.12
  2724.8 8.1 copy-start.17
  2732.9 15.6 copy-start.14
  2748.4 18.3 copy-start.24
  2748.4 18.3 copy-start.25
  2757.0 566.2 %all-reduce.12.cloned.1.call-start = ((), (), s32[]{:S(2)}) async-start(), calls=%async_computation.6 | async-start | bytes 1048576 | tf_op jit(solution)/shard_map/psum | solution.py:158
  3262.4 25.9 copy-start.4
  3262.4 79.9 %all-reduce.14.cloned.1.call-start = ((), (), s32[]{:S(2)}) async-start(), calls=%async_computation.7 | async-start | bytes 3276800 | tf_op jit(solution)/shard_map/psum | solution.py:147
  3288.3 58.2 %copy-start.1 = (bf16[256,1024]{1,0:T(8,128)(2,1)S(1)}, bf16[256,1024]{1,0:T(8,128)(2,1)}, u32[]{:S(2)}) copy-start(bf16[256,1024]{1,0:T(8,128)(2,1)} %param.36) | copy-start | bytes 1572868
Sparse Core Ops, SparseCore 0:
  30.1 804.6 reduce-scatter.2
  1071.6 490.8 all-gather.2
  1640.5 802.9 reduce-scatter.4
  2757.1 490.8 all-gather.4
  3262.5 32.0 all-reduce.11
  3297.4 44.8 all-reduce.13
where the time goes:
time: 3360 us; the launch traced here: 3350 us
  waiting for transfers between devices  2560 us (76%)
  local copies, waits for them, and re-layouts  350 us (10%)
  matrix products  201 us (6%)
  other arithmetic  190 us (6%)
  blocking collectives  37.8 us (1%)
    reduce_scatter x1, waiting for transfers between devices, local(): lax.psum_scatter(lax.dot_general(reduce_weight, block_input, (((0,), (0,)...  805 us
    reduce_scatter x1, waiting for transfers between devices, local(): lax.psum_scatter(lax.dot_general(expand_weight, expand_back, (((0,), (0,)...  801 us
    all_gather x1, waiting for transfers between devices, local(): gathered = lax.all_gather(activated, 'group', axis=1, tiled=True)  471 us
    all_gather x1, waiting for transfers between devices, local(): whole_grad = lax.all_gather(reduce_back, 'group', axis=1, tiled=True)  466 us
    scatter-add x8, other arithmetic, patch_scatter(): padded.at[:, row_off:row_off + SIDE, col_off:col_off + SIDE]  111 us
    unnamed x71, local copies, waits for them, and re-layouts  98 us
  transfers between devices with their start and end apart: 6, of which 5 were waited for; matrix products, arithmetic and copies ran while one was open for 3% of the time, Pallas kernels for 0%

commit v1 on v0

v1 whole, which is shorter than its diff:
```python
import functools

import jax
import jax.numpy as jnp
from jax import lax
from jax.experimental import pallas as pl
from jax.experimental.pallas import tpu as pltpu
from jax.sharding import PartitionSpec as P

GW = 32
SIDE = 14
EPS = 1e-05
BLK = 256
HALF = 128
PAD = 16
F32 = jnp.float32
BF16 = jnp.bfloat16
MESH = pl.DeviceIdType.MESH
VMEM_LIMIT = 60 * 1024 * 1024


def silu_slope(values):
    sigma = jax.nn.sigmoid(values)
    return sigma * (1.0 + values * (1.0 - sigma))


def row_chunk(pixels):
    return 224 if pixels % 224 == 0 else pixels


def over_rows(pixels, body):
    size = row_chunk(pixels)
    if size == pixels:
        body(0, size)
    else:

        @pl.loop(0, pixels // size)
        def _(step):
            body(pl.multiple_of(step * size, 16), size)


def coefficients(sums, params, count):
    center = sums[0:1] / count
    spread = sums[1:2] / count - center * center
    inverse = lax.rsqrt(spread + EPS)
    return center, inverse, params[0:1], params[1:2]


def standardize(values, coef):
    standard = (values - coef[0]) * coef[1]
    return standard, standard * coef[2] + coef[3]


def add_stats(ref, first, second):
    ref[0, 0:1] += jnp.sum(first, 0, keepdims=True)
    ref[0, 1:2] += jnp.sum(second, 0, keepdims=True)


def dot(a, b, dims=((1,), (0,))):
    return lax.dot_general(a, b, (dims, ((), ())), preferred_element_type=F32)


def call(kernel, grid, in_specs, out_specs, out_shape, scratch, flops):
    return pl.pallas_call(
        kernel,
        grid=grid,
        in_specs=in_specs,
        out_specs=out_specs,
        out_shape=out_shape,
        scratch_shapes=scratch,
        compiler_params=pltpu.CompilerParams(vmem_limit_bytes=VMEM_LIMIT),
        cost_estimate=pl.CostEstimate(flops=flops, bytes_accessed=20_000_000, transcendentals=0),
    )


def shape(dims, dtype=F32):
    return jax.ShapeDtypeStruct(dims, dtype)


def block(*dims):
    return pl.BlockSpec((1,) + dims, lambda j: (j,) + (0,) * len(dims))


def whole(*dims):
    return pl.BlockSpec(dims, lambda j: (0,) * len(dims))


def reduce_kernel(x_ref, w_ref, out_ref, sum_ref):
    sum_ref[...] = jnp.zeros_like(sum_ref)

    def body(start, size):
        rows = pl.ds(start, size)
        total = dot(x_ref[0, rows], w_ref[0])
        for source in range(1, x_ref.shape[0]):
            total += dot(x_ref[source, rows], w_ref[source])
        out_ref[0, rows] = total
        add_stats(sum_ref, total, total * total)

    over_rows(x_ref.shape[1], body)


def reduce_product(x, weight):
    blocks, pixels, _ = x.shape
    mids = weight.shape[2] // BLK
    return call(
        reduce_kernel,
        (mids,),
        [whole(blocks, pixels, BLK), pl.BlockSpec((blocks, BLK, BLK), lambda j: (0, 0, j))],
        [block(pixels, BLK), block(2, BLK)],
        [shape((mids, pixels, BLK)), shape((mids, 2, BLK))],
        [],
        2 * pixels * blocks * BLK * mids * BLK,
    )(x, weight)


def spread_weight(compact_ref, dense_ref):
    cols = lax.broadcasted_iota(jnp.int32, (GW, BLK), 1)
    rows = lax.broadcasted_iota(jnp.int32, (GW, BLK), 0)
    tile = jnp.where(cols % GW == rows, 1.0, 0.0).astype(BF16)
    own = lax.broadcasted_iota(jnp.int32, (BLK, BLK), 0) // GW == lax.broadcasted_iota(jnp.int32, (BLK, BLK), 1) // GW

    @pl.loop(0, 9)
    def _(tap):
        dense_ref[tap] = jnp.where(own, dot(compact_ref[0, tap], tile), 0.0).astype(BF16)


def twice(mask):
    return jnp.concatenate([mask, mask], 1)


def fill(stack_ref, mask_ref, rows_start, size, values):
    rows = pl.ds(rows_start, size)
    target = pl.ds(rows_start + PAD, size)
    for half in range(2):
        part = values[:, half * HALF : (half + 1) * HALF]
        stack_ref[1, half, target] = part
        stack_ref[0, half, target] = part * mask_ref[1, rows]
        stack_ref[2, half, target] = part * mask_ref[0, rows]


def clear_edges(stack_ref, pixels):
    edge = jnp.zeros(stack_ref.shape[:2] + (PAD, HALF), F32)
    stack_ref[:, :, 0:PAD] = edge
    stack_ref[:, :, PAD + pixels : PAD + pixels + PAD] = edge


def window(stack_ref, start, size, row_off, col_off):
    rows = pl.ds(start + (PAD + row_off * SIDE + col_off), size)
    return jnp.concatenate([stack_ref[col_off + 1, half, rows] for half in range(2)], 1).astype(BF16)


def conv_rows(stack_ref, mask_ref, dense_ref, start, size):
    rows = pl.ds(start, size)
    total = None
    for row_off in (-1, 0, 1):
        part = None
        for col_off in (-1, 0, 1):
            term = dot(
                window(stack_ref, start, size, row_off, col_off), dense_ref[(row_off + 1) * 3 + col_off + 1]
            )
            part = term if part is None else part + term
        if row_off:
            part = part * twice(mask_ref[2 if row_off < 0 else 3, rows])
        total = part if total is None else total + part
    return total


def conv_kernel(count, red_ref, sums_ref, prm_ref, weight_ref, mask_ref, out_ref, stat_ref, stack_ref, dense_ref):
    pixels = red_ref.shape[1]
    spread_weight(weight_ref, dense_ref)
    clear_edges(stack_ref, pixels)
    coef = coefficients(sums_ref[0], prm_ref[0], count)

    def enter(start, size):
        _, norm = standardize(red_ref[0, pl.ds(start, size)], coef)
        fill(stack_ref, mask_ref, start, size, (norm * jax.nn.sigmoid(norm)).astype(BF16).astype(F32))

    over_rows(pixels, enter)
    stat_ref[...] = jnp.zeros_like(stat_ref)

    def body(start, size):
        total = conv_rows(stack_ref, mask_ref, dense_ref, start, size)
        out_ref[0, pl.ds(start, size)] = total
        add_stats(stat_ref, total, total * total)

    over_rows(pixels, body)


def conv(reduced, sums, params, weight, masks, count):
    mids, pixels, _ = reduced.shape
    return call(
        functools.partial(conv_kernel, count),
        (mids,),
        [
            block(pixels, BLK),
            block(2, BLK),
            block(2, BLK),
            block(9, BLK, GW),
            whole(4, pixels, HALF),
        ],
        [block(pixels, BLK), block(2, BLK)],
        [shape((mids, pixels, BLK)), shape((mids, 2, BLK))],
        [pltpu.VMEM((3, 2, pixels + 2 * PAD, HALF), F32), pltpu.VMEM((9, BLK, BLK), BF16)],
        2 * 9 * pixels * mids * BLK * BLK,
    )(reduced, sums, params, weight, masks)


def conv_back_kernel(
    count,
    red_ref,
    sums_ref,
    prm_ref,
    grp_ref,
    gsums_ref,
    gprm_ref,
    up_ref,
    upsums_ref,
    weight_ref,
    mask_ref,
    out_ref,
    stat_ref,
    wgrad_ref,
    stack_ref,
    dense_ref,
    back_ref,
):
    pixels = red_ref.shape[1]
    spread_weight(weight_ref, dense_ref)
    clear_edges(stack_ref, pixels)
    coef = coefficients(sums_ref[0], prm_ref[0], count)
    gcoef = coefficients(gsums_ref[0], gprm_ref[0], count)
    scale = gcoef[2] * gcoef[1]
    up_mean = upsums_ref[0, 0:1] / count
    up_lean = upsums_ref[0, 1:2] / count

    def back(start, size):
        rows = pl.ds(start, size)
        standard, _ = standardize(grp_ref[0, rows], gcoef)
        values = (scale * (up_ref[0, rows] - up_mean - standard * up_lean)).astype(BF16)
        back_ref[1, rows] = values
        values = values.astype(F32)
        back_ref[0, rows] = (values * twice(mask_ref[2, rows])).astype(BF16)
        back_ref[2, rows] = (values * twice(mask_ref[3, rows])).astype(BF16)
        fill(stack_ref, mask_ref, start, size, values)

    over_rows(pixels, back)
    stat_ref[...] = jnp.zeros_like(stat_ref)

    def body(start, size):
        rows = pl.ds(start, size)
        standard, norm = standardize(red_ref[0, rows], coef)
        up = conv_rows(stack_ref, mask_ref, dense_ref, start, size) * silu_slope(norm)
        out_ref[0, rows] = up
        add_stats(stat_ref, up, up * standard)

    over_rows(pixels, body)

    def enter(start, size):
        _, norm = standardize(red_ref[0, pl.ds(start, size)], coef)
        fill(stack_ref, mask_ref, start, size, (norm * jax.nn.sigmoid(norm)).astype(BF16).astype(F32))

    over_rows(pixels, enter)
    own = lax.broadcasted_iota(jnp.int32, (BLK, BLK), 0) // GW == lax.broadcasted_iota(jnp.int32, (BLK, BLK), 1) // GW
    for row_off in (-1, 0, 1):
        for col_off in (-1, 0, 1):
            full = dot(
                back_ref[row_off + 1], window(stack_ref, 0, pixels, row_off, col_off), ((0,), (0,))
            )
            full = jnp.where(own, full, 0.0)
            kept = full[:, 0:GW]
            for group in range(1, BLK // GW):
                kept += full[:, group * GW : (group + 1) * GW]
            wgrad_ref[0, (row_off + 1) * 3 + col_off + 1] = kept


def conv_back(reduced, sums, params, grouped, gsums, gparams, up, upsums, weight, masks, count):
    mids, pixels, _ = reduced.shape
    return call(
        functools.partial(conv_back_kernel, count),
        (mids,),
        [
            block(pixels, BLK),
            block(2, BLK),
            block(2, BLK),
            block(pixels, BLK),
            block(2, BLK),
            block(2, BLK),
            block(pixels, BLK),
            block(2, BLK),
            block(9, BLK, GW),
            whole(4, pixels, HALF),
        ],
        [block(pixels, BLK), block(2, BLK), block(9, BLK, GW)],
        [shape((mids, pixels, BLK)), shape((mids, 2, BLK)), shape((mids, 9, BLK, GW))],
        [
            pltpu.VMEM((3, 2, pixels + 2 * PAD, HALF), F32),
            pltpu.VMEM((9, BLK, BLK), BF16),
            pltpu.VMEM((3, pixels, BLK), BF16),
        ],
        4 * 9 * pixels * mids * BLK * BLK,
    )(reduced, sums, params, grouped, gsums, gparams, up, upsums, weight, masks)


def expand_kernel(count, grp_ref, gsums_ref, gprm_ref, w_ref, out_ref, sum_ref, act_ref):
    mids, pixels, _ = grp_ref.shape

    @pl.when(pl.program_id(0) == 0)
    def _():
        for mid in range(mids):
            coef = coefficients(gsums_ref[mid], gprm_ref[mid], count)

            def body(start, size):
                rows = pl.ds(start, size)
                _, norm = standardize(grp_ref[mid, rows], coef)
                act_ref[rows, mid * BLK : (mid + 1) * BLK] = (norm * jax.nn.sigmoid(norm)).astype(BF16)

            over_rows(pixels, body)

    sum_ref[...] = jnp.zeros_like(sum_ref)

    def product(start, size):
        rows = pl.ds(start, size)
        total = dot(act_ref[rows], w_ref[0], ((1,), (1,)))
        out_ref[0, rows] = total
        add_stats(sum_ref, total, total * total)

    over_rows(pixels, product)


def expand_product(grouped, gsums, gparams, weight, count):
    mids, pixels, _ = grouped.shape
    blocks = weight.shape[0]
    return call(
        functools.partial(expand_kernel, count),
        (blocks,),
        [
            whole(mids, pixels, BLK),
            whole(mids, 2, BLK),
            whole(mids, 2, BLK),
            block(BLK, mids * BLK),
        ],
        [block(pixels, BLK), block(2, BLK), whole(pixels, mids * BLK)],
        [shape((blocks, pixels, BLK)), shape((blocks, 2, BLK)), shape((pixels, mids * BLK), BF16)],
        [],
        2 * pixels * blocks * BLK * mids * BLK,
    )(grouped, gsums, gparams, weight)


def output_kernel(count, exp_ref, sums_ref, prm_ref, x_ref, grad_ref, out_ref, up_ref, stat_ref):
    coef = coefficients(sums_ref[0], prm_ref[0], count)
    stat_ref[...] = jnp.zeros_like(stat_ref)

    def body(start, size):
        rows = pl.ds(start, size)
        standard, norm = standardize(exp_ref[0, rows], coef)
        summed = norm + x_ref[0, rows].astype(F32)
        sigma = jax.nn.sigmoid(summed)
        out_ref[0, rows] = (summed * sigma).astype(BF16)
        up = grad_ref[0, rows].astype(F32) * (sigma * (1.0 + summed * (1.0 - sigma)))
        up_ref[0, rows] = up
        add_stats(stat_ref, up, up * standard)

    over_rows(exp_ref.shape[1], body)


def output(expanded, sums, params, x, grad, count):
    blocks, pixels, _ = expanded.shape
    return call(
        functools.partial(output_kernel, count),
        (blocks,),
        [block(pixels, BLK), block(2, BLK), block(2, BLK), block(pixels, BLK), block(pixels, BLK)],
        [block(pixels, BLK), block(pixels, BLK), block(2, BLK)],
        [shape((blocks, pixels, BLK), BF16), shape((blocks, pixels, BLK)), shape((blocks, 2, BLK))],
        [],
        20 * pixels * blocks * BLK,
    )(expanded, sums, params, x, grad)


def expand_back_kernel(
    count,
    exp_ref,
    sums_ref,
    prm_ref,
    up_ref,
    upsums_ref,
    w_ref,
    grp_ref,
    gsums_ref,
    gprm_ref,
    back_ref,
    out_ref,
    stat_ref,
    keep_ref,
):
    blocks, pixels, _ = keep_ref.shape
    step = pl.program_id(0)

    @pl.when(step < blocks)
    def _():
        coef = coefficients(sums_ref[0], prm_ref[0], count)
        scale = coef[2] * coef[1]
        up_mean = upsums_ref[0, 0:1] / count
        up_lean = upsums_ref[0, 1:2] / count

        def back(start, size):
            rows = pl.ds(start, size)
            standard, _ = standardize(exp_ref[0, rows], coef)
            values = (scale * (up_ref[0, rows] - up_mean - standard * up_lean)).astype(BF16)
            back_ref[0, rows] = values
            keep_ref[step, rows] = values

        over_rows(pixels, back)

    @pl.when(step >= blocks)
    def _():
        coef = coefficients(gsums_ref[0], gprm_ref[0], count)
        stat_ref[...] = jnp.zeros_like(stat_ref)

        def body(start, size):
            rows = pl.ds(start, size)
            total = dot(keep_ref[0, rows], w_ref[0])
            for source in range(1, blocks):
                total += dot(keep_ref[source, rows], w_ref[source])
            standard, norm = standardize(grp_ref[0, rows], coef)
            up = total * silu_slope(norm)
            out_ref[0, rows] = up
            add_stats(stat_ref, up, up * standard)

        over_rows(pixels, body)


def expand_back(expanded, sums, params, up, upsums, weight, grouped, gsums, gparams, count):
    blocks, pixels, _ = expanded.shape
    mids = grouped.shape[0]

    def first(*dims):
        return pl.BlockSpec((1,) + dims, lambda j: (jnp.minimum(j, blocks - 1),) + (0,) * len(dims))

    def second(*dims):
        return pl.BlockSpec((1,) + dims, lambda j: (jnp.maximum(j - blocks, 0),) + (0,) * len(dims))

    return call(
        functools.partial(expand_back_kernel, count),
        (blocks + mids,),
        [
            first(pixels, BLK),
            first(2, BLK),
            first(2, BLK),
            first(pixels, BLK),
            first(2, BLK),
            pl.BlockSpec((blocks, BLK, BLK), lambda j: (0, 0, jnp.maximum(j - blocks, 0))),
            second(pixels, BLK),
            second(2, BLK),
            second(2, BLK),
        ],
        [first(pixels, BLK), second(pixels, BLK), second(2, BLK)],
        [shape((blocks, pixels, BLK), BF16), shape((mids, pixels, BLK)), shape((mids, 2, BLK))],
        [pltpu.VMEM((blocks, pixels, BLK), BF16)],
        2 * pixels * blocks * BLK * mids * BLK,
    )(expanded, sums, params, up, upsums, weight, grouped, gsums, gparams)


def weight_grad_kernel(left_ref, right_ref, out_ref):
    for first in range(0, right_ref.shape[1], BLK):
        columns = slice(first, first + BLK)
        out_ref[0, :, columns] = dot(left_ref[0], right_ref[:, columns], ((0,), (0,))).astype(BF16)


def weight_grad(left, right):
    blocks, pixels, _ = left.shape
    width = right.shape[1]
    return call(
        weight_grad_kernel,
        (blocks,),
        [block(pixels, BLK), whole(pixels, width)],
        [block(BLK, width)],
        [shape((blocks, BLK, width), BF16)],
        [],
        2 * pixels * blocks * BLK * width,
    )(left, right)[0]


def reduce_back_kernel(count, red_ref, sums_ref, prm_ref, rup_ref, rupsums_ref, x_ref, up_ref, w_ref, grad_ref, wgrad_ref, back_ref):
    mids, pixels, _ = red_ref.shape

    @pl.when(pl.program_id(0) == 0)
    def _():
        for mid in range(mids):
            coef = coefficients(sums_ref[mid], prm_ref[mid], count)
            scale = coef[2] * coef[1]
            up_mean = rupsums_ref[mid, 0:1] / count
            up_lean = rupsums_ref[mid, 1:2] / count

            def body(start, size):
                rows = pl.ds(start, size)
                standard, _ = standardize(red_ref[mid, rows], coef)
                values = scale * (rup_ref[mid, rows] - up_mean - standard * up_lean)
                back_ref[rows, mid * BLK : (mid + 1) * BLK] = values.astype(BF16)

            over_rows(pixels, body)

    def product(start, size):
        rows = pl.ds(start, size)
        total = dot(back_ref[rows], w_ref[0], ((1,), (1,)))
        grad_ref[0, rows] = (up_ref[0, rows] + total).astype(BF16)

    over_rows(pixels, product)
    for mid in range(mids):
        columns = slice(mid * BLK, (mid + 1) * BLK)
        wgrad_ref[0, :, columns] = dot(x_ref[0], back_ref[:, columns], ((0,), (0,))).astype(BF16)


def reduce_back(reduced, sums, params, rup, rupsums, x, up, weight, count):
    mids, pixels, _ = reduced.shape
    blocks = x.shape[0]
    return call(
        functools.partial(reduce_back_kernel, count),
        (blocks,),
        [
            whole(mids, pixels, BLK),
            whole(mids, 2, BLK),
            whole(mids, 2, BLK),
            whole(mids, pixels, BLK),
            whole(mids, 2, BLK),
            block(pixels, BLK),
            block(pixels, BLK),
            block(BLK, mids * BLK),
        ],
        [block(pixels, BLK), block(BLK, mids * BLK)],
        [shape((blocks, pixels, BLK), BF16), shape((blocks, BLK, mids * BLK), BF16)],
        [pltpu.VMEM((pixels, mids * BLK), BF16)],
        4 * pixels * blocks * BLK * mids * BLK,
    )(reduced, sums, params, rup, rupsums, x, up, weight)


def exchange_kernel(batches, members, x_ref, out_ref, first_ref, second_ref, mid_ref, send1, recv1, send2, recv2):
    row, me = lax.axis_index("batch"), lax.axis_index("group")
    across = [(lax.rem(row + step, batches), me) for step in range(1, batches)]
    along = [(row, lax.rem(me + step, members)) for step in range(1, members)]
    barrier = pltpu.get_barrier_semaphore()
    for device in across + along:
        pl.semaphore_signal(barrier, inc=1, device_id=device, device_id_type=MESH)
    pl.semaphore_wait(barrier, len(across) + len(along))

    def spread(source, target, send, recv, devices):
        copies = []
        for step, device in enumerate(devices):
            copy = pltpu.make_async_remote_copy(
                src_ref=source,
                dst_ref=target.at[step],
                send_sem=send.at[step],
                recv_sem=recv.at[step],
                device_id=device,
                device_id_type=MESH,
            )
            copy.start()
            copies.append(copy)
        for copy in copies:
            copy.wait()

    spread(x_ref, first_ref, send1, recv1, across)
    total = x_ref[...]
    for step in range(batches - 1):
        total += first_ref[step]
    mid_ref[...] = total
    spread(mid_ref, second_ref, send2, recv2, along)
    for step in range(members - 1):
        total += second_ref[step]
    out_ref[...] = total


def exchange(values, batches, members, collective_id):
    return pl.pallas_call(
        functools.partial(exchange_kernel, batches, members),
        in_specs=[pl.BlockSpec(memory_space=pltpu.VMEM)],
        out_specs=pl.BlockSpec(memory_space=pltpu.VMEM),
        out_shape=shape(values.shape),
        scratch_shapes=[
            pltpu.VMEM((batches - 1,) + values.shape, F32),
            pltpu.VMEM((members - 1,) + values.shape, F32),
            pltpu.VMEM(values.shape, F32),
            pltpu.SemaphoreType.DMA((batches - 1,)),
            pltpu.SemaphoreType.DMA((batches - 1,)),
            pltpu.SemaphoreType.DMA((members - 1,)),
            pltpu.SemaphoreType.DMA((members - 1,)),
        ],
        compiler_params=pltpu.CompilerParams(collective_id=collective_id, has_side_effects=True),
    )(values)


def local(
    block_input,
    reduce_weight,
    reduce_gain,
    reduce_bias,
    group_weight,
    group_gain,
    group_bias,
    expand_weight,
    expand_gain,
    expand_bias,
    out_grad,
):
    batches, members = lax.axis_size("batch"), lax.axis_size("group")
    channels, row_pixels = block_input.shape
    pixels = row_pixels // members
    count = row_pixels * batches
    mid_total = reduce_weight.shape[1]
    mids = mid_total // BLK
    blocks = channels * members // BLK
    me = lax.axis_index("group")

    def to_pixels(values):
        moved = lax.all_to_all(values.T.reshape(members, pixels, channels), "group", 0, 0)
        if channels == BLK:
            return moved
        share = BLK // channels
        moved = moved.reshape(blocks, share, pixels, channels).transpose(0, 2, 1, 3)
        return moved.reshape(blocks, pixels, BLK)

    def to_channels(values):
        if channels != BLK:
            share = BLK // channels
            values = values.reshape(blocks, pixels, share, channels).transpose(0, 2, 1, 3)
            values = values.reshape(members, pixels, channels)
        moved = lax.all_to_all(values, "group", 0, 0)
        return moved.reshape(row_pixels, channels).T

    def gather(values):
        return lax.all_gather(values, "group", axis=0, tiled=True)

    local_mid = reduce_gain.shape[0]
    pack = jnp.concatenate([reduce_gain, reduce_bias, group_gain, group_bias, expand_gain, expand_bias])
    packs = gather(pack[None])
    vectors, offset = [], 0
    for length in (local_mid, local_mid, local_mid, local_mid, channels, channels):
        vectors.append(packs[:, offset : offset + length].reshape(-1, BLK))
        offset += length
    reduce_params = jnp.stack(vectors[0:2], 1)
    group_params = jnp.stack(vectors[2:4], 1)
    expand_params = jnp.stack(vectors[4:6], 1)
    reduce_full = gather(reduce_weight).reshape(blocks, BLK, mid_total)
    expand_full = gather(expand_weight).reshape(blocks, BLK, mid_total)
    taps = gather(group_weight.reshape(group_weight.shape[0], 9, GW, GW))
    taps = taps.reshape(mids, BLK // GW, 9, GW, GW)
    forward_taps = taps.transpose(0, 2, 1, 3, 4).reshape(mids, 9, BLK, GW)
    backward_taps = taps[:, :, ::-1].transpose(0, 2, 1, 4, 3).reshape(mids, 9, BLK, GW)
    place = jnp.arange(pixels, dtype=jnp.int32)
    tall, wide = (place // SIDE) % SIDE, place % SIDE
    masks = jnp.stack([wide != 0, wide != SIDE - 1, tall != 0, tall != SIDE - 1])
    masks = jnp.broadcast_to(masks[:, :, None].astype(F32), (4, pixels, HALF))

    x = to_pixels(block_input)
    grad = to_pixels(out_grad)

    reduced, reduce_sums = reduce_product(x, reduce_full)
    reduce_sums = exchange(reduce_sums, batches, members, 1)
    grouped, group_sums = conv(reduced, reduce_sums, reduce_params, forward_taps, masks, count)
    group_sums = exchange(group_sums, batches, members, 1)
    expanded, expand_sums, act = expand_product(grouped, group_sums, group_params, expand_full, count)
    expand_sums = exchange(expand_sums, batches, members, 2)
    out, upstream, expand_stats = output(expanded, expand_sums, expand_params, x, grad, count)
    expand_stats = exchange(expand_stats, batches, members, 2)
    back, group_up, group_stats = expand_back(
        expanded, expand_sums, expand_params, upstream, expand_stats, expand_full, grouped, group_sums, group_params, count
    )
    expand_part = weight_grad(back, act)
    group_stats = exchange(group_stats, batches, members, 1)
    reduce_up, reduce_stats, taps_part = conv_back(
        reduced,
        reduce_sums,
        reduce_params,
        grouped,
        group_sums,
        group_params,
        group_up,
        group_stats,
        backward_taps,
        masks,
        count,
    )
    reduce_stats = exchange(reduce_stats, batches, members, 1)
    inner, reduce_part = reduce_back(
        reduced, reduce_sums, reduce_params, reduce_up, reduce_stats, x, upstream, reduce_full, count
    )
    block_output = to_channels(out)
    input_grad = to_channels(inner).astype(F32)

    def shared_sum(part):
        rows = channels // batches
        part = part.reshape(members, batches, rows, mid_total).transpose(1, 0, 2, 3)
        part = lax.all_to_all(part, "batch", 0, 0).astype(F32).sum(0).astype(BF16)
        part = lax.all_to_all(part, "group", 0, 0).astype(F32).sum(0)
        return lax.all_gather(part, "batch", axis=0, tiled=True)

    expand_weight_grad = shared_sum(expand_part)
    reduce_weight_grad = shared_sum(reduce_part)
    taps_part = taps_part.reshape(mids, 9, BLK // GW, GW, GW).transpose(0, 2, 1, 4, 3)
    taps_part = taps_part.reshape(members, -1, 9, GW, GW)
    group_weight_grad = lax.all_to_all(taps_part.astype(BF16), "group", 0, 0).astype(F32).sum(0)
    group_weight_grad = lax.psum(group_weight_grad, "batch").reshape(group_weight.shape)

    def own(stats, which, length):
        return lax.dynamic_slice_in_dim(stats[:, which].reshape(-1), me * length, length, 0)

    return (
        block_output,
        input_grad,
        reduce_weight_grad,
        group_weight_grad,
        expand_weight_grad,
        own(reduce_stats, 1, local_mid),
        own(reduce_stats, 0, local_mid),
        own(group_stats, 1, local_mid),
        own(group_stats, 0, local_mid),
        own(expand_stats, 1, channels),
        own(expand_stats, 0, channels),
    )


def solution(mesh):
    in_specs = (
        P("group", "batch"),
        P("group", None),
        P("group"),
        P("group"),
        P("group", None, None, None, None),
        P("group"),
        P("group"),
        P("group", None),
        P("group"),
        P("group"),
        P("group", "batch"),
    )
    out_specs = (
        P("group", "batch"),
        P("group", "batch"),
        P("group", None),
        P("group", None, None, None, None),
        P("group", None),
        P("group"),
        P("group"),
        P("group"),
        P("group"),
        P("group"),
        P("group"),
    )
    return jax.shard_map(local, mesh=mesh, in_specs=in_specs, out_specs=out_specs, check_vma=False)
```

time: 3360 us -> 1270 us (0.38)
  waiting for transfers between devices: 2560 us -> 399 us
  blocking collectives: 37.8 us -> 422 us
  Pallas kernels: 0 us -> 288 us
  local copies, waits for them, and re-layouts: 350 us -> 76.3 us
  matrix products: 201 us -> 0 us
  other arithmetic: 190 us -> 23.1 us
  starting transfers between devices: 0.25 us -> 41.3 us
    reduce_scatter x2 -> x0, waiting for transfers between devices: 1610 us -> none  [the longest x1 805 us: local(): lax.psum_scatter(lax.dot_general(reduce_weight, block_input, (((0,), (0,)...]
    all_gather x2 -> x4, waiting for transfers between devices: 938 us -> 32.6 us  [the longest x2 32.6 us: shared_sum(): return lax.all_gather(part, 'batch', axis=0, tiled=True)]
    all_to_all x0 -> x7, waiting for transfers between devices: none -> 364 us  [the longest x2 180 us: to_pixels(): lax.all_to_all(values.T.reshape(members, pixels, channels), 'group', 0, 0)]
    pallas_call x0 -> x14, Pallas kernels: none -> 288 us  [the longest x6 74.5 us: exchange(): pl.pallas_call(functools.partial(exchange_kernel, batches, members), in_s...]
    all_gather x0 -> x2, blocking collectives: none -> 248 us  [gather(): return lax.all_gather(values, 'group', axis=0, tiled=True)]
    dot_general x9 -> x0, matrix products: 201 us -> none  [the longest x1 43.4 us: local(): jnp.einsum('nhwgo,gtio->nhwtgi', back_grid, kernel, preferred_element_typ...]
    all_to_all x0 -> x2, blocking collectives: none -> 174 us  [the longest x1 145 us: to_channels(): moved = lax.all_to_all(values, 'group', 0, 0)]
    scatter-add x8 -> x0, other arithmetic: 111 us -> none  [patch_scatter(): padded.at[:, row_off:row_off + SIDE, col_off:col_off + SIDE]]
  transfers between devices with their start and end apart: 6 -> 12, of which waited for: 5 -> 7; matrix products, arithmetic and copies ran while one was open for 3% -> 6% of each run, Pallas kernels for 0% -> 13%
where the time goes in v1:
time: 1270 us; the launch traced here: 1260 us
  blocking collectives  422 us (33%)
  waiting for transfers between devices  399 us (31%)
  Pallas kernels  288 us (23%)
  local copies, waits for them, and re-layouts  76.3 us (6%)
  starting transfers between devices  41.3 us (3%)
  other arithmetic  23.1 us (2%)
  between operations  14.1 us (1%)
    all_gather x2, blocking collectives, gather(): return lax.all_gather(values, 'group', axis=0, tiled=True)  248 us
    all_to_all x2, waiting for transfers between devices, to_pixels(): lax.all_to_all(values.T.reshape(members, pixels, channels), 'group', 0, 0)  180 us
    all_to_all x1, blocking collectives, to_channels(): moved = lax.all_to_all(values, 'group', 0, 0)  145 us
    all_to_all x1, waiting for transfers between devices, to_channels(): moved = lax.all_to_all(values, 'group', 0, 0)  91.9 us
    pallas_call x6, Pallas kernels, exchange(): pl.pallas_call(functools.partial(exchange_kernel, batches, members), in_s...  74.5 us
    all_to_all x2, waiting for transfers between devices, shared_sum(): part = lax.all_to_all(part, 'batch', 0, 0).astype(F32).sum(0).astype(BF16)  72.5 us
    pallas_call x1, Pallas kernels, conv_back(): call(functools.partial(conv_back_kernel, count), (mids,), [block(pixels,...  46.9 us
    pallas_call x1, Pallas kernels, reduce_back(): call(functools.partial(reduce_back_kernel, count), (blocks,), [whole(mids...  37.3 us
  transfers between devices with their start and end apart: 12, of which 7 were waited for; matrix products, arithmetic and copies ran while one was open for 6% of the time, Pallas kernels for 13%

profile of v1, /device:TPU:25, one launch (start us, length us, event | category | flops | bytes accessed | tf_op | source)
XLA Modules:
  0.0 1263.3 jit_solution(8210971292439694982)
XLA Ops:
  7.2 9.8 copy.46
  17.0 5.5 all-to-all-start
  22.5 0.7 all-gather.6.cloned.1.call-update
  23.2 9.5 copy.49
  32.7 179.5 %all-to-all-done.x_ref = bf16[8,1568,256]{2,1,0:T(8,128)(2,1)} async-done(((bf16[8,1568,256]{2,1,0:T(8,128)(2,1)}), bf16[8,1568,256]{2,1,0:T(8,128)(2,1)}, u32[]{:S(2)}, u32[]{:S(2)}) %all-to-all-start) | async-done | bytes 6422560 | tf_op jit(solution)/shard_map/all_to_all | solution.py:614
  212.2 5.9 all-to-all-start.1
  218.1 0.7 all-gather.8.cloned.1.call-update
  219.0 202.4 %all-gather = f32[8192]{0:T(1024)S(1)} all-gather(f32[1024]{0:T(1024)S(1)} %constant_dynamic-update-slice_fusion), channel_id=2, replica_groups=mesh['batch'=4,'group'=8] {'group'}, dimensions={0}, use_global_device_ids=true | all-gather | bytes 36864 | tf_op jit(solution)/shard_map/all_gather | solution.py:630
  421.4 45.2 %all_gather.20 = bf16[32,9,32,32]{3,2,1,0:T(8,128)(2,1)S(1)} all-gather(bf16[4,9,32,32]{3,2,1,0:T(8,128)(2,1)S(1)} %bitcast.64), channel_id=1, replica_groups=mesh['batch'=4,'group'=8] {'group'}, dimensions={0}, use_global_device_ids=true | all-gather | bytes 663552 | tf_op jit(solution)/shard_map/all_gather | solution.py:630
  466.7 2.0 copy.47
  469.2 2.6 copy.51
  471.8 0.6 pad_maximum_fusion.1.prm_ref
  472.4 0.6 pad_maximum_fusion.2.gprm_ref
  473.0 0.6 pad_maximum_fusion.prm_ref
  473.9 16.2 %shard_map.194 = (f32[4,1568,256]{2,1,0:T(8,128)}, f32[4,2,256]{2,1,0:T(2,128)}) custom-call(bf16[8,1568,256]{2,1,0:T(8,128)(2,1)} %all-to-all-done.x_ref, bf16[8,256,1024]{2,1,0:T(8,128)(2,1)} %bitcast.75), custom_call_target="tpu_custom_call" | custom-call | flops 6576668672 | bytes 20000000 | tf_op jit(solution)/shard_map/pallas_call | solution.py:105
  490.0 18.2 %shard_map.195.sums_ref = f32[4,2,256]{2,1,0:T(2,128)} custom-call(f32[4,2,256]{2,1,0:T(2,128)} %get-tuple-element.30.x_ref), custom_call_target="tpu_custom_call" | custom-call | tf_op jit(solution)/shard_map/pallas_call | solution.py:573
  508.2 2.2 broadcast_in_dim.10.mask_ref
  510.4 26.2 %shard_map.196 = (f32[4,1568,256]{2,1,0:T(8,128)}, f32[4,2,256]{2,1,0:T(2,128)}) custom-call(f32[4,1568,256]{2,1,0:T(8,128)} %get-tuple-element.29.red_ref, f32[4,2,256]{2,1,0:T(2,128)} %shard_map.195.sums_ref, f32[4,2,256]{2,1,0:T(2,128)} %pad_maximum_fusion.1.prm_ref, bf16[4,9,256,32]{3,2,1,0:T(8,128)(2,1)} %bitcast.62, ...), custom_call_target="tpu_custom_call" | custom-call | flops 7398752256 | bytes 20000000 | tf_op jit(solution)/shard_map/pallas_call | solution.py:191
  536.6 10.3 shard_map.197.gsums_ref
  547.0 26.5 %shard_map.198 = (f32[8,1568,256]{2,1,0:T(8,128)}, f32[8,2,256]{2,1,0:T(2,128)}, bf16[1568,1024]{1,0:T(8,128)(2,1)}) custom-call(f32[4,1568,256]{2,1,0:T(8,128)} %get-tuple-element.31.grp_ref, f32[4,2,256]{2,1,0:T(2,128)} %shard_map.197.gsums_ref, f32[4,2,256]{2,1,0:T(2,128)} %pad_maximum_fusion.2.gprm_ref, bf16[8,256,1024]{2,1,0:T(8,128)(2,1)} %bitcast.57), custom_call_target="tpu_custom_call" | custom-call | flops 6576668672 | bytes 20000000 | tf_op jit(solution)/shard_map/pallas_call | solution.py:333
  573.5 12.4 shard_map.199.sums_ref
  585.9 20.6 %shard_map.200 = (bf16[8,1568,256]{2,1,0:T(8,128)(2,1)}, f32[8,1568,256]{2,1,0:T(8,128)}, f32[8,2,256]{2,1,0:T(2,128)}) custom-call(f32[8,1568,256]{2,1,0:T(8,128)} %get-tuple-element.33.exp_ref, f32[8,2,256]{2,1,0:T(2,128)} %shard_map.199.sums_ref, f32[8,2,256]{2,1,0:T(2,128)} %pad_maximum_fusion.prm_ref, bf16[8,1568,256]{2,1,0:T(8,128)(2,1)} %all-to-all-done.x_ref, ...), custom_call_target="tpu_custom_call" | custom-call | flops 64225280 | bytes 20000000 | tf_op jit(solution)/shard_map/pallas_call | solution.py:368
  606.5 11.5 shard_map.201.upsums_ref
  618.0 27.2 %shard_map.202 = (bf16[8,1568,256]{2,1,0:T(8,128)(2,1)}, f32[4,1568,256]{2,1,0:T(8,128)}, f32[4,2,256]{2,1,0:T(2,128)}) custom-call(f32[8,1568,256]{2,1,0:T(8,128)} %get-tuple-element.33.exp_ref, f32[8,2,256]{2,1,0:T(2,128)} %shard_map.199.sums_ref, f32[8,2,256]{2,1,0:T(2,128)} %pad_maximum_fusion.prm_ref, f32[8,1568,256]{2,1,0:T(8,128)} %get-tuple-element.36.up_ref, ...), custom_call_target="tpu_custom_call" | custom-call | flops 6576668672 | bytes 20000000 | tf_op jit(solution)/shard_map/pallas_call | solution.py:442
  645.2 11.7 shard_map.203.upsums_ref
  656.9 46.9 %shard_map.204 = (f32[4,1568,256]{2,1,0:T(8,128)}, f32[4,2,256]{2,1,0:T(2,128)}, f32[4,9,256,32]{3,2,1,0:T(8,128)}) custom-call(f32[4,1568,256]{2,1,0:T(8,128)} %get-tuple-element.29.red_ref, f32[4,2,256]{2,1,0:T(2,128)} %shard_map.195.sums_ref, f32[4,2,256]{2,1,0:T(2,128)} %pad_maximum_fusion.1.prm_ref, f32[4,1568,256]{2,1,0:T(8,128)} %get-tuple-element.31.grp_ref, ...), custom_call_target="tpu_custom_call" | custom-call | flops 14797504512 | bytes 20000000 | tf_op jit(solution)/shard_map/pallas_call | solution.py:278
  703.8 10.4 shard_map.205.rupsums_ref
  714.2 2.7 convert_element_type.47
  716.9 2.5 copy.54
  719.4 4.8 reshape.186
  724.1 5.5 all-to-all-start.6
  729.7 37.3 %shard_map.206 = (bf16[8,1568,256]{2,1,0:T(8,128)(2,1)}, bf16[8,256,1024]{2,1,0:T(8,128)(2,1)}) custom-call(f32[4,1568,256]{2,1,0:T(8,128)} %get-tuple-element.29.red_ref, f32[4,2,256]{2,1,0:T(2,128)} %shard_map.195.sums_ref, f32[4,2,256]{2,1,0:T(2,128)} %pad_maximum_fusion.1.prm_ref, f32[4,1568,256]{2,1,0:T(8,128)} %get-tuple-element.40.rup_ref, ...), custom_call_target="tpu_custom_call" | custom-call | flops 13153337344 | bytes 20000000 | tf_op jit(solution)/shard_map/pallas_call | solution.py:516
  766.9 4.9 copy.59
  771.9 6.6 all-to-all-start.4
  778.5 12.9 %shard_map.207 = bf16[8,256,1024]{2,1,0:T(8,128)(2,1)} custom-call(bf16[8,1568,256]{2,1,0:T(8,128)(2,1)} %get-tuple-element.45.left_ref, bf16[1568,1024]{1,0:T(8,128)(2,1)} %get-tuple-element.46.right_ref), custom_call_target="tpu_custom_call" | custom-call | flops 6576668672 | bytes 20000000 | tf_op jit(solution)/shard_map/pallas_call | solution.py:472
  791.4 4.9 copy.58
  796.4 29.5 %all-to-all-done.4 = bf16[4,8,64,1024]{3,2,1,0:T(8,128)(2,1)} async-done(((bf16[4,8,64,1024]{3,2,1,0:T(8,128)(2,1)}), bf16[4,8,64,1024]{3,2,1,0:T(8,128)(2,1)}, u32[]{:S(2)}, u32[]{:S(2)}) %all-to-all-start.4) | async-done | bytes 4194336 | tf_op jit(solution)/shard_map/all_to_all | solution.py:692
  825.9 5.7 all-to-all-start.7
  831.6 4.4 reduce_sum.51
  836.0 43.0 %all-to-all-done.7 = bf16[4,8,64,1024]{3,2,1,0:T(8,128)(2,1)} async-done(((bf16[4,8,64,1024]{3,2,1,0:T(8,128)(2,1)}), bf16[4,8,64,1024]{3,2,1,0:T(8,128)(2,1)}, u32[]{:S(2)}, u32[]{:S(2)}) %all-to-all-start.7) | async-done | bytes 4194336 | tf_op jit(solution)/shard_map/all_to_all | solution.py:692
  879.0 5.4 all-to-all-start.5
  884.4 3.3 reduce_sum.54
  887.7 20.4 %all-to-all-done.5 = bf16[8,64,1024]{2,1,0:T(8,128)(2,1)S(1)} async-done(((bf16[8,64,1024]{2,1,0:T(8,128)(2,1)}), bf16[8,64,1024]{2,1,0:T(8,128)(2,1)S(1)}, u32[]{:S(2)}, u32[]{:S(2)}) %all-to-all-start.5) | async-done | bytes 1048608 | tf_op jit(solution)/shard_map/all_to_all | solution.py:693
  908.1 29.0 %all_to_all.45 = bf16[8,64,1024]{2,1,0:T(8,128)(2,1)S(1)} all-to-all(bf16[8,64,1024]{2,1,0:T(8,128)(2,1)S(1)} %reduce_sum.54), channel_id=1, replica_groups=mesh['batch'=4,'group'=8] {'group'}, dimensions={0} | all-to-all | bytes 2097152 | tf_op jit(solution)/shard_map/all_to_all | solution.py:693
  937.1 145.1 %all_to_all.46 = bf16[8,1568,256]{2,1,0:T(8,128)(2,1)} all-to-all(bf16[8,1568,256]{2,1,0:T(8,128)(2,1)} %get-tuple-element.42), channel_id=1, replica_groups=mesh['batch'=4,'group'=8] {'group'}, dimensions={0} | all-to-all | bytes 12845056 | tf_op jit(solution)/shard_map/all_to_all | solution.py:626
  1082.2 6.6 all-to-all-start.2
  1088.8 0.9 convert_reduce_fusion.2
  1089.8 0.9 convert_reduce_fusion.1
  1090.7 0.6 dynamic_slice.18
  1091.3 0.6 dynamic_slice.19
  1091.9 0.6 dynamic_slice.20
  1093.1 0.6 dynamic_slice.22
  1093.8 0.6 dynamic_slice.23
  1094.4 1.1 reshape.187
  1095.6 1.3 convert_reduce_fusion
  1096.9 13.8 %all-gather.10.cloned.1.call-done = f32[256,1024]{1,0:T(8,128)} async-done(((f32[64,1024]{1,0:T(8,128)}), f32[256,1024]{1,0:T(8,128)}) %all-gather.10.cloned.1.call-update) | async-done | bytes 1048592 | tf_op jit(solution)/shard_map/all_gather | solution.py:694
  1110.7 18.7 %all-gather.12.cloned.1.call-done = f32[256,1024]{1,0:T(8,128)} async-done(((f32[64,1024]{1,0:T(8,128)}), f32[256,1024]{1,0:T(8,128)}) %all-gather.12.cloned.1.call-update) | async-done | bytes 1048592 | tf_op jit(solution)/shard_map/all_gather | solution.py:694
  1129.5 7.6 bitcast_convert_fusion
  1137.1 91.9 %all-to-all-done.2 = bf16[8,1568,256]{2,1,0:T(8,128)(2,1)} async-done(((bf16[8,1568,256]{2,1,0:T(8,128)(2,1)}), bf16[8,1568,256]{2,1,0:T(8,128)(2,1)}, u32[]{:S(2)}, u32[]{:S(2)}) %all-to-all-start.2) | async-done | bytes 6422560 | tf_op jit(solution)/shard_map/all_to_all | solution.py:626
  1229.0 9.6 copy.50
  1238.6 14.3 %copy.52 = f32[12544,256]{0,1:T(8,128)} copy(f32[12544,256]{1,0:T(8,128)} %bitcast_convert_fusion) | data formatting | bytes 25690112 | tf_op jit(solution)/shard_map/convert_element_type | solution.py:687
  1252.9 1.0 copy.69
  1253.9 1.9 copy.70
  1255.8 1.0 copy.71
  (61 shorter events, 1.6 us)
Async XLA Ops:
  17.0 195.2 %all-to-all-start = ((bf16[8,1568,256]{2,1,0:T(8,128)(2,1)}), bf16[8,1568,256]{2,1,0:T(8,128)(2,1)}, u32[]{:S(2)}, u32[]{:S(2)}) async-start(bf16[8,1568,256]{2,1,0:T(8,128)(2,1)} %bitcast.46), calls=%async_computation | async-start | bytes 12845056 | tf_op jit(solution)/shard_map/all_to_all | solution.py:614
  22.5 451.4 %all-gather.6.cloned.1.call-start = ((), (), s32[]{:S(2)}) async-start(), calls=%async_computation.9 | async-start | bytes 4718592 | tf_op jit(solution)/shard_map/all_gather | solution.py:630
  212.2 6.7 copy-start.10
  212.2 6.7 copy-start.11
  212.2 6.7 copy-start.12
  212.2 6.7 copy-start.13
  212.2 6.8 copy-start.8
  212.2 6.8 copy-start.9
  212.2 209.2 %copy-start.4 = (bf16[4,3,3,32,32]{4,3,2,1,0:T(8,128)(2,1)S(1)}, bf16[4,3,3,32,32]{4,3,2,1,0:T(8,128)(2,1)}, u32[]{:S(2)}) copy-start(bf16[4,3,3,32,32]{4,3,2,1,0:T(8,128)(2,1)} %param.15) | copy-start | bytes 221188
  212.2 373.7 %all-to-all-start.1 = ((bf16[8,1568,256]{2,1,0:T(8,128)(2,1)}), bf16[8,1568,256]{2,1,0:T(8,128)(2,1)}, u32[]{:S(2)}, u32[]{:S(2)}) async-start(bf16[8,1568,256]{2,1,0:T(8,128)(2,1)} %bitcast.45), calls=%async_computation.1 | async-start | bytes 12845056 | tf_op jit(solution)/shard_map/all_to_all | solution.py:614
  218.1 328.8 %all-gather.8.cloned.1.call-start = ((), (), s32[]{:S(2)}) async-start(), calls=%async_computation.10 | async-start | bytes 4718592 | tf_op jit(solution)/shard_map/all_gather | solution.py:630
  724.1 47.7 %all-to-all-start.6 = ((bf16[8,2,18432]{2,1,0:T(2,128)(2,1)}), bf16[8,2,18432]{2,1,0:T(2,128)(2,1)S(1)}, u32[]{:S(2)}, u32[]{:S(2)}) async-start(bf16[8,2,18432]{2,1,0:T(2,128)(2,1)} %reshape.186), calls=%async_computation.6 | async-start | bytes 1179648 | tf_op jit(solution)/shard_map/all_to_all | solution.py:700
  771.9 19.6 %copy-start = (bf16[8,2,18432]{2,1,0:T(2,128)(2,1)}, bf16[8,2,18432]{2,1,0:T(2,128)(2,1)S(1)}, u32[]{:S(2)}) copy-start(bf16[8,2,18432]{2,1,0:T(2,128)(2,1)S(1)} %all-to-all-done.6) | copy-start | bytes 1769476
  771.9 54.0 %all-to-all-start.4 = ((bf16[4,8,64,1024]{3,2,1,0:T(8,128)(2,1)}), bf16[4,8,64,1024]{3,2,1,0:T(8,128)(2,1)}, u32[]{:S(2)}, u32[]{:S(2)}) async-start(bf16[4,8,64,1024]{3,2,1,0:T(8,128)(2,1)} %bitcast.49), calls=%async_computation.4 | async-start | bytes 8388608 | tf_op jit(solution)/shard_map/all_to_all | solution.py:692
  825.9 53.1 %all-to-all-start.7 = ((bf16[4,8,64,1024]{3,2,1,0:T(8,128)(2,1)}), bf16[4,8,64,1024]{3,2,1,0:T(8,128)(2,1)}, u32[]{:S(2)}, u32[]{:S(2)}) async-start(bf16[4,8,64,1024]{3,2,1,0:T(8,128)(2,1)} %bitcast.50), calls=%async_computation.7 | async-start | bytes 8388608 | tf_op jit(solution)/shard_map/all_to_all | solution.py:692
  879.0 29.1 %all-to-all-start.5 = ((bf16[8,64,1024]{2,1,0:T(8,128)(2,1)}), bf16[8,64,1024]{2,1,0:T(8,128)(2,1)S(1)}, u32[]{:S(2)}, u32[]{:S(2)}) async-start(bf16[8,64,1024]{2,1,0:T(8,128)(2,1)} %reduce_sum.51), calls=%async_computation.5 | async-start | bytes 2097152 | tf_op jit(solution)/shard_map/all_to_all | solution.py:693
  1082.2 8.6 copy-start.7
  1082.2 9.7 copy-start.6
  1082.2 10.9 copy-start.5
  1082.2 12.2 copy-start.1
  1082.2 146.9 %all-to-all-start.2 = ((bf16[8,1568,256]{2,1,0:T(8,128)(2,1)}), bf16[8,1568,256]{2,1,0:T(8,128)(2,1)}, u32[]{:S(2)}, u32[]{:S(2)}) async-start(bf16[8,1568,256]{2,1,0:T(8,128)(2,1)} %get-tuple-element.35), calls=%async_computation.2 | async-start | bytes 12845056 | tf_op jit(solution)/shard_map/all_to_all | solution.py:626
  1088.8 21.9 %all-gather.10.cloned.1.call-start = ((), (), s32[]{:S(2)}) async-start(), calls=%async_computation.11 | async-start | bytes 1310720 | tf_op jit(solution)/shard_map/all_gather | solution.py:694
  1089.7 39.8 %all-gather.12.cloned.1.call-start = ((), (), s32[]{:S(2)}) async-start(), calls=%async_computation.13 | async-start | bytes 1310720 | tf_op jit(solution)/shard_map/all_gather | solution.py:694
  1090.7 162.2 %all-reduce.2.cloned.1.call-start = ((), (), s32[]{:S(2)}) async-start(), calls=%async_computation.12 | async-start | bytes 1179648 | tf_op jit(solution)/shard_map/psum | solution.py:701
  1238.6 14.3 %copy-start.2 = (f32[256,1024]{1,0:T(8,128)S(1)}, f32[256,1024]{1,0:T(8,128)}, u32[]{:S(2)}) copy-start(f32[256,1024]{1,0:T(8,128)} %all-gather.10.cloned.1.call-done) | copy-start | bytes 3145732
  1238.6 17.2 %copy-start.3 = (f32[256,1024]{1,0:T(8,128)S(1)}, f32[256,1024]{1,0:T(8,128)}, u32[]{:S(2)}) copy-start(f32[256,1024]{1,0:T(8,128)} %all-gather.12.cloned.1.call-done) | copy-start | bytes 3145732
Sparse Core Ops, SparseCore 0:
  25.4 169.8 all-gather.5
  221.1 170.1 all-gather.7
  1091.8 18.9 all-gather.9
  1112.7 16.7 all-gather.11
  1132.2 32.2 all-reduce.1

commit v2 on v1

--- a/solution.py
+++ b/solution.py
@@ -25,7 +25,10 @@
 
 
 def row_chunk(pixels):
-    return 224 if pixels % 224 == 0 else pixels
+    for size in (224, 208, 192, 176, 160, 144, 128, 112):
+        if pixels % size == 0:
+            return size
+    return pixels
 
 
 def over_rows(pixels, body):
@@ -51,16 +54,157 @@
     return standard, standard * coef[2] + coef[3]
 
 
-def add_stats(ref, first, second):
-    ref[0, 0:1] += jnp.sum(first, 0, keepdims=True)
-    ref[0, 1:2] += jnp.sum(second, 0, keepdims=True)
+def add_stats(ref, slot, first, second):
+    ref[slot, 0:1] += jnp.sum(first, 0, keepdims=True)
+    ref[slot, 1:2] += jnp.sum(second, 0, keepdims=True)
+
+
+def clear_stats(ref):
+    @pl.when(pl.program_id(0) == 0)
+    def _():
+        ref[...] = jnp.zeros_like(ref)
 
 
 def dot(a, b, dims=((1,), (0,))):
     return lax.dot_general(a, b, (dims, ((), ())), preferred_element_type=F32)
 
 
-def call(kernel, grid, in_specs, out_specs, out_shape, scratch, flops):
+def devices(batches, members):
+    row, me = lax.axis_index("batch"), lax.axis_index("group")
+    across = [(lax.rem(row + step, batches), me) for step in range(1, batches)]
+    along = [(row, lax.rem(me + step, members)) for step in range(1, members)]
+    return row, me, across, along
+
+
+def greet(others):
+    barrier = pltpu.get_barrier_semaphore()
+    for device in others:
+        pl.semaphore_signal(barrier, inc=1, device_id=device, device_id_type=MESH)
+    pl.semaphore_wait(barrier, len(others))
+
+
+def remote(source, target, send, recv, device):
+    return pltpu.make_async_remote_copy(
+        src_ref=source, dst_ref=target, send_sem=send, recv_sem=recv, device_id=device, device_id_type=MESH
+    )
+
+
+def spread(source, target, send, recv, others):
+    copies = [
+        remote(source, target.at[step], send.at[step], recv.at[step], device) for step, device in enumerate(others)
+    ]
+    for copy in copies:
+        copy.start()
+    for copy in copies:
+        copy.wait()
+
+
+def total_stats(ref, across, along, first_ref, second_ref, mid_ref, send1, recv1, send2, recv2):
+    mid_ref[0] = ref[...]
+    spread(mid_ref.at[0], first_ref, send1, recv1, across)
+    total = mid_ref[0]
+    for step in range(len(across)):
+        total += first_ref[step]
+    mid_ref[1] = total
+    spread(mid_ref.at[1], second_ref, send2, recv2, along)
+    for step in range(len(along)):
+        total += second_ref[step]
+    ref[...] = total
+
+
+def stats_scratch(dims, batches, members):
+    return [
+        pltpu.VMEM((batches - 1,) + dims, F32),
+        pltpu.VMEM((members - 1,) + dims, F32),
+        pltpu.VMEM((2,) + dims, F32),
+        pltpu.SemaphoreType.DMA((batches - 1,)),
+        pltpu.SemaphoreType.DMA((batches - 1,)),
+        pltpu.SemaphoreType.DMA((members - 1,)),
+        pltpu.SemaphoreType.DMA((members - 1,)),
+    ]
+
+
+class Comm:
+    def __init__(self, batches, members, collective_id, source=None, rows=None, into=None):
+        self.batches, self.members, self.collective_id = batches, members, collective_id
+        self.source, self.rows, self.into = source, rows, into
+
+
+def piece_copies(source, target, rows, me, along, send, recv):
+    rows = pl.ds(*rows)
+    copies = [
+        remote(source.at[device[1], rows], target.at[me, rows], send.at[step], recv.at[step], device)
+        for step, device in enumerate(along)
+    ]
+    return copies + [pltpu.make_async_copy(source.at[me, rows], target.at[me, rows], send.at[len(along)])]
+
+
+def call(kernel, grid, in_specs, out_specs, out_shape, scratch, flops, comm=None):
+    if comm is None:
+        return functools.partial(
+            plain_call, kernel, grid, in_specs, out_specs, out_shape, scratch, flops, pltpu.CompilerParams(vmem_limit_bytes=VMEM_LIMIT)
+        )
+    n_in, n_out, n_scratch = len(in_specs), len(out_specs), len(scratch)
+    stats = out_shape[-1].shape
+    batches, members = comm.batches, comm.members
+
+    def wrapped(*refs):
+        refs = list(refs)
+        ins = refs[:n_in]
+        del refs[:n_in]
+        source = refs.pop(0) if comm.rows else None
+        if comm.into is not None:
+            refs.pop(0)
+        outs = refs[:n_out]
+        del refs[:n_out]
+        target = refs.pop(0) if comm.rows else None
+        own = refs[:n_scratch]
+        del refs[:n_scratch]
+        stats_refs = refs[:7]
+        del refs[:7]
+        row, me, across, along = devices(batches, members)
+
+        def copies():
+            return piece_copies(source, target, comm.rows, me, along, *refs)
+
+        @pl.when(pl.program_id(0) == 0)
+        def _():
+            greet(across + along)
+            if comm.rows:
+                for copy in copies():
+                    copy.start()
+
+        kernel(*ins, *outs, *own)
+
+        @pl.when(pl.program_id(0) == pl.num_programs(0) - 1)
+        def _():
+            total_stats(outs[-1], across, along, *stats_refs)
+            if comm.rows:
+                for copy in copies():
+                    copy.wait()
+
+    scratch = list(scratch) + stats_scratch(stats, batches, members)
+    in_specs, out_specs, out_shape = list(in_specs), list(out_specs), list(out_shape)
+    extra, aliases = [], {}
+    if comm.rows:
+        extra = [comm.source]
+        if comm.into is not None:
+            extra.append(comm.into)
+            aliases = {len(in_specs) + 1: len(out_specs)}
+        in_specs += [pl.BlockSpec(memory_space=pl.ANY)] * len(extra)
+        out_specs.append(pl.BlockSpec(memory_space=pl.ANY))
+        out_shape.append(shape(comm.source.shape, comm.source.dtype))
+        scratch += [pltpu.SemaphoreType.DMA((members,)), pltpu.SemaphoreType.DMA((members - 1,))]
+    params = pltpu.CompilerParams(
+        vmem_limit_bytes=VMEM_LIMIT, collective_id=comm.collective_id, has_side_effects=True
+    )
+    inner = functools.partial(
+        plain_call, wrapped, grid, in_specs, out_specs, out_shape, scratch, flops, params, aliases=aliases
+    )
+    return lambda *args: inner(*args, *extra)
+
+
+def plain_call(kernel, grid, in_specs, out_specs, out_shape, scratch, flops, params, *args, aliases={}):
     return pl.pallas_call(
         kernel,
         grid=grid,
@@ -68,9 +212,10 @@
         out_specs=out_specs,
         out_shape=out_shape,
         scratch_shapes=scratch,
-        compiler_params=pltpu.CompilerParams(vmem_limit_bytes=VMEM_LIMIT),
+        input_output_aliases=aliases,
+        compiler_params=params,
         cost_estimate=pl.CostEstimate(flops=flops, bytes_accessed=20_000_000, transcendentals=0),
-    )
+    )(*args)
 
 
 def shape(dims, dtype=F32):
@@ -86,7 +231,8 @@
 
 
 def reduce_kernel(x_ref, w_ref, out_ref, sum_ref):
-    sum_ref[...] = jnp.zeros_like(sum_ref)
+    clear_stats(sum_ref)
+    slot = pl.program_id(0)
 
     def body(start, size):
         rows = pl.ds(start, size)
@@ -94,34 +240,37 @@
         for source in range(1, x_ref.shape[0]):
             total += dot(x_ref[source, rows], w_ref[source])
         out_ref[0, rows] = total
-        add_stats(sum_ref, total, total * total)
+        add_stats(sum_ref, slot, total, total * total)
 
     over_rows(x_ref.shape[1], body)
 
 
-def reduce_product(x, weight):
+def reduce_product(x, weight, comm):
     blocks, pixels, _ = x.shape
     mids = weight.shape[2] // BLK
     return call(
         reduce_kernel,
         (mids,),
         [whole(blocks, pixels, BLK), pl.BlockSpec((blocks, BLK, BLK), lambda j: (0, 0, j))],
-        [block(pixels, BLK), block(2, BLK)],
+        [block(pixels, BLK), whole(mids, 2, BLK)],
         [shape((mids, pixels, BLK)), shape((mids, 2, BLK))],
         [],
         2 * pixels * blocks * BLK * mids * BLK,
+        comm,
     )(x, weight)
 
 
+def same_group():
+    return lax.broadcasted_iota(jnp.int32, (BLK, BLK), 0) // GW == lax.broadcasted_iota(jnp.int32, (BLK, BLK), 1) // GW
+
+
 def spread_weight(compact_ref, dense_ref):
-    cols = lax.broadcasted_iota(jnp.int32, (GW, BLK), 1)
-    rows = lax.broadcasted_iota(jnp.int32, (GW, BLK), 0)
-    tile = jnp.where(cols % GW == rows, 1.0, 0.0).astype(BF16)
-    own = lax.broadcasted_iota(jnp.int32, (BLK, BLK), 0) // GW == lax.broadcasted_iota(jnp.int32, (BLK, BLK), 1) // GW
-
-    @pl.loop(0, 9)
-    def _(tap):
-        dense_ref[tap] = jnp.where(own, dot(compact_ref[0, tap], tile), 0.0).astype(BF16)
+    own = same_group()
+    for tap in range(9):
+        rows = pl.ds(tap * GW, GW)
+        compact = jnp.concatenate([compact_ref[0, rows], compact_ref[1, rows]], 1).astype(F32)
+        tiled = jnp.concatenate([compact] * (BLK // GW), 0)
+        dense_ref[tap] = jnp.where(own, tiled, 0.0).astype(BF16)
 
 
 def twice(mask):
@@ -149,15 +298,15 @@
     return jnp.concatenate([stack_ref[col_off + 1, half, rows] for half in range(2)], 1).astype(BF16)
 
 
-def conv_rows(stack_ref, mask_ref, dense_ref, start, size):
+def conv_rows(stack_ref, mask_ref, dense_ref, start, size, flipped=False):
     rows = pl.ds(start, size)
     total = None
     for row_off in (-1, 0, 1):
         part = None
         for col_off in (-1, 0, 1):
-            term = dot(
-                window(stack_ref, start, size, row_off, col_off), dense_ref[(row_off + 1) * 3 + col_off + 1]
-            )
+            values = window(stack_ref, start, size, row_off, col_off)
+            tap = (row_off + 1) * 3 + col_off + 1
+            term = dot(values, dense_ref[8 - tap], ((1,), (1,))) if flipped else dot(values, dense_ref[tap])
             part = term if part is None else part + term
         if row_off:
             part = part * twice(mask_ref[2 if row_off < 0 else 3, rows])
@@ -176,17 +325,18 @@
         fill(stack_ref, mask_ref, start, size, (norm * jax.nn.sigmoid(norm)).astype(BF16).astype(F32))
 
     over_rows(pixels, enter)
-    stat_ref[...] = jnp.zeros_like(stat_ref)
+    clear_stats(stat_ref)
+    slot = pl.program_id(0)
 
     def body(start, size):
         total = conv_rows(stack_ref, mask_ref, dense_ref, start, size)
         out_ref[0, pl.ds(start, size)] = total
-        add_stats(stat_ref, total, total * total)
+        add_stats(stat_ref, slot, total, total * total)
 
     over_rows(pixels, body)
 
 
-def conv(reduced, sums, params, weight, masks, count):
+def conv(reduced, sums, params, weight, masks, count, comm):
     mids, pixels, _ = reduced.shape
     return call(
         functools.partial(conv_kernel, count),
@@ -195,13 +345,14 @@
             block(pixels, BLK),
             block(2, BLK),
             block(2, BLK),
-            block(9, BLK, GW),
+            pl.BlockSpec((2,) + weight.shape[1:], lambda j: (j, 0, 0)),
             whole(4, pixels, HALF),
         ],
-        [block(pixels, BLK), block(2, BLK)],
+        [block(pixels, BLK), whole(mids, 2, BLK)],
         [shape((mids, pixels, BLK)), shape((mids, 2, BLK))],
         [pltpu.VMEM((3, 2, pixels + 2 * PAD, HALF), F32), pltpu.VMEM((9, BLK, BLK), BF16)],
         2 * 9 * pixels * mids * BLK * BLK,
+        comm,
     )(reduced, sums, params, weight, masks)
 
 
@@ -218,8 +369,8 @@
     weight_ref,
     mask_ref,
     out_ref,
+    wgrad_ref,
     stat_ref,
-    wgrad_ref,
     stack_ref,
     dense_ref,
     back_ref,
@@ -244,14 +395,15 @@
         fill(stack_ref, mask_ref, start, size, values)
 
     over_rows(pixels, back)
-    stat_ref[...] = jnp.zeros_like(stat_ref)
+    clear_stats(stat_ref)
+    slot = pl.program_id(0)
 
     def body(start, size):
         rows = pl.ds(start, size)
         standard, norm = standardize(red_ref[0, rows], coef)
-        up = conv_rows(stack_ref, mask_ref, dense_ref, start, size) * silu_slope(norm)
+        up = conv_rows(stack_ref, mask_ref, dense_ref, start, size, True) * silu_slope(norm)
         out_ref[0, rows] = up
-        add_stats(stat_ref, up, up * standard)
+        add_stats(stat_ref, slot, up, up * standard)
 
     over_rows(pixels, body)
 
@@ -260,20 +412,20 @@
         fill(stack_ref, mask_ref, start, size, (norm * jax.nn.sigmoid(norm)).astype(BF16).astype(F32))
 
     over_rows(pixels, enter)
-    own = lax.broadcasted_iota(jnp.int32, (BLK, BLK), 0) // GW == lax.broadcasted_iota(jnp.int32, (BLK, BLK), 1) // GW
-    for row_off in (-1, 0, 1):
-        for col_off in (-1, 0, 1):
-            full = dot(
-                back_ref[row_off + 1], window(stack_ref, 0, pixels, row_off, col_off), ((0,), (0,))
-            )
-            full = jnp.where(own, full, 0.0)
-            kept = full[:, 0:GW]
-            for group in range(1, BLK // GW):
-                kept += full[:, group * GW : (group + 1) * GW]
-            wgrad_ref[0, (row_off + 1) * 3 + col_off + 1] = kept
-
-
-def conv_back(reduced, sums, params, grouped, gsums, gparams, up, upsums, weight, masks, count):
+    own = same_group()
+    for tap in range(9):
+        full = dot(back_ref[tap // 3], window(stack_ref, 0, pixels, tap // 3 - 1, tap % 3 - 1), ((0,), (0,)))
+        full = jnp.where(own, full, 0.0)
+        kept = full[0:GW]
+        for group in range(1, BLK // GW):
+            kept += full[group * GW : (group + 1) * GW]
+        for half in range(2):
+            wgrad_ref[half, tap * GW : (tap + 1) * GW] = kept[:, half * HALF : (half + 1) * HALF].astype(BF16)
+    for half in range(2):
+        wgrad_ref[half, 9 * GW :] = jnp.zeros((wgrad_ref.shape[1] - 9 * GW, HALF), BF16)
+
+
+def conv_back(reduced, sums, params, grouped, gsums, gparams, up, upsums, weight, masks, count, comm):
     mids, pixels, _ = reduced.shape
     return call(
         functools.partial(conv_back_kernel, count),
@@ -287,21 +439,22 @@
             block(2, BLK),
             block(pixels, BLK),
             block(2, BLK),
-            block(9, BLK, GW),
+            pl.BlockSpec((2,) + weight.shape[1:], lambda j: (j, 0, 0)),
             whole(4, pixels, HALF),
         ],
-        [block(pixels, BLK), block(2, BLK), block(9, BLK, GW)],
-        [shape((mids, pixels, BLK)), shape((mids, 2, BLK)), shape((mids, 9, BLK, GW))],
+        [block(pixels, BLK), pl.BlockSpec((2,) + weight.shape[1:], lambda j: (j, 0, 0)), whole(mids, 2, BLK)],
+        [shape((mids, pixels, BLK)), shape(weight.shape, BF16), shape((mids, 2, BLK))],
         [
             pltpu.VMEM((3, 2, pixels + 2 * PAD, HALF), F32),
             pltpu.VMEM((9, BLK, BLK), BF16),
             pltpu.VMEM((3, pixels, BLK), BF16),
         ],
         4 * 9 * pixels * mids * BLK * BLK,
+        comm,
     )(reduced, sums, params, grouped, gsums, gparams, up, upsums, weight, masks)
 
 
-def expand_kernel(count, grp_ref, gsums_ref, gprm_ref, w_ref, out_ref, sum_ref, act_ref):
+def expand_kernel(count, grp_ref, gsums_ref, gprm_ref, w_ref, out_ref, act_ref, sum_ref):
     mids, pixels, _ = grp_ref.shape
 
     @pl.when(pl.program_id(0) == 0)
@@ -316,18 +469,19 @@
 
             over_rows(pixels, body)
 
-    sum_ref[...] = jnp.zeros_like(sum_ref)
+    clear_stats(sum_ref)
+    slot = pl.program_id(0)
 
     def product(start, size):
         rows = pl.ds(start, size)
         total = dot(act_ref[rows], w_ref[0], ((1,), (1,)))
         out_ref[0, rows] = total
-        add_stats(sum_ref, total, total * total)
+        add_stats(sum_ref, slot, total, total * total)
 
     over_rows(pixels, product)
 
 
-def expand_product(grouped, gsums, gparams, weight, count):
+def expand_product(grouped, gsums, gparams, weight, count, comm):
     mids, pixels, _ = grouped.shape
     blocks = weight.shape[0]
     return call(
@@ -339,16 +493,18 @@
             whole(mids, 2, BLK),
             block(BLK, mids * BLK),
         ],
-        [block(pixels, BLK), block(2, BLK), whole(pixels, mids * BLK)],
-        [shape((blocks, pixels, BLK)), shape((blocks, 2, BLK)), shape((pixels, mids * BLK), BF16)],
+        [block(pixels, BLK), whole(pixels, mids * BLK), whole(blocks, 2, BLK)],
+        [shape((blocks, pixels, BLK)), shape((pixels, mids * BLK), BF16), shape((blocks, 2, BLK))],
         [],
         2 * pixels * blocks * BLK * mids * BLK,
+        comm,
     )(grouped, gsums, gparams, weight)
 
 
 def output_kernel(count, exp_ref, sums_ref, prm_ref, x_ref, grad_ref, out_ref, up_ref, stat_ref):
     coef = coefficients(sums_ref[0], prm_ref[0], count)
-    stat_ref[...] = jnp.zeros_like(stat_ref)
+    clear_stats(stat_ref)
+    slot = pl.program_id(0)
 
     def body(start, size):
         rows = pl.ds(start, size)
@@ -358,21 +514,22 @@
         out_ref[0, rows] = (summed * sigma).astype(BF16)
         up = grad_ref[0, rows].astype(F32) * (sigma * (1.0 + summed * (1.0 - sigma)))
         up_ref[0, rows] = up
-        add_stats(stat_ref, up, up * standard)
+        add_stats(stat_ref, slot, up, up * standard)
 
     over_rows(exp_ref.shape[1], body)
 
 
-def output(expanded, sums, params, x, grad, count):
+def output(expanded, sums, params, x, grad, count, comm):
     blocks, pixels, _ = expanded.shape
     return call(
         functools.partial(output_kernel, count),
         (blocks,),
         [block(pixels, BLK), block(2, BLK), block(2, BLK), block(pixels, BLK), block(pixels, BLK)],
-        [block(pixels, BLK), block(pixels, BLK), block(2, BLK)],
+        [block(pixels, BLK), block(pixels, BLK), whole(blocks, 2, BLK)],
         [shape((blocks, pixels, BLK), BF16), shape((blocks, pixels, BLK)), shape((blocks, 2, BLK))],
         [],
         20 * pixels * blocks * BLK,
+        comm,
     )(expanded, sums, params, x, grad)
 
 
@@ -394,6 +551,7 @@
 ):
     blocks, pixels, _ = keep_ref.shape
     step = pl.program_id(0)
+    clear_stats(stat_ref)
 
     @pl.when(step < blocks)
     def _():
@@ -414,7 +572,6 @@
     @pl.when(step >= blocks)
     def _():
         coef = coefficients(gsums_ref[0], gprm_ref[0], count)
-        stat_ref[...] = jnp.zeros_like(stat_ref)
 
         def body(start, size):
             rows = pl.ds(start, size)
@@ -424,12 +581,12 @@
             standard, norm = standardize(grp_ref[0, rows], coef)
             up = total * silu_slope(norm)
             out_ref[0, rows] = up
-            add_stats(stat_ref, up, up * standard)
+            add_stats(stat_ref, step - blocks, up, up * standard)
 
         over_rows(pixels, body)
 
 
-def expand_back(expanded, sums, params, up, upsums, weight, grouped, gsums, gparams, count):
+def expand_back(expanded, sums, params, up, upsums, weight, grouped, gsums, gparams, count, comm):
     blocks, pixels, _ = expanded.shape
     mids = grouped.shape[0]
 
@@ -453,17 +610,16 @@
             second(2, BLK),
             second(2, BLK),
         ],
-        [first(pixels, BLK), second(pixels, BLK), second(2, BLK)],
+        [first(pixels, BLK), second(pixels, BLK), whole(mids, 2, BLK)],
         [shape((blocks, pixels, BLK), BF16), shape((mids, pixels, BLK)), shape((mids, 2, BLK))],
         [pltpu.VMEM((blocks, pixels, BLK), BF16)],
         2 * pixels * blocks * BLK * mids * BLK,
+        comm,
     )(expanded, sums, params, up, upsums, weight, grouped, gsums, gparams)
 
 
 def weight_grad_kernel(left_ref, right_ref, out_ref):
-    for first in range(0, right_ref.shape[1], BLK):
-        columns = slice(first, first + BLK)
-        out_ref[0, :, columns] = dot(left_ref[0], right_ref[:, columns], ((0,), (0,))).astype(BF16)
+    weight_grad_block(left_ref[0], right_ref, out_ref, 0)
 
 
 def weight_grad(left, right):
@@ -480,34 +636,41 @@
     )(left, right)[0]
 
 
+def first_back(count, red_ref, sums_ref, prm_ref, rup_ref, rupsums_ref, back_ref):
+    mids, pixels, _ = red_ref.shape
+    for mid in range(mids):
+        coef = coefficients(sums_ref[mid], prm_ref[mid], count)
+        scale = coef[2] * coef[1]
+        up_mean = rupsums_ref[mid, 0:1] / count
+        up_lean = rupsums_ref[mid, 1:2] / count
+
+        def body(start, size):
+            rows = pl.ds(start, size)
+            standard, _ = standardize(red_ref[mid, rows], coef)
+            values = scale * (rup_ref[mid, rows] - up_mean - standard * up_lean)
+            back_ref[rows, mid * BLK : (mid + 1) * BLK] = values.astype(BF16)
+
+        over_rows(pixels, body)
+
+
+def weight_grad_block(left, right_ref, out_ref, slot):
+    for first in range(0, right_ref.shape[1], BLK):
+        columns = slice(first, first + BLK)
+        out_ref[slot, :, columns] = dot(left, right_ref[:, columns], ((0,), (0,))).astype(BF16)
+
+
 def reduce_back_kernel(count, red_ref, sums_ref, prm_ref, rup_ref, rupsums_ref, x_ref, up_ref, w_ref, grad_ref, wgrad_ref, back_ref):
-    mids, pixels, _ = red_ref.shape
-
     @pl.when(pl.program_id(0) == 0)
     def _():
-        for mid in range(mids):
-            coef = coefficients(sums_ref[mid], prm_ref[mid], count)
-            scale = coef[2] * coef[1]
-            up_mean = rupsums_ref[mid, 0:1] / count
-            up_lean = rupsums_ref[mid, 1:2] / count
-
-            def body(start, size):
-                rows = pl.ds(start, size)
-                standard, _ = standardize(red_ref[mid, rows], coef)
-                values = scale * (rup_ref[mid, rows] - up_mean - standard * up_lean)
-                back_ref[rows, mid * BLK : (mid + 1) * BLK] = values.astype(BF16)
-
-            over_rows(pixels, body)
+        first_back(count, red_ref, sums_ref, prm_ref, rup_ref, rupsums_ref, back_ref)
 
     def product(start, size):
         rows = pl.ds(start, size)
         total = dot(back_ref[rows], w_ref[0], ((1,), (1,)))
         grad_ref[0, rows] = (up_ref[0, rows] + total).astype(BF16)
 
-    over_rows(pixels, product)
-    for mid in range(mids):
-        columns = slice(mid * BLK, (mid + 1) * BLK)
-        wgrad_ref[0, :, columns] = dot(x_ref[0], back_ref[:, columns], ((0,), (0,))).astype(BF16)
+    over_rows(x_ref.shape[1], product)
+    weight_grad_block(x_ref[0], back_ref, wgrad_ref, 0)
 
 
 def reduce_back(reduced, sums, params, rup, rupsums, x, up, weight, count):
@@ -533,40 +696,11 @@
     )(reduced, sums, params, rup, rupsums, x, up, weight)
 
 
-def exchange_kernel(batches, members, x_ref, out_ref, first_ref, second_ref, mid_ref, send1, recv1, send2, recv2):
-    row, me = lax.axis_index("batch"), lax.axis_index("group")
-    across = [(lax.rem(row + step, batches), me) for step in range(1, batches)]
-    along = [(row, lax.rem(me + step, members)) for step in range(1, members)]
-    barrier = pltpu.get_barrier_semaphore()
-    for device in across + along:
-        pl.semaphore_signal(barrier, inc=1, device_id=device, device_id_type=MESH)
-    pl.semaphore_wait(barrier, len(across) + len(along))
-
-    def spread(source, target, send, recv, devices):
-        copies = []
-        for step, device in enumerate(devices):
-            copy = pltpu.make_async_remote_copy(
-                src_ref=source,
-                dst_ref=target.at[step],
-                send_sem=send.at[step],
-                recv_sem=recv.at[step],
-                device_id=device,
-                device_id_type=MESH,
-            )
-            copy.start()
-            copies.append(copy)
-        for copy in copies:
-            copy.wait()
-
-    spread(x_ref, first_ref, send1, recv1, across)
-    total = x_ref[...]
-    for step in range(batches - 1):
-        total += first_ref[step]
-    mid_ref[...] = total
-    spread(mid_ref, second_ref, send2, recv2, along)
-    for step in range(members - 1):
-        total += second_ref[step]
-    out_ref[...] = total
+def exchange_kernel(batches, members, x_ref, out_ref, *scratch):
+    row, me, across, along = devices(batches, members)
+    greet(across + along)
+    out_ref[...] = x_ref[...]
+    total_stats(out_ref, across, along, *scratch)
 
 
 def exchange(values, batches, members, collective_id):
@@ -575,20 +709,458 @@
         in_specs=[pl.BlockSpec(memory_space=pltpu.VMEM)],
         out_specs=pl.BlockSpec(memory_space=pltpu.VMEM),
         out_shape=shape(values.shape),
-        scratch_shapes=[
-            pltpu.VMEM((batches - 1,) + values.shape, F32),
-            pltpu.VMEM((members - 1,) + values.shape, F32),
-            pltpu.VMEM(values.shape, F32),
-            pltpu.SemaphoreType.DMA((batches - 1,)),
-            pltpu.SemaphoreType.DMA((batches - 1,)),
-            pltpu.SemaphoreType.DMA((members - 1,)),
-            pltpu.SemaphoreType.DMA((members - 1,)),
-        ],
+        scratch_shapes=stats_scratch(values.shape, batches, members),
         compiler_params=pltpu.CompilerParams(collective_id=collective_id, has_side_effects=True),
     )(values)
 
 
-def local(
+def turn(source_ref, target_ref, slot, chunk):
+    first = (49 * chunk) // 4
+
+    @pl.loop(0, 13)
+    def _(tile):
+        columns = pl.ds(pl.multiple_of((first + tile) * HALF, HALF), HALF)
+        rows = pl.ds(pl.multiple_of(tile * HALF, HALF), HALF)
+        target_ref[slot, rows] = source_ref[:, columns].T
+
+
+def turned(target_ref, slot, chunk, pixels):
+    return target_ref.at[slot, pl.ds(pl.multiple_of(32 * (chunk % 4), 16), pixels)]
+
+
+def opening_kernel(batches, members, *refs):
+    x_ref, grad_ref, wr_ref, we_ref, wg_ref, prm_ref = refs[:6]
+    xp_ref, gradt_ref, wr_out, we_out, wg_out, prm_out = refs[6:12]
+    xin, xturn, gin, gturn, load, own, xsend, xrecv, gsend, psend, precv, wsend, wrecv, fsend, frecv = refs[12:]
+    row, me, across, along = devices(batches, members)
+    pixels = xp_ref.shape[1]
+    load_x = pltpu.make_async_copy(x_ref, xin, load.at[0])
+    load_grad = pltpu.make_async_copy(grad_ref, gin, load.at[1])
+    load_x.start()
+    load_grad.start()
+    weights = [(wr_ref, wr_out), (wg_ref, wg_out), (we_ref, we_out)]
+    local_copies = [pltpu.make_async_copy(prm_ref, prm_out.at[me], own.at[3])]
+    parts = []
+    for index, (source, target) in enumerate(weights):
+        size = source.shape[0] // batches
+        part = pl.ds(pl.multiple_of(row * size, 16), size)
+        parts.append(part)
+        local_copies.append(pltpu.make_async_copy(source.at[part], target.at[me, part], own.at[index]))
+    for copy in local_copies:
+        copy.start()
+    greet(across + along)
+    copies = []
+    for step, device in enumerate(along):
+        copies.append(remote(prm_ref, prm_out.at[me], psend.at[step], precv.at[step], device))
+    first = []
+    for index, (source, target) in enumerate(weights):
+        for step, device in enumerate(along):
+            first.append(
+                remote(
+                    source.at[parts[index]],
+                    target.at[me, parts[index]],
+                    wsend.at[index, step],
+                    wrecv.at[index, step],
+                    device,
+                )
+            )
+    for copy in copies + first:
+        copy.start()
+    load_x.wait()
+    for step, device in enumerate(along):
+        turn(xin, xturn, step, device[1])
+        copy = remote(turned(xturn, step, device[1], pixels), xp_ref.at[me], xsend.at[step], xrecv.at[step], device)
+        copy.start()
+        copies.append(copy)
+    last = members - 1
+    turn(xin, xturn, last, me)
+    copy = pltpu.make_async_copy(turned(xturn, last, me, pixels), xp_ref.at[me], xsend.at[last])
+    copy.start()
+    copies.append(copy)
+    load_grad.wait()
+    for member in range(members):
+        turn(gin, gturn, member, member)
+        copy = pltpu.make_async_copy(turned(gturn, member, member, pixels), gradt_ref.at[member], gsend.at[member])
+        copy.start()
+        copies.append(copy)
+    for copy in local_copies:
+        copy.wait()
+    for index, (source, target) in enumerate(weights):
+        for copy in first[index * len(along) : (index + 1) * len(along)]:
+            copy.wait()
+        for step, device in enumerate(across):
+            held = target.at[:, parts[index]]
+            copy = remote(held, held, fsend.at[index, step], frecv.at[index, step], device)
+            copy.start()
+            copies.append(copy)
+    for copy in copies:
+        copy.wait()
+
+
+def opening(block_input, out_grad, reduce_weight, expand_weight, taps, params, batches, members):
+    channels, row_pixels = block_input.shape
+    pixels = row_pixels // members
+    dma = pltpu.SemaphoreType.DMA
+    other, across = members - 1, batches - 1
+    padded = 13 * HALF
+    return pl.pallas_call(
+        functools.partial(opening_kernel, batches, members),
+        in_specs=[pl.BlockSpec(memory_space=pl.ANY)] * 6,
+        out_specs=[pl.BlockSpec(memory_space=pl.ANY)] * 6,
+        out_shape=[
+            shape((members, pixels, channels), BF16),
+            shape((members, pixels, channels), BF16),
+            shape((members,) + reduce_weight.shape, BF16),
+            shape((members,) + expand_weight.shape, BF16),
+            shape((members,) + taps.shape, BF16),
+            shape((members,) + params.shape),
+        ],
+        scratch_shapes=[
+            pltpu.VMEM((channels, row_pixels), BF16),
+            pltpu.VMEM((members, padded, channels), BF16),
+            pltpu.VMEM((channels, row_pixels), BF16),
+            pltpu.VMEM((members, padded, channels), BF16),
+            dma((2,)),
+            dma((4,)),
+            dma((members,)),
+            dma((other,)),
+            dma((members,)),
+            dma((other,)),
+            dma((other,)),
+            dma((3, other)),
+            dma((3, other)),
+            dma((3, across)),
+            dma((3, across)),
+        ],
+        compiler_params=pltpu.CompilerParams(vmem_limit_bytes=VMEM_LIMIT, collective_id=0, has_side_effects=True),
+    )(block_input, out_grad, reduce_weight, expand_weight, taps, params)
+
+
+class Reduce:
+    def __init__(self, part, out, row, me, across, along, refs):
+        self.part, self.out, self.row, self.me, self.across, self.along = part, out, row, me, across, along
+        self.first, self.held, self.second, self.total = refs[:4]
+        self.s1, self.r1, self.s2, self.r2, self.s3, self.r3 = refs[4:]
+        self.size = self.total.shape[0]
+
+    def rows(self, row):
+        return pl.ds(pl.multiple_of(row * self.size, 16), self.size)
+
+    def over_batch(self):
+        return [
+            remote(
+                self.part.at[:, self.rows(device[0])], self.first.at[step], self.s1.at[step], self.r1.at[step], device
+            )
+            for step, device in enumerate(self.across)
+        ]
+
+    def add_batch(self):
+        @pl.loop(0, self.held.shape[0])
+        def _(member):
+            total = self.part[member, self.rows(self.row)].astype(F32)
+            for step in range(len(self.across)):
+                total += self.first[step, member].astype(F32)
+            self.held[member] = total.astype(BF16)
+
+    def over_group(self):
+        return [
+            remote(self.held.at[device[1]], self.second.at[step], self.s2.at[step], self.r2.at[step], device)
+            for step, device in enumerate(self.along)
+        ]
+
+    def add_group(self):
+        total = self.held[self.me].astype(F32)
+        for step in range(len(self.along)):
+            total += self.second[step].astype(F32)
+        self.total[...] = total
+
+    def share(self):
+        rows = self.rows(self.row)
+        copies = [
+            remote(self.total, self.out.at[rows], self.s3.at[step], self.r3.at[step], device)
+            for step, device in enumerate(self.across)
+        ]
+        return copies + [pltpu.make_async_copy(self.total, self.out.at[rows], self.s3.at[len(self.across)])]
+
+
+def reduce_scratch(dims, batches, members):
+    rows, columns = dims[1] // batches, dims[2]
+    dma = pltpu.SemaphoreType.DMA
+    return [
+        pltpu.VMEM((batches - 1, members, rows, columns), BF16),
+        pltpu.VMEM((members, rows, columns), BF16),
+        pltpu.VMEM((members - 1, rows, columns), BF16),
+        pltpu.VMEM((rows, columns), F32),
+        dma((batches - 1,)),
+        dma((batches - 1,)),
+        dma((members - 1,)),
+        dma((members - 1,)),
+        dma((batches,)),
+        dma((batches - 1,)),
+    ]
+
+
+def each(copies, what):
+    for copy in copies:
+        getattr(copy, what)()
+
+
+def closing_kernel(count, batches, members, rows, *refs):
+    red_ref, sums_ref, prm_ref, rup_ref, rupsums_ref, x_ref, up_ref, w_ref, epart_ref, tpart_ref, src_ref, _ = refs[:12]
+    recv_ref, rout_ref, eout_ref, tout_ref, dst_ref = refs[12:17]
+    back_ref, grad_ref, wpart_ref, gsend, grecv, psend, precv = refs[17:24]
+    row, me, across, along = devices(batches, members)
+    step = pl.program_id(0)
+    last = members - 1
+    expand_sum = Reduce(epart_ref, eout_ref, row, me, across, along, refs[24:34])
+    taps_sum = Reduce(tpart_ref, tout_ref, row, me, across, along, refs[34:44])
+    reduce_sum = Reduce(wpart_ref, rout_ref, row, me, across, along, refs[44:54])
+    other = lax.rem(me + 1 + step, members)
+
+    def pieces():
+        return piece_copies(src_ref, dst_ref, rows, me, along, psend, precv)
+
+    @pl.when(step == 0)
+    def _():
+        greet(across + along)
+        each(pieces(), "start")
+        each(expand_sum.over_batch(), "start")
+        each(taps_sum.over_batch(), "start")
+        first_back(count, red_ref, sums_ref, prm_ref, rup_ref, rupsums_ref, back_ref)
+
+    def product(start, size):
+        part = pl.ds(start, size)
+        total = dot(back_ref[part], w_ref[0], ((1,), (1,)))
+        grad_ref[step, part] = (up_ref[0, part] + total).astype(BF16)
+
+    over_rows(x_ref.shape[1], product)
+
+    @pl.when(step < last)
+    def _():
+        remote(grad_ref.at[step], recv_ref.at[me], gsend.at[step], grecv.at[step], (row, other)).start()
+
+    weight_grad_block(x_ref[0], back_ref, wpart_ref, other)
+
+    @pl.when(step == last)
+    def _():
+        own = pltpu.make_async_copy(grad_ref.at[last], recv_ref.at[me], gsend.at[last])
+        own.start()
+        each(reduce_sum.over_batch(), "start")
+        for part in (expand_sum, taps_sum, reduce_sum):
+            each(part.over_batch(), "wait")
+            part.add_batch()
+            each(part.over_group(), "start")
+        own.wait()
+        each(pieces(), "wait")
+        for past, device in enumerate(along):
+            remote(grad_ref.at[past], recv_ref.at[me], gsend.at[past], grecv.at[past], device).wait()
+        for part in (expand_sum, taps_sum, reduce_sum):
+            each(part.over_group(), "wait")
+            part.add_group()
+            each(part.share(), "start")
+        for part in (expand_sum, taps_sum, reduce_sum):
+            each(part.share(), "wait")
+
+
+def closing(reduced, sums, params, rup, rupsums, x, up, weight, epart, tpart, source, into, rows, count, batches, members):
+    mids, pixels, _ = reduced.shape
+    blocks = x.shape[0]
+    once = pl.Buffered(1)
+
+    def keep(*dims):
+        return pl.BlockSpec(dims, lambda j: (0,) * len(dims), pipeline_mode=once)
+
+    def turn_block(*dims):
+        def index(j):
+            return (lax.rem(lax.axis_index("group") + 1 + j, members),) + (0,) * len(dims)
+
+        return pl.BlockSpec((1,) + dims, index)
+
+    anywhere = pl.BlockSpec(memory_space=pl.ANY)
+    dma = pltpu.SemaphoreType.DMA
+    wdims = (blocks, BLK, mids * BLK)
+    scratch = [
+        pltpu.VMEM((pixels, mids * BLK), BF16),
+        pltpu.VMEM((blocks, pixels, BLK), BF16),
+        pltpu.VMEM(wdims, BF16),
+        dma((members,)),
+        dma((members - 1,)),
+        dma((members,)),
+        dma((members - 1,)),
+    ]
+    for dims in (wdims, tpart.shape, wdims):
+        scratch += reduce_scratch(dims, batches, members)
+    return pl.pallas_call(
+        functools.partial(closing_kernel, count, batches, members, rows),
+        grid=(blocks,),
+        in_specs=[
+            keep(mids, pixels, BLK),
+            keep(mids, 2, BLK),
+            keep(mids, 2, BLK),
+            keep(mids, pixels, BLK),
+            keep(mids, 2, BLK),
+            turn_block(pixels, BLK),
+            turn_block(pixels, BLK),
+            turn_block(BLK, mids * BLK),
+            keep(*wdims),
+            keep(*tpart.shape),
+            anywhere,
+            anywhere,
+        ],
+        out_specs=[anywhere] * 5,
+        out_shape=[
+            shape((members, pixels, BLK), BF16),
+            shape(wdims[1:]),
+            shape(wdims[1:]),
+            shape(tpart.shape[1:]),
+            shape(source.shape, BF16),
+        ],
+        scratch_shapes=scratch,
+        input_output_aliases={11: 4},
+        compiler_params=pltpu.CompilerParams(vmem_limit_bytes=VMEM_LIMIT, collective_id=7, has_side_effects=True),
+    )(reduced, sums, params, rup, rupsums, x, up, weight, epart, tpart, source, into)
+
+
+def turn_out_kernel(in_ref, out_ref):
+    for first in range(0, in_ref.shape[0], HALF):
+        out_ref[:, first : first + HALF] = in_ref[first : first + HALF].astype(out_ref.dtype).T
+
+
+def turn_out(values, dtype):
+    rows, channels = values.shape
+    size = next(part for part in (1792, 896, HALF) if rows % part == 0)
+    return call(
+        turn_out_kernel,
+        (rows // size,),
+        [pl.BlockSpec((size, channels), lambda j: (j, 0))],
+        [pl.BlockSpec((channels, size), lambda j: (0, j))],
+        [shape((channels, rows), dtype)],
+        [],
+        rows * channels,
+    )(values)[0]
+
+
+def pixel_masks(pixels):
+    place = jnp.arange(pixels, dtype=jnp.int32)
+    tall, wide = (place // SIDE) % SIDE, place % SIDE
+    masks = jnp.stack([wide != 0, wide != SIDE - 1, tall != 0, tall != SIDE - 1])
+    return jnp.broadcast_to(masks[:, :, None].astype(F32), (4, pixels, HALF))
+
+
+def own_part(stats, which, length):
+    return lax.dynamic_slice_in_dim(stats[:, which].reshape(-1), lax.axis_index("group") * length, length, 0)
+
+
+TAP_ROWS = 320
+
+
+def fused(
+    block_input,
+    reduce_weight,
+    reduce_gain,
+    reduce_bias,
+    group_weight,
+    group_gain,
+    group_bias,
+    expand_weight,
+    expand_gain,
+    expand_bias,
+    out_grad,
+):
+    batches, members = lax.axis_size("batch"), lax.axis_size("group")
+    channels, row_pixels = block_input.shape
+    pixels = row_pixels // members
+    count = row_pixels * batches
+    local_mid = reduce_gain.shape[0]
+    pack = jnp.concatenate([reduce_gain, reduce_bias, group_gain, group_bias, expand_gain, expand_bias]).reshape(-1, HALF)
+    taps = group_weight.reshape(-1, 9, GW, GW).transpose(1, 2, 0, 3).reshape(9 * GW, HALF)
+    taps = jnp.pad(taps, ((0, TAP_ROWS - 9 * GW), (0, 0)))
+    masks = pixel_masks(pixels)
+    x, grad_turned, reduce_full, expand_full, taps_full, packs = opening(
+        block_input, out_grad, reduce_weight, expand_weight, taps, pack, batches, members
+    )
+    vectors = packs[:, :4].reshape(-1, 2, 4, HALF).transpose(0, 2, 1, 3).reshape(-1, 4, BLK)
+    reduce_params, group_params = vectors[:, :2], vectors[:, 2:]
+    expand_params = packs[:, 4:].reshape(-1, 2, BLK)
+
+    def comm(collective_id, source=None, rows=None, into=None):
+        return Comm(batches, members, collective_id, source, rows, into)
+
+    first, second = 448, 1008
+    reduced, reduce_sums, grad = reduce_product(x, reduce_full, comm(1, grad_turned, (0, first)))
+    grouped, group_sums, grad = conv(
+        reduced, reduce_sums, reduce_params, taps_full, masks, count, comm(2, grad_turned, (first, second - first), grad)
+    )
+    expanded, act, expand_sums, grad = expand_product(
+        grouped, group_sums, group_params, expand_full, count, comm(3, grad_turned, (second, pixels - second), grad)
+    )
+    out, upstream, expand_stats = output(expanded, expand_sums, expand_params, x, grad, count, comm(4))
+    first, second = 448, 1120
+    back, group_up, group_stats, moved = expand_back(
+        expanded,
+        expand_sums,
+        expand_params,
+        upstream,
+        expand_stats,
+        expand_full,
+        grouped,
+        group_sums,
+        group_params,
+        count,
+        comm(5, out, (0, first)),
+    )
+    reduce_up, taps_part, reduce_stats, moved = conv_back(
+        reduced,
+        reduce_sums,
+        reduce_params,
+        grouped,
+        group_sums,
+        group_params,
+        group_up,
+        group_stats,
+        taps_full,
+        masks,
+        count,
+        comm(6, out, (first, second - first), moved),
+    )
+    expand_part = weight_grad(back, act)
+    inner, reduce_weight_grad, expand_weight_grad, taps_grad, moved = closing(
+        reduced,
+        reduce_sums,
+        reduce_params,
+        reduce_up,
+        reduce_stats,
+        x,
+        upstream,
+        reduce_full,
+        expand_part,
+        taps_part,
+        out,
+        moved,
+        (second, pixels - second),
+        count,
+        batches,
+        members,
+    )
+    block_output = turn_out(moved.reshape(row_pixels, channels), BF16)
+    input_grad = turn_out(inner.reshape(row_pixels, channels), F32)
+    taps_grad = taps_grad[: 9 * GW].reshape(9, GW, -1, GW).transpose(2, 0, 3, 1)
+    return (
+        block_output,
+        input_grad,
+        reduce_weight_grad,
+        taps_grad.reshape(group_weight.shape),
+        expand_weight_grad,
+        own_part(reduce_stats, 1, local_mid),
+        own_part(reduce_stats, 0, local_mid),
+        own_part(group_stats, 1, local_mid),
+        own_part(group_stats, 0, local_mid),
+        own_part(expand_stats, 1, channels),
+        own_part(expand_stats, 0, channels),
+    )
+
+
+def modular(
     block_input,
     reduce_weight,
     reduce_gain,
@@ -642,31 +1214,27 @@
     reduce_full = gather(reduce_weight).reshape(blocks, BLK, mid_total)
     expand_full = gather(expand_weight).reshape(blocks, BLK, mid_total)
     taps = gather(group_weight.reshape(group_weight.shape[0], 9, GW, GW))
-    taps = taps.reshape(mids, BLK // GW, 9, GW, GW)
-    forward_taps = taps.transpose(0, 2, 1, 3, 4).reshape(mids, 9, BLK, GW)
-    backward_taps = taps[:, :, ::-1].transpose(0, 2, 1, 4, 3).reshape(mids, 9, BLK, GW)
-    place = jnp.arange(pixels, dtype=jnp.int32)
-    tall, wide = (place // SIDE) % SIDE, place % SIDE
-    masks = jnp.stack([wide != 0, wide != SIDE - 1, tall != 0, tall != SIDE - 1])
-    masks = jnp.broadcast_to(masks[:, :, None].astype(F32), (4, pixels, HALF))
+    taps = taps.reshape(-1, HALF // GW, 9, GW, GW).transpose(0, 2, 3, 1, 4).reshape(-1, 9 * GW, HALF)
+    taps = jnp.pad(taps, ((0, 0), (0, TAP_ROWS - 9 * GW), (0, 0)))
+    masks = pixel_masks(pixels)
 
     x = to_pixels(block_input)
     grad = to_pixels(out_grad)
 
-    reduced, reduce_sums = reduce_product(x, reduce_full)
+    reduced, reduce_sums = reduce_product(x, reduce_full, None)
     reduce_sums = exchange(reduce_sums, batches, members, 1)
-    grouped, group_sums = conv(reduced, reduce_sums, reduce_params, forward_taps, masks, count)
+    grouped, group_sums = conv(reduced, reduce_sums, reduce_params, taps, masks, count, None)
     group_sums = exchange(group_sums, batches, members, 1)
-    expanded, expand_sums, act = expand_product(grouped, group_sums, group_params, expand_full, count)
+    expanded, act, expand_sums = expand_product(grouped, group_sums, group_params, expand_full, count, None)
     expand_sums = exchange(expand_sums, batches, members, 2)
-    out, upstream, expand_stats = output(expanded, expand_sums, expand_params, x, grad, count)
+    out, upstream, expand_stats = output(expanded, expand_sums, expand_params, x, grad, count, None)
     expand_stats = exchange(expand_stats, batches, members, 2)
     back, group_up, group_stats = expand_back(
-        expanded, expand_sums, expand_params, upstream, expand_stats, expand_full, grouped, group_sums, group_params, count
+        expanded, expand_sums, expand_params, upstream, expand_stats, expand_full, grouped, group_sums, group_params, count, None
     )
     expand_part = weight_grad(back, act)
     group_stats = exchange(group_stats, batches, members, 1)
-    reduce_up, reduce_stats, taps_part = conv_back(
+    reduce_up, taps_part, reduce_stats = conv_back(
         reduced,
         reduce_sums,
         reduce_params,
@@ -675,9 +1243,10 @@
         group_params,
         group_up,
         group_stats,
-        backward_taps,
+        taps,
         masks,
         count,
+        None,
     )
     reduce_stats = exchange(reduce_stats, batches, members, 1)
     inner, reduce_part = reduce_back(
@@ -695,13 +1264,10 @@
 
     expand_weight_grad = shared_sum(expand_part)
     reduce_weight_grad = shared_sum(reduce_part)
-    taps_part = taps_part.reshape(mids, 9, BLK // GW, GW, GW).transpose(0, 2, 1, 4, 3)
+    taps_part = taps_part[:, : 9 * GW].reshape(-1, 9, GW, HALF // GW, GW).transpose(0, 3, 1, 4, 2)
     taps_part = taps_part.reshape(members, -1, 9, GW, GW)
-    group_weight_grad = lax.all_to_all(taps_part.astype(BF16), "group", 0, 0).astype(F32).sum(0)
+    group_weight_grad = lax.all_to_all(taps_part, "group", 0, 0).astype(F32).sum(0)
     group_weight_grad = lax.psum(group_weight_grad, "batch").reshape(group_weight.shape)
-
-    def own(stats, which, length):
-        return lax.dynamic_slice_in_dim(stats[:, which].reshape(-1), me * length, length, 0)
 
     return (
         block_output,
@@ -709,13 +1275,21 @@
         reduce_weight_grad,
         group_weight_grad,
         expand_weight_grad,
-        own(reduce_stats, 1, local_mid),
-        own(reduce_stats, 0, local_mid),
-        own(group_stats, 1, local_mid),
-        own(group_stats, 0, local_mid),
-        own(expand_stats, 1, channels),
-        own(expand_stats, 0, channels),
-    )
+        own_part(reduce_stats, 1, local_mid),
+        own_part(reduce_stats, 0, local_mid),
+        own_part(group_stats, 1, local_mid),
+        own_part(group_stats, 0, local_mid),
+        own_part(expand_stats, 1, channels),
+        own_part(expand_stats, 0, channels),
+    )
+
+
+def local(*args):
+    block_input = args[0]
+    pixels = block_input.shape[1] // lax.axis_size("group")
+    if block_input.shape[0] == BLK and pixels == 1568 and args[2].shape[0] == HALF and lax.axis_size("batch") == 4:
+        return fused(*args)
+    return modular(*args)
 
 
 def solution(mesh):

time: 1270 us -> 811 us (0.64)
  Pallas kernels: 288 us -> 789 us
  blocking collectives: 422 us -> 0 us
  waiting for transfers between devices: 399 us -> 0 us
  local copies, waits for them, and re-layouts: 76.3 us -> 17 us
  starting transfers between devices: 41.3 us -> 0 us
  other arithmetic: 23.1 us -> 0.21 us
  between operations: 14.1 us -> 0.83 us
    pallas_call x14 -> x11, Pallas kernels: 288 us -> 789 us  [the longest x9 366 us: plain_call(): pl.pallas_call(kernel, grid=grid, in_specs=in_specs, out_specs=out_specs,...]
    all_to_all x7 -> x0, waiting for transfers between devices: 364 us -> none  [the longest x2 180 us: to_pixels(): lax.all_to_all(values.T.reshape(members, pixels, channels), 'group', 0, 0)]
    all_gather x2 -> x0, blocking collectives: 248 us -> none  [gather(): return lax.all_gather(values, 'group', axis=0, tiled=True)]
    all_to_all x2 -> x0, blocking collectives: 174 us -> none  [the longest x1 145 us: to_channels(): moved = lax.all_to_all(values, 'group', 0, 0)]
    all_to_all x7 -> x0, starting transfers between devices: 41.2 us -> none  [the longest x2 12.3 us: shared_sum(): part = lax.all_to_all(part, 'batch', 0, 0).astype(F32).sum(0).astype(BF16)]
    all_gather x4 -> x0, waiting for transfers between devices: 32.6 us -> none  [the longest x2 32.6 us: shared_sum(): return lax.all_gather(part, 'batch', axis=0, tiled=True)]
    transpose x5 -> x1, local copies, waits for them, and re-layouts: 24.3 us -> 1.05 us  [fused(): taps_grad = taps_grad[:9 * GW].reshape(9, GW, -1, GW).transpose(2, 0, 3, 1)]
    reshape x3 -> x6, local copies, waits for them, and re-layouts: 19.4 us -> 2.25 us  [the longest x2 1.3 us: fused(): group_weight.reshape(-1, 9, GW, GW).transpose(1, 2, 0, 3)]
  transfers between devices with their start and end apart: 12 -> 0, of which waited for: 7 -> 0; matrix products, arithmetic and copies ran while one was open for 6% -> 0% of each run, Pallas kernels for 13% -> 0%
where the time goes in v2:
time: 811 us; the launch traced here: 807 us
  Pallas kernels  789 us (97%)
  local copies, waits for them, and re-layouts  17 us (2%)
    pallas_call x9, Pallas kernels, plain_call(): pl.pallas_call(kernel, grid=grid, in_specs=in_specs, out_specs=out_specs,...  366 us
    pallas_call x1, Pallas kernels, closing(): pl.pallas_call(functools.partial(closing_kernel, count, batches, members,...  248 us
    pallas_call x1, Pallas kernels, opening(): pl.pallas_call(functools.partial(opening_kernel, batches, members), in_sp...  174 us

profile of v2, /device:TPU:25, one launch (start us, length us, event | category | flops | bytes accessed | tf_op | source)
XLA Modules:
  0.0 806.7 jit_solution(12696302876690348282)
XLA Ops:
  0.6 1.1 copy.31
  1.8 0.2 reshape.160
  1.9 0.6 pad.4.refs_4_
  2.6 0.7 constant_dynamic-update-slice_fusion.5
  3.3 0.7 constant_dynamic-update-slice_fusion.4
  3.9 0.7 constant_dynamic-update-slice_fusion.3
  4.6 0.7 constant_dynamic-update-slice_fusion.2
  5.2 0.7 constant_dynamic-update-slice_fusion.1
  5.9 0.7 constant_dynamic-update-slice_fusion
  6.6 0.0 copy-start.7
  6.6 0.6 copy-done.7
  7.2 174.5 %shard_map.194 = (bf16[8,1568,256]{2,1,0:T(8,128)(2,1)}, bf16[8,1568,256]{2,1,0:T(8,128)(2,1)}, bf16[8,256,1024]{2,1,0:T(8,128)(2,1)}, bf16[8,256,1024]{2,1,0:T(...) custom-call(bf16[256,12544]{1,0:T(8,128)(2,1)} %refs_0_.1, bf16[256,12544]{1,0:T(8,128)(2,1)} %refs_1_.1, ...), custom_call_target="tpu_custom_call" | custom-call | tf_op jit(solution)/shard_map/pallas_call | solution.py:806
  181.7 0.0 copy-start.4
  181.7 66.2 %shard_map.195 = (f32[4,1568,256]{2,1,0:T(8,128)}, f32[4,2,256]{2,1,0:T(2,128)}, bf16[8,1568,256]{2,1,0:T(8,128)(2,1)}) custom-call(bf16[8,1568,256]{2,1,0:T(8,128)(2,1)} %get-tuple-element.43.refs_0_.refs_3_.refs_5_, bf16[8,256,1024]{2,1,0:T(8,128)(2,1)} %get-tuple-element.44.refs_1_.refs_7_, bf16[8,1568,256]{2,1,0:T(8,128)(2,1)} %get-tuple-element.45.refs_2_.refs_5_.refs_4_), custom_call_target="tpu_custom_call" | custom-call | flops 6576668672 | bytes 20000000 | tf_op jit(solution)/shard_map/pallas_call | solution.py:208
  247.9 0.0 copy-done.4
  247.9 0.6 fusion.3
  248.6 0.1 broadcast_compare_fusion
  248.6 0.1 broadcast_compare_fusion.2
  248.8 2.2 broadcast_in_dim.2.refs_4_.refs_9_
  251.0 57.9 %shard_map.196 = (f32[4,1568,256]{2,1,0:T(8,128)}, f32[4,2,256]{2,1,0:T(2,128)}, bf16[8,1568,256]{2,1,0:T(8,128)(2,1)}) custom-call(f32[4,1568,256]{2,1,0:T(8,128)} %get-tuple-element.46.refs_0_, f32[4,2,256]{2,1,0:T(2,128)} %get-tuple-element.47.refs_1_, f32[4,2,256]{2,1,0:T(2,128)} %get-tuple-element.80.refs_2_, ...), custom_call_target="tpu_custom_call", output_to_operand_aliasing={{2}: (6, {})} | custom-call | flops 7398752256 | bytes 20000000 | tf_op jit(solution)/shard_map/pallas_call | solution.py:208
  308.9 60.7 %shard_map.197 = (f32[8,1568,256]{2,1,0:T(8,128)}, bf16[1568,1024]{1,0:T(8,128)(2,1)}, f32[8,2,256]{2,1,0:T(2,128)}, bf16[8,1568,256]{2,1,0:T(8,128)(2,1)}) custom-call(f32[4,1568,256]{2,1,0:T(8,128)} %get-tuple-element.51.refs_0_.refs_6_.refs_3_, f32[4,2,256]{2,1,0:T(2,128)} %get-tuple-element.52.refs_1_.refs_7_.refs_4_, ...), custom_call_target="tpu_custom_call", output_to_operand_aliasing={{3}: (5, {})} | custom-call | flops 6576668672 | bytes 20000000 | tf_op jit(solution)/shard_map/pallas_call | solution.py:208
  369.6 0.6 reshape.164.refs_2_
  370.2 32.7 %shard_map.198 = (bf16[8,1568,256]{2,1,0:T(8,128)(2,1)}, f32[8,1568,256]{2,1,0:T(8,128)}, f32[8,2,256]{2,1,0:T(2,128)}) custom-call(f32[8,1568,256]{2,1,0:T(8,128)} %get-tuple-element.55.refs_0_, f32[8,2,256]{2,1,0:T(2,128)} %get-tuple-element.56.refs_1_, f32[8,2,256]{2,1,0:T(2,128)} %reshape.164.refs_2_, ...), custom_call_target="tpu_custom_call" | custom-call | flops 64225280 | bytes 20000000 | tf_op jit(solution)/shard_map/pallas_call | solution.py:208
  402.9 48.3 %shard_map.199 = (bf16[8,1568,256]{2,1,0:T(8,128)(2,1)}, f32[4,1568,256]{2,1,0:T(8,128)}, f32[4,2,256]{2,1,0:T(2,128)}, bf16[8,1568,256]{2,1,0:T(8,128)(2,1)}) custom-call(f32[8,1568,256]{2,1,0:T(8,128)} %get-tuple-element.55.refs_0_, f32[8,2,256]{2,1,0:T(2,128)} %get-tuple-element.56.refs_1_, f32[8,2,256]{2,1,0:T(2,128)} %reshape.164.refs_2_, ...), custom_call_target="tpu_custom_call" | custom-call | flops 6576668672 | bytes 20000000 | tf_op jit(solution)/shard_map/pallas_call | solution.py:208
  451.2 12.8 %shard_map.201.refs_8_ = bf16[8,256,1024]{2,1,0:T(8,128)(2,1)} custom-call(bf16[8,1568,256]{2,1,0:T(8,128)(2,1)} %get-tuple-element.66.left_ref, bf16[1568,1024]{1,0:T(8,128)(2,1)} %get-tuple-element.67.right_ref), custom_call_target="tpu_custom_call" | custom-call | flops 6576668672 | bytes 20000000 | tf_op jit(solution)/shard_map/pallas_call | solution.py:208
  464.0 68.9 %shard_map.200 = (f32[4,1568,256]{2,1,0:T(8,128)}, bf16[8,320,128]{2,1,0:T(8,128)(2,1)}, f32[4,2,256]{2,1,0:T(2,128)}, bf16[8,1568,256]{2,1,0:T(8,128)(2,1)}) custom-call(f32[4,1568,256]{2,1,0:T(8,128)} %get-tuple-element.46.refs_0_, f32[4,2,256]{2,1,0:T(2,128)} %get-tuple-element.47.refs_1_, ...), custom_call_target="tpu_custom_call", output_to_operand_aliasing={{3}: (11, {})} | custom-call | flops 14797504512 | bytes 20000000 | tf_op jit(solution)/shard_map/pallas_call | solution.py:208
  532.9 248.4 %shard_map.202 = (bf16[8,1568,256]{2,1,0:T(8,128)(2,1)}, f32[256,1024]{1,0:T(8,128)}, f32[256,1024]{1,0:T(8,128)}, f32[320,128]{1,0:T(8,128)}, bf16[8,1568,256]{2,1,0:T(8,128)(2,1)}) custom-call(f32[4,1568,256]{2,1,0:T(8,128)} %get-tuple-element.46.refs_0_, f32[4,2,256]{2,1,0:T(2,128)} %get-tuple-element.47.refs_1_, ...), custom_call_target="tpu_custom_call", output_to_operand_aliasing={{4}: (11, {})} | custom-call | tf_op jit(solution)/shard_map/pallas_call | solution.py:993
  781.3 9.3 %shard_map.204 = f32[256,12544]{1,0:T(8,128)} custom-call(bf16[12544,256]{1,0:T(8,128)(2,1)} %bitcast.20), custom_call_target="tpu_custom_call" | custom-call | flops 3211264 | bytes 20000000 | tf_op jit(solution)/shard_map/pallas_call | solution.py:208
  790.7 0.0 copy-start.2
  790.7 0.0 copy-start.5
  790.7 0.0 copy-start.6
  790.7 0.0 copy-start.3
  790.7 0.0 copy-start.1
  790.7 0.0 copy-start
  790.7 9.0 %shard_map.203 = bf16[256,12544]{1,0:T(8,128)(2,1)} custom-call(bf16[12544,256]{1,0:T(8,128)(2,1)} %bitcast.19), custom_call_target="tpu_custom_call" | custom-call | flops 3211264 | bytes 20000000 | tf_op jit(solution)/shard_map/pallas_call | solution.py:208
  799.7 0.0 copy-done.2
  799.7 0.3 reshape.167
  800.0 1.1 copy.28
  801.1 0.0 copy-done.5
  801.1 0.6 dynamic_slice.18
  801.7 0.6 dynamic_slice.19
  802.2 0.0 copy-done.6
  802.3 0.6 dynamic_slice.20
  802.8 0.6 dynamic_slice.21
  803.4 0.0 copy-done.3
  803.4 0.6 dynamic_slice.22
  804.1 0.6 dynamic_slice.23
  804.7 0.0 copy-done.1
  804.7 1.0 copy.45
  805.7 0.0 copy-done
  805.7 1.0 copy.46
  (9 shorter events, 0.1 us)
Async XLA Ops:
  6.6 0.6 copy-start.7
  181.7 66.2 %copy-start.4 = (f32[8,8,128]{2,1,0:T(8,128)S(1)}, f32[8,8,128]{2,1,0:T(8,128)}, u32[]{:S(2)}) copy-start(f32[8,8,128]{2,1,0:T(8,128)} %get-tuple-element.48) | copy-start | bytes 98308
  790.7 9.0 %copy-start.2 = (f32[320,128]{1,0:T(8,128)S(1)}, f32[320,128]{1,0:T(8,128)}, u32[]{:S(2)}) copy-start(f32[320,128]{1,0:T(8,128)} %get-tuple-element.73) | copy-start | bytes 491524
  790.7 10.4 %copy-start.5 = (f32[4,2,256]{2,1,0:T(2,128)S(1)}, f32[4,2,256]{2,1,0:T(2,128)}, u32[]{:S(2)}) copy-start(f32[4,2,256]{2,1,0:T(2,128)} %get-tuple-element.65.refs_4_) | copy-start | bytes 24580
  790.7 11.6 %copy-start.6 = (f32[4,2,256]{2,1,0:T(2,128)S(1)}, f32[4,2,256]{2,1,0:T(2,128)}, u32[]{:S(2)}) copy-start(f32[4,2,256]{2,1,0:T(2,128)} %get-tuple-element.62.refs_7_) | copy-start | bytes 24580
  790.7 12.8 %copy-start.3 = (f32[8,2,256]{2,1,0:T(2,128)S(1)}, f32[8,2,256]{2,1,0:T(2,128)}, u32[]{:S(2)}) copy-start(f32[8,2,256]{2,1,0:T(2,128)} %get-tuple-element.59.refs_4_) | copy-start | bytes 49156
  790.7 14.0 %copy-start.1 = (f32[256,1024]{1,0:T(8,128)S(1)}, f32[256,1024]{1,0:T(8,128)}, u32[]{:S(2)}) copy-start(f32[256,1024]{1,0:T(8,128)} %get-tuple-element.102) | copy-start | bytes 3145732
  790.7 15.0 %copy-start = (f32[256,1024]{1,0:T(8,128)S(1)}, f32[256,1024]{1,0:T(8,128)}, u32[]{:S(2)}) copy-start(f32[256,1024]{1,0:T(8,128)} %get-tuple-element.104) | copy-start | bytes 3145732

commit v3 on v2

--- a/solution.py
+++ b/solution.py
@@ -2,6 +2,7 @@
 
 import jax
 import jax.numpy as jnp
+import numpy as np
 from jax import lax
 from jax.experimental import pallas as pl
 from jax.experimental.pallas import tpu as pltpu
@@ -89,24 +90,28 @@
     )
 
 
-def spread(source, target, send, recv, others):
+def each(copies, what):
+    for copy in copies:
+        getattr(copy, what)()
+
+
+def spread(source, target, send, recv, others, beside):
     copies = [
         remote(source, target.at[step], send.at[step], recv.at[step], device) for step, device in enumerate(others)
     ]
-    for copy in copies:
-        copy.start()
-    for copy in copies:
-        copy.wait()
-
-
-def total_stats(ref, across, along, first_ref, second_ref, mid_ref, send1, recv1, send2, recv2):
+    each(copies, "start")
+    each(beside, "start")
+    each(copies, "wait")
+
+
+def total_stats(ref, across, along, first_ref, second_ref, mid_ref, send1, recv1, send2, recv2, beside=((), ())):
     mid_ref[0] = ref[...]
-    spread(mid_ref.at[0], first_ref, send1, recv1, across)
+    spread(mid_ref.at[0], first_ref, send1, recv1, across, beside[0])
     total = mid_ref[0]
     for step in range(len(across)):
         total += first_ref[step]
     mid_ref[1] = total
-    spread(mid_ref.at[1], second_ref, send2, recv2, along)
+    spread(mid_ref.at[1], second_ref, send2, recv2, along, beside[1])
     for step in range(len(along)):
         total += second_ref[step]
     ref[...] = total
@@ -125,18 +130,24 @@
 
 
 class Comm:
-    def __init__(self, batches, members, collective_id, source=None, rows=None, into=None):
+    def __init__(self, batches, members, collective_id, source=None, low=0, sizes=(), into=None, stream=False):
         self.batches, self.members, self.collective_id = batches, members, collective_id
-        self.source, self.rows, self.into = source, rows, into
-
-
-def piece_copies(source, target, rows, me, along, send, recv):
-    rows = pl.ds(*rows)
+        self.source, self.low, self.sizes, self.into, self.stream = source, low, sizes, into, stream
+        self.high = low + sum(sizes)
+
+
+def piece_copies(source, target, low, size, me, along, send, recv, staged=False):
+    rows = pl.ds(low, size)
+    last = len(along)
     copies = [
-        remote(source.at[device[1], rows], target.at[me, rows], send.at[step], recv.at[step], device)
+        remote(
+            source.at[step if staged else device[1], rows], target.at[me, rows], send.at[step], recv.at[step], device
+        )
         for step, device in enumerate(along)
     ]
-    return copies + [pltpu.make_async_copy(source.at[me, rows], target.at[me, rows], send.at[len(along)])]
+    return copies + [
+        pltpu.make_async_copy(source.at[last if staged else me, rows], target.at[me, rows], send.at[last])
+    ]
 
 
 def call(kernel, grid, in_specs, out_specs, out_shape, scratch, flops, comm=None):
@@ -148,53 +159,79 @@
     stats = out_shape[-1].shape
     batches, members = comm.batches, comm.members
 
+    sends = bool(comm.sizes)
+
     def wrapped(*refs):
         refs = list(refs)
         ins = refs[:n_in]
         del refs[:n_in]
-        source = refs.pop(0) if comm.rows else None
+        source = refs.pop(0) if sends and not comm.stream else None
         if comm.into is not None:
             refs.pop(0)
         outs = refs[:n_out]
         del refs[:n_out]
-        target = refs.pop(0) if comm.rows else None
+        target = refs.pop(0) if sends else None
         own = refs[:n_scratch]
         del refs[:n_scratch]
         stats_refs = refs[:7]
         del refs[:7]
+        if comm.stream:
+            source = refs.pop(0)
         row, me, across, along = devices(batches, members)
-
-        def copies():
-            return piece_copies(source, target, comm.rows, me, along, *refs)
-
-        @pl.when(pl.program_id(0) == 0)
+        step = pl.program_id(0)
+
+        def copies(part):
+            low = comm.low + sum(comm.sizes[:part])
+            return piece_copies(
+                source, target, low, comm.sizes[part], me, along, refs[0].at[part], refs[1].at[part], comm.stream
+            )
+
+        @pl.when(step == 0)
         def _():
             greet(across + along)
-            if comm.rows:
-                for copy in copies():
-                    copy.start()
+            if sends and not comm.stream:
+                each(copies(0), "start")
 
         kernel(*ins, *outs, *own)
-
-        @pl.when(pl.program_id(0) == pl.num_programs(0) - 1)
+        if comm.stream:
+            source[step] = outs[0][0, : comm.high]
+            rows = pl.ds(0, comm.sizes[0])
+
+            @pl.when(step < members - 1)
+            def _():
+                device = (row, lax.rem(me + 1 + step, members))
+                remote(
+                    source.at[step, rows], target.at[me, rows], refs[0].at[0, step], refs[1].at[0, step], device
+                ).start()
+
+            @pl.when(step == members - 1)
+            def _():
+                pltpu.make_async_copy(source.at[step, rows], target.at[me, rows], refs[0].at[0, step]).start()
+
+        @pl.when(step == pl.num_programs(0) - 1)
         def _():
-            total_stats(outs[-1], across, along, *stats_refs)
-            if comm.rows:
-                for copy in copies():
-                    copy.wait()
+            total_stats(outs[-1], across, along, *stats_refs, beside=(copies(1), copies(2)) if sends else ((), ()))
+            if sends:
+                for part in range(3):
+                    each(copies(part), "wait")
 
     scratch = list(scratch) + stats_scratch(stats, batches, members)
     in_specs, out_specs, out_shape = list(in_specs), list(out_specs), list(out_shape)
     extra, aliases = [], {}
-    if comm.rows:
-        extra = [comm.source]
+    if sends:
+        if comm.stream:
+            dims, dtype = out_shape[0].shape, out_shape[0].dtype
+            scratch.append(pltpu.VMEM((members, comm.high, dims[2]), dtype))
+        else:
+            dims, dtype = comm.source.shape, comm.source.dtype
+            extra = [comm.source]
         if comm.into is not None:
+            aliases = {len(in_specs) + len(extra): len(out_specs)}
             extra.append(comm.into)
-            aliases = {len(in_specs) + 1: len(out_specs)}
         in_specs += [pl.BlockSpec(memory_space=pl.ANY)] * len(extra)
         out_specs.append(pl.BlockSpec(memory_space=pl.ANY))
-        out_shape.append(shape(comm.source.shape, comm.source.dtype))
-        scratch += [pltpu.SemaphoreType.DMA((members,)), pltpu.SemaphoreType.DMA((members - 1,))]
+        out_shape.append(shape(dims, dtype))
+        scratch += [pltpu.SemaphoreType.DMA((3, members)), pltpu.SemaphoreType.DMA((3, members - 1))]
     params = pltpu.CompilerParams(
         vmem_limit_bytes=VMEM_LIMIT, collective_id=comm.collective_id, has_side_effects=True
     )
@@ -224,6 +261,13 @@
 
 def block(*dims):
     return pl.BlockSpec((1,) + dims, lambda j: (j,) + (0,) * len(dims))
+
+
+def turned_block(members, *dims):
+    def index(j):
+        return (lax.rem(lax.axis_index("group") + 1 + j, members),) + (0,) * len(dims)
+
+    return pl.BlockSpec((1,) + dims, index)
 
 
 def whole(*dims):
@@ -368,13 +412,13 @@
     upsums_ref,
     weight_ref,
     mask_ref,
-    out_ref,
-    wgrad_ref,
-    stat_ref,
-    stack_ref,
-    dense_ref,
-    back_ref,
+    *refs,
 ):
+    *beside, out_ref, wgrad_ref, stat_ref, stack_ref, dense_ref, back_ref = refs
+    if beside:
+        left_ref, act_ref, epart_ref = beside
+        for slot in range(left_ref.shape[0]):
+            weight_grad_block(left_ref[slot], act_ref, epart_ref, slot)
     pixels = red_ref.shape[1]
     spread_weight(weight_ref, dense_ref)
     clear_edges(stack_ref, pixels)
@@ -425,8 +469,19 @@
         wgrad_ref[half, 9 * GW :] = jnp.zeros((wgrad_ref.shape[1] - 9 * GW, HALF), BF16)
 
 
-def conv_back(reduced, sums, params, grouped, gsums, gparams, up, upsums, weight, masks, count, comm):
+def conv_back(reduced, sums, params, grouped, gsums, gparams, up, upsums, weight, masks, count, comm, product=()):
     mids, pixels, _ = reduced.shape
+    more_in, more_out, more_shape = [], [], []
+    if product:
+        left, right = product
+        share = left.shape[0] // mids
+        dims = (share, BLK, right.shape[1])
+        more_in = [
+            pl.BlockSpec((share, pixels, BLK), lambda j: (j, 0, 0)),
+            pl.BlockSpec(right.shape, lambda j: (0, 0), pipeline_mode=pl.Buffered(1)),
+        ]
+        more_out = [pl.BlockSpec(dims, lambda j: (j, 0, 0))]
+        more_shape = [shape((mids * share,) + dims[1:], BF16)]
     return call(
         functools.partial(conv_back_kernel, count),
         (mids,),
@@ -441,9 +496,11 @@
             block(2, BLK),
             pl.BlockSpec((2,) + weight.shape[1:], lambda j: (j, 0, 0)),
             whole(4, pixels, HALF),
-        ],
-        [block(pixels, BLK), pl.BlockSpec((2,) + weight.shape[1:], lambda j: (j, 0, 0)), whole(mids, 2, BLK)],
-        [shape((mids, pixels, BLK)), shape(weight.shape, BF16), shape((mids, 2, BLK))],
+        ]
+        + more_in,
+        more_out
+        + [block(pixels, BLK), pl.BlockSpec((2,) + weight.shape[1:], lambda j: (j, 0, 0)), whole(mids, 2, BLK)],
+        more_shape + [shape((mids, pixels, BLK)), shape(weight.shape, BF16), shape((mids, 2, BLK))],
         [
             pltpu.VMEM((3, 2, pixels + 2 * PAD, HALF), F32),
             pltpu.VMEM((9, BLK, BLK), BF16),
@@ -451,7 +508,7 @@
         ],
         4 * 9 * pixels * mids * BLK * BLK,
         comm,
-    )(reduced, sums, params, grouped, gsums, gparams, up, upsums, weight, masks)
+    )(reduced, sums, params, grouped, gsums, gparams, up, upsums, weight, masks, *product)
 
 
 def expand_kernel(count, grp_ref, gsums_ref, gprm_ref, w_ref, out_ref, act_ref, sum_ref):
@@ -501,10 +558,12 @@
     )(grouped, gsums, gparams, weight)
 
 
-def output_kernel(count, exp_ref, sums_ref, prm_ref, x_ref, grad_ref, out_ref, up_ref, stat_ref):
+def output_kernel(count, members, exp_ref, sums_ref, prm_ref, x_ref, grad_ref, out_ref, up_ref, stat_ref):
     coef = coefficients(sums_ref[0], prm_ref[0], count)
     clear_stats(stat_ref)
     slot = pl.program_id(0)
+    if members:
+        slot = lax.rem(lax.axis_index("group") + 1 + slot, members)
 
     def body(start, size):
         rows = pl.ds(start, size)
@@ -521,11 +580,13 @@
 
 def output(expanded, sums, params, x, grad, count, comm):
     blocks, pixels, _ = expanded.shape
+    members = comm.members if comm else None
+    one = functools.partial(turned_block, members) if comm else block
     return call(
-        functools.partial(output_kernel, count),
+        functools.partial(output_kernel, count, members),
         (blocks,),
-        [block(pixels, BLK), block(2, BLK), block(2, BLK), block(pixels, BLK), block(pixels, BLK)],
-        [block(pixels, BLK), block(pixels, BLK), whole(blocks, 2, BLK)],
+        [one(pixels, BLK), one(2, BLK), one(2, BLK), one(pixels, BLK), one(pixels, BLK)],
+        [one(pixels, BLK), one(pixels, BLK), whole(blocks, 2, BLK)],
         [shape((blocks, pixels, BLK), BF16), shape((blocks, pixels, BLK)), shape((blocks, 2, BLK))],
         [],
         20 * pixels * blocks * BLK,
@@ -729,9 +790,11 @@
 
 
 def opening_kernel(batches, members, *refs):
-    x_ref, grad_ref, wr_ref, we_ref, wg_ref, prm_ref = refs[:6]
-    xp_ref, gradt_ref, wr_out, we_out, wg_out, prm_out = refs[6:12]
-    xin, xturn, gin, gturn, load, own, xsend, xrecv, gsend, psend, precv, wsend, wrecv, fsend, frecv = refs[12:]
+    x_ref, grad_ref, wr_ref, we_ref, wg_ref = refs[:5]
+    vectors = refs[5:11]
+    xp_ref, gradt_ref, wr_out, we_out, wg_out, prm_out = refs[11:17]
+    xin, xturn, gin, gturn, prm_ref, load, own, xsend, xrecv, gsend, psend, precv = refs[17:29]
+    zsend, zrecv, ysend, yrecv, fsend, frecv = refs[29:]
     row, me, across, along = devices(batches, members)
     pixels = xp_ref.shape[1]
     load_x = pltpu.make_async_copy(x_ref, xin, load.at[0])
@@ -739,33 +802,44 @@
     load_x.start()
     load_grad.start()
     weights = [(wr_ref, wr_out), (wg_ref, wg_out), (we_ref, we_out)]
-    local_copies = [pltpu.make_async_copy(prm_ref, prm_out.at[me], own.at[3])]
+    height, side = me // 2, me % 2
+    levels = members // 2
+    line = [(row, lax.rem(me + 2 * step, members)) for step in range(1, levels)]
+    peer = (row, height * 2 + 1 - side)
+    local_copies = []
     parts = []
     for index, (source, target) in enumerate(weights):
         size = source.shape[0] // batches
         part = pl.ds(pl.multiple_of(row * size, 16), size)
         parts.append(part)
-        local_copies.append(pltpu.make_async_copy(source.at[part], target.at[me, part], own.at[index]))
-    for copy in local_copies:
-        copy.start()
+        local_copies.append(pltpu.make_async_copy(source.at[part], target.at[height, side, part], own.at[index]))
+    each(local_copies, "start")
+    place = 0
+    for vector in vectors:
+        for low in range(0, vector.shape[0], HALF):
+            prm_ref[place : place + 1] = vector[low : low + HALF].reshape(1, HALF)
+            place += 1
+    prm_own = pltpu.make_async_copy(prm_ref, prm_out.at[me], own.at[3])
+    prm_own.start()
     greet(across + along)
-    copies = []
-    for step, device in enumerate(along):
-        copies.append(remote(prm_ref, prm_out.at[me], psend.at[step], precv.at[step], device))
+    copies = [prm_own]
     first = []
     for index, (source, target) in enumerate(weights):
-        for step, device in enumerate(along):
+        for step, device in enumerate(line):
             first.append(
                 remote(
                     source.at[parts[index]],
-                    target.at[me, parts[index]],
-                    wsend.at[index, step],
-                    wrecv.at[index, step],
+                    target.at[height, side, parts[index]],
+                    zsend.at[index, step],
+                    zrecv.at[index, step],
                     device,
                 )
             )
-    for copy in copies + first:
+    for step, device in enumerate(along):
+        copy = remote(prm_ref, prm_out.at[me], psend.at[step], precv.at[step], device)
         copy.start()
+        copies.append(copy)
+    each(first, "start")
     load_x.wait()
     for step, device in enumerate(along):
         turn(xin, xturn, step, device[1])
@@ -783,43 +857,51 @@
         copy = pltpu.make_async_copy(turned(gturn, member, member, pixels), gradt_ref.at[member], gsend.at[member])
         copy.start()
         copies.append(copy)
-    for copy in local_copies:
-        copy.wait()
+    each(local_copies, "wait")
+    far, near = (lax.bitwise_xor(row, 2), me), (lax.bitwise_xor(row, 1), me)
+    second, third = [], []
+    for index, (_, target) in enumerate(weights):
+        each(first[index * len(line) : (index + 1) * len(line)], "wait")
+        held = target.at[:, side, parts[index]]
+        second.append(remote(held, held, ysend.at[index], yrecv.at[index], peer))
+        second[-1].start()
+    for index, (_, target) in enumerate(weights):
+        second[index].wait()
+        held = target.at[:, :, parts[index]]
+        third.append(remote(held, held, fsend.at[index, 0], frecv.at[index, 0], far))
+        third[-1].start()
     for index, (source, target) in enumerate(weights):
-        for copy in first[index * len(along) : (index + 1) * len(along)]:
-            copy.wait()
-        for step, device in enumerate(across):
-            held = target.at[:, parts[index]]
-            copy = remote(held, held, fsend.at[index, step], frecv.at[index, step], device)
+        size = source.shape[0] // batches
+        third[index].wait()
+        for step, origin in enumerate((row, lax.bitwise_xor(row, 2))):
+            held = target.at[:, :, pl.ds(pl.multiple_of(origin * size, 16), size)]
+            copy = remote(held, held, fsend.at[index, 1 + step], frecv.at[index, 1 + step], near)
             copy.start()
             copies.append(copy)
-    for copy in copies:
-        copy.wait()
-
-
-def opening(block_input, out_grad, reduce_weight, expand_weight, taps, params, batches, members):
+    each(copies, "wait")
+
+
+def opening(block_input, out_grad, reduce_weight, expand_weight, taps, vectors, batches, members):
     channels, row_pixels = block_input.shape
     pixels = row_pixels // members
     dma = pltpu.SemaphoreType.DMA
-    other, across = members - 1, batches - 1
+    other, across, levels = members - 1, batches - 1, members // 2
     padded = 13 * HALF
-    return pl.pallas_call(
+    lines = sum(vector.shape[0] for vector in vectors) // HALF
+    weights = [reduce_weight, expand_weight, taps]
+    x, grad, *gathered, params = pl.pallas_call(
         functools.partial(opening_kernel, batches, members),
-        in_specs=[pl.BlockSpec(memory_space=pl.ANY)] * 6,
+        in_specs=[pl.BlockSpec(memory_space=pl.ANY)] * 5 + [pl.BlockSpec(memory_space=pltpu.VMEM)] * len(vectors),
         out_specs=[pl.BlockSpec(memory_space=pl.ANY)] * 6,
-        out_shape=[
-            shape((members, pixels, channels), BF16),
-            shape((members, pixels, channels), BF16),
-            shape((members,) + reduce_weight.shape, BF16),
-            shape((members,) + expand_weight.shape, BF16),
-            shape((members,) + taps.shape, BF16),
-            shape((members,) + params.shape),
-        ],
+        out_shape=[shape((members, pixels, channels), BF16)] * 2
+        + [shape((levels, 2) + weight.shape, BF16) for weight in weights]
+        + [shape((members, lines, HALF))],
         scratch_shapes=[
             pltpu.VMEM((channels, row_pixels), BF16),
             pltpu.VMEM((members, padded, channels), BF16),
             pltpu.VMEM((channels, row_pixels), BF16),
             pltpu.VMEM((members, padded, channels), BF16),
+            pltpu.VMEM((lines, HALF), F32),
             dma((2,)),
             dma((4,)),
             dma((members,)),
@@ -827,21 +909,29 @@
             dma((members,)),
             dma((other,)),
             dma((other,)),
-            dma((3, other)),
-            dma((3, other)),
+            dma((3, levels - 1)),
+            dma((3, levels - 1)),
+            dma((3,)),
+            dma((3,)),
             dma((3, across)),
             dma((3, across)),
         ],
         compiler_params=pltpu.CompilerParams(vmem_limit_bytes=VMEM_LIMIT, collective_id=0, has_side_effects=True),
-    )(block_input, out_grad, reduce_weight, expand_weight, taps, params)
+    )(block_input, out_grad, *weights, *vectors)
+    gathered = [full.reshape((members,) + full.shape[2:]) for full in gathered]
+    return x, grad, *gathered, params
 
 
 class Reduce:
-    def __init__(self, part, out, row, me, across, along, refs):
-        self.part, self.out, self.row, self.me, self.across, self.along = part, out, row, me, across, along
-        self.first, self.held, self.second, self.total = refs[:4]
-        self.s1, self.r1, self.s2, self.r2, self.s3, self.r3 = refs[4:]
+    def __init__(self, part, out, row, me, across, refs):
+        self.part, self.out, self.row, self.across = part, out, row, across
+        self.height, self.side = me // 2, me % 2
+        self.first, self.held, self.pair, self.line, self.second, self.total = refs[:6]
+        self.s1, self.r1, self.s2, self.r2, self.s3, self.r3, self.s4, self.r4 = refs[6:]
+        self.levels = self.held.shape[0]
         self.size = self.total.shape[0]
+        self.peer = (row, self.height * 2 + 1 - self.side)
+        self.along = [(row, lax.rem(me + 2 * step, 2 * self.levels)) for step in range(1, self.levels)]
 
     def rows(self, row):
         return pl.ds(pl.multiple_of(row * self.size, 16), self.size)
@@ -855,21 +945,31 @@
         ]
 
     def add_batch(self):
-        @pl.loop(0, self.held.shape[0])
-        def _(member):
-            total = self.part[member, self.rows(self.row)].astype(F32)
-            for step in range(len(self.across)):
-                total += self.first[step, member].astype(F32)
-            self.held[member] = total.astype(BF16)
-
-    def over_group(self):
+        @pl.loop(0, self.levels)
+        def _(level):
+            for side in range(2):
+                total = self.part[2 * level + side, self.rows(self.row)].astype(F32)
+                for step in range(len(self.across)):
+                    total += self.first[step, 2 * level + side].astype(F32)
+                self.held[level, side] = total.astype(BF16)
+
+    def over_pair(self):
+        return [remote(self.held.at[:, 1 - self.side], self.pair, self.s2.at[0], self.r2.at[0], self.peer)]
+
+    def add_pair(self):
+        @pl.loop(0, self.levels)
+        def _(level):
+            total = self.held[level, self.side].astype(F32) + self.pair[level].astype(F32)
+            self.line[level] = total.astype(BF16)
+
+    def over_line(self):
         return [
-            remote(self.held.at[device[1]], self.second.at[step], self.s2.at[step], self.r2.at[step], device)
+            remote(self.line.at[device[1] // 2], self.second.at[step], self.s3.at[step], self.r3.at[step], device)
             for step, device in enumerate(self.along)
         ]
 
-    def add_group(self):
-        total = self.held[self.me].astype(F32)
+    def add_line(self):
+        total = self.line[self.height].astype(F32)
         for step in range(len(self.along)):
             total += self.second[step].astype(F32)
         self.total[...] = total
@@ -877,48 +977,56 @@
     def share(self):
         rows = self.rows(self.row)
         copies = [
-            remote(self.total, self.out.at[rows], self.s3.at[step], self.r3.at[step], device)
+            remote(self.total, self.out.at[rows], self.s4.at[step], self.r4.at[step], device)
             for step, device in enumerate(self.across)
         ]
-        return copies + [pltpu.make_async_copy(self.total, self.out.at[rows], self.s3.at[len(self.across)])]
+        return copies + [pltpu.make_async_copy(self.total, self.out.at[rows], self.s4.at[len(self.across)])]
 
 
 def reduce_scratch(dims, batches, members):
     rows, columns = dims[1] // batches, dims[2]
+    levels = members // 2
     dma = pltpu.SemaphoreType.DMA
     return [
         pltpu.VMEM((batches - 1, members, rows, columns), BF16),
-        pltpu.VMEM((members, rows, columns), BF16),
-        pltpu.VMEM((members - 1, rows, columns), BF16),
+        pltpu.VMEM((levels, 2, rows, columns), BF16),
+        pltpu.VMEM((levels, rows, columns), BF16),
+        pltpu.VMEM((levels, rows, columns), BF16),
+        pltpu.VMEM((levels - 1, rows, columns), BF16),
         pltpu.VMEM((rows, columns), F32),
         dma((batches - 1,)),
         dma((batches - 1,)),
-        dma((members - 1,)),
-        dma((members - 1,)),
+        dma((1,)),
+        dma((1,)),
+        dma((levels - 1,)),
+        dma((levels - 1,)),
         dma((batches,)),
         dma((batches - 1,)),
     ]
 
 
-def each(copies, what):
-    for copy in copies:
-        getattr(copy, what)()
-
-
-def closing_kernel(count, batches, members, rows, *refs):
+HELD_BACK = 2
+
+
+def closing_kernel(count, batches, members, low, size, *refs):
     red_ref, sums_ref, prm_ref, rup_ref, rupsums_ref, x_ref, up_ref, w_ref, epart_ref, tpart_ref, src_ref, _ = refs[:12]
     recv_ref, rout_ref, eout_ref, tout_ref, dst_ref = refs[12:17]
     back_ref, grad_ref, wpart_ref, gsend, grecv, psend, precv = refs[17:24]
     row, me, across, along = devices(batches, members)
     step = pl.program_id(0)
     last = members - 1
-    expand_sum = Reduce(epart_ref, eout_ref, row, me, across, along, refs[24:34])
-    taps_sum = Reduce(tpart_ref, tout_ref, row, me, across, along, refs[34:44])
-    reduce_sum = Reduce(wpart_ref, rout_ref, row, me, across, along, refs[44:54])
+    expand_sum = Reduce(epart_ref, eout_ref, row, me, across, refs[24:38])
+    taps_sum = Reduce(tpart_ref, tout_ref, row, me, across, refs[38:52])
+    reduce_sum = Reduce(wpart_ref, rout_ref, row, me, across, refs[52:66])
+    parts = (expand_sum, taps_sum, reduce_sum)
     other = lax.rem(me + 1 + step, members)
 
     def pieces():
-        return piece_copies(src_ref, dst_ref, rows, me, along, psend, precv)
+        return piece_copies(src_ref, dst_ref, low, size, me, along, psend, precv)
+
+    def send(index):
+        device = (row, lax.rem(me + 1 + index, members))
+        return remote(grad_ref.at[index], recv_ref.at[me], gsend.at[index], grecv.at[index], device)
 
     @pl.when(step == 0)
     def _():
@@ -935,9 +1043,9 @@
 
     over_rows(x_ref.shape[1], product)
 
-    @pl.when(step < last)
+    @pl.when(step < last - HELD_BACK)
     def _():
-        remote(grad_ref.at[step], recv_ref.at[me], gsend.at[step], grecv.at[step], (row, other)).start()
+        send(step).start()
 
     weight_grad_block(x_ref[0], back_ref, wpart_ref, other)
 
@@ -946,23 +1054,31 @@
         own = pltpu.make_async_copy(grad_ref.at[last], recv_ref.at[me], gsend.at[last])
         own.start()
         each(reduce_sum.over_batch(), "start")
-        for part in (expand_sum, taps_sum, reduce_sum):
+        for part in parts:
             each(part.over_batch(), "wait")
             part.add_batch()
-            each(part.over_group(), "start")
+            each(part.over_pair(), "start")
+        for part in parts:
+            each(part.over_pair(), "wait")
+            part.add_pair()
+            each(part.over_line(), "start")
+        for index in range(last - HELD_BACK, last):
+            send(index).start()
+        for part in parts:
+            each(part.over_line(), "wait")
+            part.add_line()
+            each(part.share(), "start")
         own.wait()
         each(pieces(), "wait")
-        for past, device in enumerate(along):
-            remote(grad_ref.at[past], recv_ref.at[me], gsend.at[past], grecv.at[past], device).wait()
-        for part in (expand_sum, taps_sum, reduce_sum):
-            each(part.over_group(), "wait")
-            part.add_group()
-            each(part.share(), "start")
-        for part in (expand_sum, taps_sum, reduce_sum):
+        for index in range(last):
+            send(index).wait()
+        for part in parts:
             each(part.share(), "wait")
 
 
-def closing(reduced, sums, params, rup, rupsums, x, up, weight, epart, tpart, source, into, rows, count, batches, members):
+def closing(
+    reduced, sums, params, rup, rupsums, x, up, weight, epart, tpart, source, into, low, size, count, batches, members
+):
     mids, pixels, _ = reduced.shape
     blocks = x.shape[0]
     once = pl.Buffered(1)
@@ -970,12 +1086,7 @@
     def keep(*dims):
         return pl.BlockSpec(dims, lambda j: (0,) * len(dims), pipeline_mode=once)
 
-    def turn_block(*dims):
-        def index(j):
-            return (lax.rem(lax.axis_index("group") + 1 + j, members),) + (0,) * len(dims)
-
-        return pl.BlockSpec((1,) + dims, index)
-
+    turn_block = functools.partial(turned_block, members)
     anywhere = pl.BlockSpec(memory_space=pl.ANY)
     dma = pltpu.SemaphoreType.DMA
     wdims = (blocks, BLK, mids * BLK)
@@ -991,7 +1102,7 @@
     for dims in (wdims, tpart.shape, wdims):
         scratch += reduce_scratch(dims, batches, members)
     return pl.pallas_call(
-        functools.partial(closing_kernel, count, batches, members, rows),
+        functools.partial(closing_kernel, count, batches, members, low, size),
         grid=(blocks,),
         in_specs=[
             keep(mids, pixels, BLK),
@@ -1041,10 +1152,10 @@
 
 
 def pixel_masks(pixels):
-    place = jnp.arange(pixels, dtype=jnp.int32)
+    place = np.arange(pixels)
     tall, wide = (place // SIDE) % SIDE, place % SIDE
-    masks = jnp.stack([wide != 0, wide != SIDE - 1, tall != 0, tall != SIDE - 1])
-    return jnp.broadcast_to(masks[:, :, None].astype(F32), (4, pixels, HALF))
+    masks = np.stack([wide != 0, wide != SIDE - 1, tall != 0, tall != SIDE - 1])
+    return jnp.asarray(np.broadcast_to(masks[:, :, None], (4, pixels, HALF)).astype(np.float32))
 
 
 def own_part(stats, which, length):
@@ -1072,30 +1183,28 @@
     pixels = row_pixels // members
     count = row_pixels * batches
     local_mid = reduce_gain.shape[0]
-    pack = jnp.concatenate([reduce_gain, reduce_bias, group_gain, group_bias, expand_gain, expand_bias]).reshape(-1, HALF)
+    vectors = [reduce_gain, reduce_bias, group_gain, group_bias, expand_gain, expand_bias]
     taps = group_weight.reshape(-1, 9, GW, GW).transpose(1, 2, 0, 3).reshape(9 * GW, HALF)
     taps = jnp.pad(taps, ((0, TAP_ROWS - 9 * GW), (0, 0)))
     masks = pixel_masks(pixels)
     x, grad_turned, reduce_full, expand_full, taps_full, packs = opening(
-        block_input, out_grad, reduce_weight, expand_weight, taps, pack, batches, members
+        block_input, out_grad, reduce_weight, expand_weight, taps, vectors, batches, members
     )
     vectors = packs[:, :4].reshape(-1, 2, 4, HALF).transpose(0, 2, 1, 3).reshape(-1, 4, BLK)
     reduce_params, group_params = vectors[:, :2], vectors[:, 2:]
     expand_params = packs[:, 4:].reshape(-1, 2, BLK)
 
-    def comm(collective_id, source=None, rows=None, into=None):
-        return Comm(batches, members, collective_id, source, rows, into)
-
-    first, second = 448, 1008
-    reduced, reduce_sums, grad = reduce_product(x, reduce_full, comm(1, grad_turned, (0, first)))
-    grouped, group_sums, grad = conv(
-        reduced, reduce_sums, reduce_params, taps_full, masks, count, comm(2, grad_turned, (first, second - first), grad)
-    )
-    expanded, act, expand_sums, grad = expand_product(
-        grouped, group_sums, group_params, expand_full, count, comm(3, grad_turned, (second, pixels - second), grad)
-    )
-    out, upstream, expand_stats = output(expanded, expand_sums, expand_params, x, grad, count, comm(4))
-    first, second = 448, 1120
+    comm = functools.partial(Comm, batches, members)
+    beside = (64, 48)
+    sends = comm(1, grad_turned, 0, (336,) + beside)
+    reduced, reduce_sums, grad = reduce_product(x, reduce_full, sends)
+    sends = comm(2, grad_turned, sends.high, (448,) + beside, grad)
+    grouped, group_sums, grad = conv(reduced, reduce_sums, reduce_params, taps_full, masks, count, sends)
+    sends = comm(3, grad_turned, sends.high, (pixels - sends.high - sum(beside),) + beside, grad)
+    expanded, act, expand_sums, grad = expand_product(grouped, group_sums, group_params, expand_full, count, sends)
+    sends = comm(4, None, 0, (224,) + beside, None, True)
+    out, upstream, expand_stats, moved = output(expanded, expand_sums, expand_params, x, grad, count, sends)
+    sends = comm(5, out, sends.high, (304,) + beside, moved)
     back, group_up, group_stats, moved = expand_back(
         expanded,
         expand_sums,
@@ -1107,9 +1216,10 @@
         group_sums,
         group_params,
         count,
-        comm(5, out, (0, first)),
+        sends,
     )
-    reduce_up, taps_part, reduce_stats, moved = conv_back(
+    sends = comm(6, out, sends.high, (560,) + beside, moved)
+    expand_part, reduce_up, taps_part, reduce_stats, moved = conv_back(
         reduced,
         reduce_sums,
         reduce_params,
@@ -1121,9 +1231,9 @@
         taps_full,
         masks,
         count,
-        comm(6, out, (first, second - first), moved),
+        sends,
+        (back, act),
     )
-    expand_part = weight_grad(back, act)
     inner, reduce_weight_grad, expand_weight_grad, taps_grad, moved = closing(
         reduced,
         reduce_sums,
@@ -1137,7 +1247,8 @@
         taps_part,
         out,
         moved,
-        (second, pixels - second),
+        sends.high,
+        pixels - sends.high,
         count,
         batches,
         members,
@@ -1287,7 +1398,7 @@
 def local(*args):
     block_input = args[0]
     pixels = block_input.shape[1] // lax.axis_size("group")
-    if block_input.shape[0] == BLK and pixels == 1568 and args[2].shape[0] == HALF and lax.axis_size("batch") == 4:
+    if block_input.shape[0] == BLK and pixels == 1568 and args[2].shape[0] == HALF and lax.axis_size("group") == 8:
         return fused(*args)
     return modular(*args)
 

time: 811 us -> 734 us (0.905)
  Pallas kernels: 789 us -> 716 us
    pallas_call x1, Pallas kernels: 248 us -> 199 us  [closing(): pl.pallas_call(functools.partial(closing_kernel, count, batches, members,...]
    pallas_call x1, Pallas kernels: 174 us -> 151 us  [opening(): pl.pallas_call(functools.partial(opening_kernel, batches, members), in_sp...]
    pallas_call x9 -> x8, Pallas kernels: 366 us -> 367 us  [plain_call(): pl.pallas_call(kernel, grid=grid, in_specs=in_specs, out_specs=out_specs,...]
where the time goes in v3:
time: 734 us; the launch traced here: 727 us
  Pallas kernels  716 us (98%)
  local copies, waits for them, and re-layouts  10.2 us (1%)
    pallas_call x8, Pallas kernels, plain_call(): pl.pallas_call(kernel, grid=grid, in_specs=in_specs, out_specs=out_specs,...  367 us
    pallas_call x1, Pallas kernels, closing(): pl.pallas_call(functools.partial(closing_kernel, count, batches, members,...  199 us
    pallas_call x1, Pallas kernels, opening(): pl.pallas_call(functools.partial(opening_kernel, batches, members), in_sp...  151 us

profile of v3, /device:TPU:25, one launch (start us, length us, event | category | flops | bytes accessed | tf_op | source)
XLA Modules:
  0.0 727.4 jit_solution(13818310167599652791)
XLA Ops:
  0.6 1.1 copy.33
  1.8 0.2 reshape.59
  1.9 0.6 pad.4.refs_4_
  2.6 150.7 %shard_map.203 = (bf16[8,1568,256]{2,1,0:T(8,128)(2,1)}, bf16[8,1568,256]{2,1,0:T(8,128)(2,1)}, bf16[4,2,256,1024]{3,2,1,0:T(8,128)(2,1)}, bf16[4,2,256,1024]{3,...) custom-call(bf16[256,12544]{1,0:T(8,128)(2,1)} %refs_0_.1, bf16[256,12544]{1,0:T(8,128)(2,1)} %refs_1_.1, ...), custom_call_target="tpu_custom_call" | custom-call | tf_op jit(solution)/shard_map/pallas_call | solution.py:892
  153.3 0.0 copy-start.4
  153.3 66.1 %shard_map.204 = (f32[4,1568,256]{2,1,0:T(8,128)}, f32[4,2,256]{2,1,0:T(2,128)}, bf16[8,1568,256]{2,1,0:T(8,128)(2,1)}) custom-call(bf16[8,1568,256]{2,1,0:T(8,128)(2,1)} %get-tuple-element.45.refs_0_.refs_3_.refs_5_, bf16[8,256,1024]{2,1,0:T(8,128)(2,1)} %bitcast.25, bf16[8,1568,256]{2,1,0:T(8,128)(2,1)} %get-tuple-element.47.refs_2_.refs_5_.refs_4_), custom_call_target="tpu_custom_call" | custom-call | flops 6576668672 | bytes 20000000 | tf_op jit(solution)/shard_map/pallas_call | solution.py:245
  219.4 0.0 copy-done.4
  219.5 0.6 fusion.2
  220.1 58.6 %shard_map.205 = (f32[4,1568,256]{2,1,0:T(8,128)}, f32[4,2,256]{2,1,0:T(2,128)}, bf16[8,1568,256]{2,1,0:T(8,128)(2,1)}) custom-call(f32[4,1568,256]{2,1,0:T(8,128)} %get-tuple-element.48.refs_0_, f32[4,2,256]{2,1,0:T(2,128)} %get-tuple-element.49.refs_1_, f32[4,2,256]{2,1,0:T(2,128)} %get-tuple-element.84.refs_2_, ...), custom_call_target="tpu_custom_call", output_to_operand_aliasing={{2}: (6, {})} | custom-call | flops 7398752256 | bytes 20000000 | tf_op jit(solution)/shard_map/pallas_call | solution.py:245
  278.7 60.0 %shard_map.206 = (f32[8,1568,256]{2,1,0:T(8,128)}, bf16[1568,1024]{1,0:T(8,128)(2,1)}, f32[8,2,256]{2,1,0:T(2,128)}, bf16[8,1568,256]{2,1,0:T(8,128)(2,1)}) custom-call(f32[4,1568,256]{2,1,0:T(8,128)} %get-tuple-element.53.refs_0_.refs_6_.refs_3_, f32[4,2,256]{2,1,0:T(2,128)} %get-tuple-element.54.refs_1_.refs_7_.refs_4_, ...), custom_call_target="tpu_custom_call", output_to_operand_aliasing={{3}: (5, {})} | custom-call | flops 6576668672 | bytes 20000000 | tf_op jit(solution)/shard_map/pallas_call | solution.py:245
  338.7 0.6 reshape.65.refs_2_
  339.3 44.0 %shard_map.207 = (bf16[8,1568,256]{2,1,0:T(8,128)(2,1)}, f32[8,1568,256]{2,1,0:T(8,128)}, f32[8,2,256]{2,1,0:T(2,128)}, bf16[8,1568,256]{2,1,0:T(8,128)(2,1)}) custom-call(f32[8,1568,256]{2,1,0:T(8,128)} %get-tuple-element.57.refs_0_, f32[8,2,256]{2,1,0:T(2,128)} %get-tuple-element.58.refs_1_, f32[8,2,256]{2,1,0:T(2,128)} %reshape.65.refs_2_, ...), custom_call_target="tpu_custom_call" | custom-call | flops 64225280 | bytes 20000000 | tf_op jit(solution)/shard_map/pallas_call | solution.py:245
  383.4 48.8 %shard_map.208 = (bf16[8,1568,256]{2,1,0:T(8,128)(2,1)}, f32[4,1568,256]{2,1,0:T(8,128)}, f32[4,2,256]{2,1,0:T(2,128)}, bf16[8,1568,256]{2,1,0:T(8,128)(2,1)}) custom-call(f32[8,1568,256]{2,1,0:T(8,128)} %get-tuple-element.57.refs_0_, f32[8,2,256]{2,1,0:T(2,128)} %get-tuple-element.58.refs_1_, ...), custom_call_target="tpu_custom_call", output_to_operand_aliasing={{3}: (10, {})} | custom-call | flops 6576668672 | bytes 20000000 | tf_op jit(solution)/shard_map/pallas_call | solution.py:245
  432.2 70.9 %shard_map.209 = (bf16[8,256,1024]{2,1,0:T(8,128)(2,1)}, f32[4,1568,256]{2,1,0:T(8,128)}, bf16[8,320,128]{2,1,0:T(8,128)(2,1)}, f32[4,2,256]{2,1,0:T(2,128)}, bf16[8,1568,256]{2,1,0:T(8,128)(2,1)}) custom-call(f32[4,1568,256]{2,1,0:T(8,128)} %get-tuple-element.48.refs_0_, f32[4,2,256]{2,1,0:T(2,128)} %get-tuple-element.49.refs_1_, ...), custom_call_target="tpu_custom_call", output_to_operand_aliasing={{4}: (13, {})} | custom-call | flops 14797504512 | bytes 20000000 | tf_op jit(solution)/shard_map/pallas_call | solution.py:245
  503.0 199.1 %shard_map.210 = (bf16[8,1568,256]{2,1,0:T(8,128)(2,1)}, f32[256,1024]{1,0:T(8,128)}, f32[256,1024]{1,0:T(8,128)}, f32[320,128]{1,0:T(8,128)}, bf16[8,1568,256]{2,1,0:T(8,128)(2,1)}) custom-call(f32[4,1568,256]{2,1,0:T(8,128)} %get-tuple-element.48.refs_0_, f32[4,2,256]{2,1,0:T(2,128)} %get-tuple-element.49.refs_1_, ...), custom_call_target="tpu_custom_call", output_to_operand_aliasing={{4}: (11, {})} | custom-call | tf_op jit(solution)/shard_map/pallas_call | solution.py:1104
  702.1 9.3 %shard_map.212 = f32[256,12544]{1,0:T(8,128)} custom-call(bf16[12544,256]{1,0:T(8,128)(2,1)} %bitcast.22), custom_call_target="tpu_custom_call" | custom-call | flops 3211264 | bytes 20000000 | tf_op jit(solution)/shard_map/pallas_call | solution.py:245
  711.4 0.0 copy-start.2
  711.4 0.0 copy-start.5
  711.4 0.0 copy-start.6
  711.4 0.0 copy-start.3
  711.5 0.0 copy-start.1
  711.5 0.0 copy-start
  711.5 9.0 %shard_map.211 = bf16[256,12544]{1,0:T(8,128)(2,1)} custom-call(bf16[12544,256]{1,0:T(8,128)(2,1)} %bitcast.21), custom_call_target="tpu_custom_call" | custom-call | flops 3211264 | bytes 20000000 | tf_op jit(solution)/shard_map/pallas_call | solution.py:245
  720.5 0.0 copy-done.2
  720.5 0.3 reshape.68
  720.8 1.1 copy.30
  721.8 0.0 copy-done.5
  721.8 0.6 dynamic_slice.18
  722.4 0.6 dynamic_slice.19
  723.0 0.0 copy-done.6
  723.0 0.6 dynamic_slice.20
  723.6 0.6 dynamic_slice.21
  724.2 0.0 copy-done.3
  724.2 0.6 dynamic_slice.22
  724.9 0.6 dynamic_slice.23
  725.5 0.0 copy-done.1
  725.5 1.0 copy.42
  726.5 0.0 copy-done
  726.5 1.0 copy.43
  (7 shorter events, 0.1 us)
Async XLA Ops:
  153.3 66.2 %copy-start.4 = (f32[8,8,128]{2,1,0:T(8,128)S(1)}, f32[8,8,128]{2,1,0:T(8,128)}, u32[]{:S(2)}) copy-start(f32[8,8,128]{2,1,0:T(8,128)} %get-tuple-element.50) | copy-start | bytes 98308
  711.4 9.0 %copy-start.2 = (f32[320,128]{1,0:T(8,128)S(1)}, f32[320,128]{1,0:T(8,128)}, u32[]{:S(2)}) copy-start(f32[320,128]{1,0:T(8,128)} %get-tuple-element.77) | copy-start | bytes 491524
  711.4 10.4 %copy-start.5 = (f32[4,2,256]{2,1,0:T(2,128)S(1)}, f32[4,2,256]{2,1,0:T(2,128)}, u32[]{:S(2)}) copy-start(f32[4,2,256]{2,1,0:T(2,128)} %get-tuple-element.70.refs_4_) | copy-start | bytes 24580
  711.4 11.6 %copy-start.6 = (f32[4,2,256]{2,1,0:T(2,128)S(1)}, f32[4,2,256]{2,1,0:T(2,128)}, u32[]{:S(2)}) copy-start(f32[4,2,256]{2,1,0:T(2,128)} %get-tuple-element.65.refs_7_) | copy-start | bytes 24580
  711.4 12.8 %copy-start.3 = (f32[8,2,256]{2,1,0:T(2,128)S(1)}, f32[8,2,256]{2,1,0:T(2,128)}, u32[]{:S(2)}) copy-start(f32[8,2,256]{2,1,0:T(2,128)} %get-tuple-element.61.refs_4_) | copy-start | bytes 49156
  711.5 14.0 %copy-start.1 = (f32[256,1024]{1,0:T(8,128)S(1)}, f32[256,1024]{1,0:T(8,128)}, u32[]{:S(2)}) copy-start(f32[256,1024]{1,0:T(8,128)} %get-tuple-element.102) | copy-start | bytes 3145732
  711.5 15.0 %copy-start = (f32[256,1024]{1,0:T(8,128)S(1)}, f32[256,1024]{1,0:T(8,128)}, u32[]{:S(2)}) copy-start(f32[256,1024]{1,0:T(8,128)} %get-tuple-element.104) | copy-start | bytes 3145732

commit v4 on v3

--- a/solution.py
+++ b/solution.py
@@ -104,16 +104,16 @@
     each(copies, "wait")
 
 
-def total_stats(ref, across, along, first_ref, second_ref, mid_ref, send1, recv1, send2, recv2, beside=((), ())):
+def total_stats(ref, across, along, first_ref, second_ref, mid_ref, send1, recv1, send2, recv2, beside=()):
     mid_ref[0] = ref[...]
-    spread(mid_ref.at[0], first_ref, send1, recv1, across, beside[0])
+    spread(mid_ref.at[0], second_ref, send2, recv2, along, beside)
     total = mid_ref[0]
+    for step in range(len(along)):
+        total += second_ref[step]
+    mid_ref[1] = total
+    spread(mid_ref.at[1], first_ref, send1, recv1, across, ())
     for step in range(len(across)):
         total += first_ref[step]
-    mid_ref[1] = total
-    spread(mid_ref.at[1], second_ref, send2, recv2, along, beside[1])
-    for step in range(len(along)):
-        total += second_ref[step]
     ref[...] = total
 
 
@@ -150,8 +150,14 @@
     ]
 
 
+class Late:
+    def __init__(self, dims, dtype=F32):
+        self.dims, self.dtype = dims, dtype
+
+
 def call(kernel, grid, in_specs, out_specs, out_shape, scratch, flops, comm=None):
     if comm is None:
+        in_specs = [whole(*spec.dims) if isinstance(spec, Late) else spec for spec in in_specs]
         return functools.partial(
             plain_call, kernel, grid, in_specs, out_specs, out_shape, scratch, flops, pltpu.CompilerParams(vmem_limit_bytes=VMEM_LIMIT)
         )
@@ -160,6 +166,8 @@
     batches, members = comm.batches, comm.members
 
     sends = bool(comm.sizes)
+    late = [index for index, spec in enumerate(in_specs) if isinstance(spec, Late)]
+    late_specs = [in_specs[index] for index in late]
 
     def wrapped(*refs):
         refs = list(refs)
@@ -177,6 +185,13 @@
         del refs[:7]
         if comm.stream:
             source = refs.pop(0)
+        loads = []
+        if late:
+            load_sem = refs.pop(0)
+            for place, index in enumerate(late):
+                held = refs.pop(0)
+                loads.append(pltpu.make_async_copy(ins[index], held, load_sem.at[place]))
+                ins[index] = held
         row, me, across, along = devices(batches, members)
         step = pl.program_id(0)
 
@@ -191,6 +206,8 @@
             greet(across + along)
             if sends and not comm.stream:
                 each(copies(0), "start")
+            each(loads, "start")
+            each(loads, "wait")
 
         kernel(*ins, *outs, *own)
         if comm.stream:
@@ -210,9 +227,9 @@
 
         @pl.when(step == pl.num_programs(0) - 1)
         def _():
-            total_stats(outs[-1], across, along, *stats_refs, beside=(copies(1), copies(2)) if sends else ((), ()))
+            total_stats(outs[-1], across, along, *stats_refs, beside=copies(1) if sends else ())
             if sends:
-                for part in range(3):
+                for part in range(2):
                     each(copies(part), "wait")
 
     scratch = list(scratch) + stats_scratch(stats, batches, members)
@@ -228,10 +245,14 @@
         if comm.into is not None:
             aliases = {len(in_specs) + len(extra): len(out_specs)}
             extra.append(comm.into)
+        in_specs = [pl.BlockSpec(memory_space=pl.ANY) if isinstance(spec, Late) else spec for spec in in_specs]
         in_specs += [pl.BlockSpec(memory_space=pl.ANY)] * len(extra)
+        if late:
+            scratch.append(pltpu.SemaphoreType.DMA((len(late),)))
+            scratch += [pltpu.VMEM(spec.dims, spec.dtype) for spec in late_specs]
         out_specs.append(pl.BlockSpec(memory_space=pl.ANY))
         out_shape.append(shape(dims, dtype))
-        scratch += [pltpu.SemaphoreType.DMA((3, members)), pltpu.SemaphoreType.DMA((3, members - 1))]
+        scratch += [pltpu.SemaphoreType.DMA((2, members)), pltpu.SemaphoreType.DMA((2, members - 1))]
     params = pltpu.CompilerParams(
         vmem_limit_bytes=VMEM_LIMIT, collective_id=comm.collective_id, has_side_effects=True
     )
@@ -295,7 +316,7 @@
     return call(
         reduce_kernel,
         (mids,),
-        [whole(blocks, pixels, BLK), pl.BlockSpec((blocks, BLK, BLK), lambda j: (0, 0, j))],
+        [Late((blocks, pixels, BLK), BF16), pl.BlockSpec((blocks, BLK, BLK), lambda j: (0, 0, j))],
         [block(pixels, BLK), whole(mids, 2, BLK)],
         [shape((mids, pixels, BLK)), shape((mids, 2, BLK))],
         [],
@@ -390,7 +411,7 @@
             block(2, BLK),
             block(2, BLK),
             pl.BlockSpec((2,) + weight.shape[1:], lambda j: (j, 0, 0)),
-            whole(4, pixels, HALF),
+            Late((4, pixels, HALF)),
         ],
         [block(pixels, BLK), whole(mids, 2, BLK)],
         [shape((mids, pixels, BLK)), shape((mids, 2, BLK))],
@@ -414,11 +435,7 @@
     mask_ref,
     *refs,
 ):
-    *beside, out_ref, wgrad_ref, stat_ref, stack_ref, dense_ref, back_ref = refs
-    if beside:
-        left_ref, act_ref, epart_ref = beside
-        for slot in range(left_ref.shape[0]):
-            weight_grad_block(left_ref[slot], act_ref, epart_ref, slot)
+    out_ref, wgrad_ref, stat_ref, stack_ref, dense_ref, back_ref = refs
     pixels = red_ref.shape[1]
     spread_weight(weight_ref, dense_ref)
     clear_edges(stack_ref, pixels)
@@ -469,19 +486,8 @@
         wgrad_ref[half, 9 * GW :] = jnp.zeros((wgrad_ref.shape[1] - 9 * GW, HALF), BF16)
 
 
-def conv_back(reduced, sums, params, grouped, gsums, gparams, up, upsums, weight, masks, count, comm, product=()):
+def conv_back(reduced, sums, params, grouped, gsums, gparams, up, upsums, weight, masks, count, comm):
     mids, pixels, _ = reduced.shape
-    more_in, more_out, more_shape = [], [], []
-    if product:
-        left, right = product
-        share = left.shape[0] // mids
-        dims = (share, BLK, right.shape[1])
-        more_in = [
-            pl.BlockSpec((share, pixels, BLK), lambda j: (j, 0, 0)),
-            pl.BlockSpec(right.shape, lambda j: (0, 0), pipeline_mode=pl.Buffered(1)),
-        ]
-        more_out = [pl.BlockSpec(dims, lambda j: (j, 0, 0))]
-        more_shape = [shape((mids * share,) + dims[1:], BF16)]
     return call(
         functools.partial(conv_back_kernel, count),
         (mids,),
@@ -495,12 +501,10 @@
             block(pixels, BLK),
             block(2, BLK),
             pl.BlockSpec((2,) + weight.shape[1:], lambda j: (j, 0, 0)),
-            whole(4, pixels, HALF),
-        ]
-        + more_in,
-        more_out
-        + [block(pixels, BLK), pl.BlockSpec((2,) + weight.shape[1:], lambda j: (j, 0, 0)), whole(mids, 2, BLK)],
-        more_shape + [shape((mids, pixels, BLK)), shape(weight.shape, BF16), shape((mids, 2, BLK))],
+            Late((4, pixels, HALF)),
+        ],
+        [block(pixels, BLK), pl.BlockSpec((2,) + weight.shape[1:], lambda j: (j, 0, 0)), whole(mids, 2, BLK)],
+        [shape((mids, pixels, BLK)), shape(weight.shape, BF16), shape((mids, 2, BLK))],
         [
             pltpu.VMEM((3, 2, pixels + 2 * PAD, HALF), F32),
             pltpu.VMEM((9, BLK, BLK), BF16),
@@ -508,7 +512,7 @@
         ],
         4 * 9 * pixels * mids * BLK * BLK,
         comm,
-    )(reduced, sums, params, grouped, gsums, gparams, up, upsums, weight, masks, *product)
+    )(reduced, sums, params, grouped, gsums, gparams, up, upsums, weight, masks)
 
 
 def expand_kernel(count, grp_ref, gsums_ref, gprm_ref, w_ref, out_ref, act_ref, sum_ref):
@@ -545,7 +549,7 @@
         functools.partial(expand_kernel, count),
         (blocks,),
         [
-            whole(mids, pixels, BLK),
+            Late((mids, pixels, BLK)),
             whole(mids, 2, BLK),
             whole(mids, 2, BLK),
             block(BLK, mids * BLK),
@@ -605,7 +609,8 @@
     grp_ref,
     gsums_ref,
     gprm_ref,
-    back_ref,
+    act_ref,
+    wgrad_ref,
     out_ref,
     stat_ref,
     keep_ref,
@@ -625,10 +630,10 @@
             rows = pl.ds(start, size)
             standard, _ = standardize(exp_ref[0, rows], coef)
             values = (scale * (up_ref[0, rows] - up_mean - standard * up_lean)).astype(BF16)
-            back_ref[0, rows] = values
             keep_ref[step, rows] = values
 
         over_rows(pixels, back)
+        weight_grad_block(keep_ref[step], act_ref, wgrad_ref, 0)
 
     @pl.when(step >= blocks)
     def _():
@@ -647,7 +652,7 @@
         over_rows(pixels, body)
 
 
-def expand_back(expanded, sums, params, up, upsums, weight, grouped, gsums, gparams, count, comm):
+def expand_back(expanded, sums, params, up, upsums, weight, grouped, gsums, gparams, act, count, comm):
     blocks, pixels, _ = expanded.shape
     mids = grouped.shape[0]
 
@@ -670,36 +675,21 @@
             second(pixels, BLK),
             second(2, BLK),
             second(2, BLK),
+            Late((pixels, mids * BLK), BF16),
         ],
-        [first(pixels, BLK), second(pixels, BLK), whole(mids, 2, BLK)],
-        [shape((blocks, pixels, BLK), BF16), shape((mids, pixels, BLK)), shape((mids, 2, BLK))],
+        [first(BLK, mids * BLK), second(pixels, BLK), whole(mids, 2, BLK)],
+        [shape((blocks, BLK, mids * BLK), BF16), shape((mids, pixels, BLK)), shape((mids, 2, BLK))],
         [pltpu.VMEM((blocks, pixels, BLK), BF16)],
-        2 * pixels * blocks * BLK * mids * BLK,
+        4 * pixels * blocks * BLK * mids * BLK,
         comm,
-    )(expanded, sums, params, up, upsums, weight, grouped, gsums, gparams)
-
-
-def weight_grad_kernel(left_ref, right_ref, out_ref):
-    weight_grad_block(left_ref[0], right_ref, out_ref, 0)
-
-
-def weight_grad(left, right):
-    blocks, pixels, _ = left.shape
-    width = right.shape[1]
-    return call(
-        weight_grad_kernel,
-        (blocks,),
-        [block(pixels, BLK), whole(pixels, width)],
-        [block(BLK, width)],
-        [shape((blocks, BLK, width), BF16)],
-        [],
-        2 * pixels * blocks * BLK * width,
-    )(left, right)[0]
-
-
-def first_back(count, red_ref, sums_ref, prm_ref, rup_ref, rupsums_ref, back_ref):
+    )(expanded, sums, params, up, upsums, weight, grouped, gsums, gparams, act)
+
+
+def first_back(count, red_ref, sums_ref, prm_ref, rup_ref, rupsums_ref, back_ref, loads=()):
     mids, pixels, _ = red_ref.shape
     for mid in range(mids):
+        for load in loads[2 * mid : 2 * mid + 2]:
+            load.wait()
         coef = coefficients(sums_ref[mid], prm_ref[mid], count)
         scale = coef[2] * coef[1]
         up_mean = rupsums_ref[mid, 0:1] / count
@@ -923,38 +913,52 @@
 
 
 class Reduce:
-    def __init__(self, part, out, row, me, across, refs):
-        self.part, self.out, self.row, self.across = part, out, row, across
+    def __init__(self, part, out, row, me, refs, source=None):
+        self.part, self.out, self.row = part, out, row
+        self.source = part if source is None else source
         self.height, self.side = me // 2, me % 2
-        self.first, self.held, self.pair, self.line, self.second, self.total = refs[:6]
-        self.s1, self.r1, self.s2, self.r2, self.s3, self.r3, self.s4, self.r4 = refs[6:]
+        self.place, self.core = row // 2, row % 2
+        self.fresh, self.chip, self.cross, self.held, self.pair, self.line, self.second, self.total = refs[:8]
+        self.send, self.recv = refs[8:]
         self.levels = self.held.shape[0]
         self.size = self.total.shape[0]
+        self.near = (self.place * 2 + 1 - self.core, me)
+        self.far = ((1 - self.place) * 2 + self.core, me)
         self.peer = (row, self.height * 2 + 1 - self.side)
         self.along = [(row, lax.rem(me + 2 * step, 2 * self.levels)) for step in range(1, self.levels)]
 
     def rows(self, row):
         return pl.ds(pl.multiple_of(row * self.size, 16), self.size)
 
-    def over_batch(self):
+    def copy(self, source, target, index, device):
+        return remote(source, target, self.send.at[index], self.recv.at[index], device)
+
+    def over_cores(self):
         return [
-            remote(
-                self.part.at[:, self.rows(device[0])], self.first.at[step], self.s1.at[step], self.r1.at[step], device
-            )
-            for step, device in enumerate(self.across)
+            self.copy(self.source.at[:, self.rows(2 * place + 1 - self.core)], self.fresh.at[place], place, self.near)
+            for place in range(2)
         ]
 
-    def add_batch(self):
+    def add_cores(self):
+        @pl.loop(0, 2 * self.levels)
+        def _(member):
+            for place in range(2):
+                total = self.part[member, self.rows(2 * place + self.core)].astype(F32)
+                self.chip[place, member] = (total + self.fresh[place, member].astype(F32)).astype(BF16)
+
+    def over_x(self):
+        return [self.copy(self.chip.at[1 - self.place], self.cross, 2, self.far)]
+
+    def add_x(self):
         @pl.loop(0, self.levels)
         def _(level):
             for side in range(2):
-                total = self.part[2 * level + side, self.rows(self.row)].astype(F32)
-                for step in range(len(self.across)):
-                    total += self.first[step, 2 * level + side].astype(F32)
+                member = 2 * level + side
+                total = self.chip[self.place, member].astype(F32) + self.cross[member].astype(F32)
                 self.held[level, side] = total.astype(BF16)
 
     def over_pair(self):
-        return [remote(self.held.at[:, 1 - self.side], self.pair, self.s2.at[0], self.r2.at[0], self.peer)]
+        return [self.copy(self.held.at[:, 1 - self.side], self.pair, 3, self.peer)]
 
     def add_pair(self):
         @pl.loop(0, self.levels)
@@ -964,7 +968,7 @@
 
     def over_line(self):
         return [
-            remote(self.line.at[device[1] // 2], self.second.at[step], self.s3.at[step], self.r3.at[step], device)
+            self.copy(self.line.at[device[1] // 2], self.second.at[step], 4 + step, device)
             for step, device in enumerate(self.along)
         ]
 
@@ -974,52 +978,57 @@
             total += self.second[step].astype(F32)
         self.total[...] = total
 
-    def share(self):
-        rows = self.rows(self.row)
-        copies = [
-            remote(self.total, self.out.at[rows], self.s4.at[step], self.r4.at[step], device)
-            for step, device in enumerate(self.across)
-        ]
-        return copies + [pltpu.make_async_copy(self.total, self.out.at[rows], self.s4.at[len(self.across)])]
+    def keep(self):
+        return [pltpu.make_async_copy(self.total, self.out.at[self.rows(self.row)], self.send.at[10])]
+
+    def share_x(self):
+        return [self.copy(self.total, self.out.at[self.rows(self.row)], 7, self.far)]
+
+    def share_cores(self):
+        own = self.copy(self.total, self.out.at[self.rows(self.row)], 8, self.near)
+        rows = self.rows((1 - self.place) * 2 + self.core)
+        return [own, self.copy(self.out.at[rows], self.out.at[rows], 9, self.near)]
 
 
 def reduce_scratch(dims, batches, members):
     rows, columns = dims[1] // batches, dims[2]
     levels = members // 2
-    dma = pltpu.SemaphoreType.DMA
     return [
-        pltpu.VMEM((batches - 1, members, rows, columns), BF16),
+        pltpu.VMEM((2, members, rows, columns), BF16),
+        pltpu.VMEM((2, members, rows, columns), BF16),
+        pltpu.VMEM((members, rows, columns), BF16),
         pltpu.VMEM((levels, 2, rows, columns), BF16),
         pltpu.VMEM((levels, rows, columns), BF16),
         pltpu.VMEM((levels, rows, columns), BF16),
         pltpu.VMEM((levels - 1, rows, columns), BF16),
         pltpu.VMEM((rows, columns), F32),
-        dma((batches - 1,)),
-        dma((batches - 1,)),
-        dma((1,)),
-        dma((1,)),
-        dma((levels - 1,)),
-        dma((levels - 1,)),
-        dma((batches,)),
-        dma((batches - 1,)),
+        pltpu.SemaphoreType.DMA((11,)),
+        pltpu.SemaphoreType.DMA((10,)),
     ]
 
 
 HELD_BACK = 2
+EARLY = 3
+
+
+def closing_steps(step, members):
+    late = jnp.maximum(step - members, EARLY)
+    return jnp.where(step < EARLY, step, late), jnp.clip(step - EARLY, 0, members - 1)
 
 
 def closing_kernel(count, batches, members, low, size, *refs):
     red_ref, sums_ref, prm_ref, rup_ref, rupsums_ref, x_ref, up_ref, w_ref, epart_ref, tpart_ref, src_ref, _ = refs[:12]
     recv_ref, rout_ref, eout_ref, tout_ref, dst_ref = refs[12:17]
     back_ref, grad_ref, wpart_ref, gsend, grecv, psend, precv = refs[17:24]
+    red_held, rup_held, epart_held, load_sem = refs[54:]
     row, me, across, along = devices(batches, members)
     step = pl.program_id(0)
     last = members - 1
-    expand_sum = Reduce(epart_ref, eout_ref, row, me, across, refs[24:38])
-    taps_sum = Reduce(tpart_ref, tout_ref, row, me, across, refs[38:52])
-    reduce_sum = Reduce(wpart_ref, rout_ref, row, me, across, refs[52:66])
+    expand_sum = Reduce(epart_held, eout_ref, row, me, refs[24:34], epart_ref)
+    taps_sum = Reduce(tpart_ref, tout_ref, row, me, refs[34:44])
+    reduce_sum = Reduce(wpart_ref, rout_ref, row, me, refs[44:54])
     parts = (expand_sum, taps_sum, reduce_sum)
-    other = lax.rem(me + 1 + step, members)
+    grad_step, weight_step = closing_steps(step, members)
 
     def pieces():
         return piece_copies(src_ref, dst_ref, low, size, me, along, psend, precv)
@@ -1027,53 +1036,94 @@
     def send(index):
         device = (row, lax.rem(me + 1 + index, members))
         return remote(grad_ref.at[index], recv_ref.at[me], gsend.at[index], grecv.at[index], device)
+
+    mids = red_held.shape[0]
+    load_part = pltpu.make_async_copy(epart_ref, epart_held, load_sem.at[2 * mids])
 
     @pl.when(step == 0)
     def _():
         greet(across + along)
         each(pieces(), "start")
-        each(expand_sum.over_batch(), "start")
-        each(taps_sum.over_batch(), "start")
-        first_back(count, red_ref, sums_ref, prm_ref, rup_ref, rupsums_ref, back_ref)
-
-    def product(start, size):
-        part = pl.ds(start, size)
-        total = dot(back_ref[part], w_ref[0], ((1,), (1,)))
-        grad_ref[step, part] = (up_ref[0, part] + total).astype(BF16)
-
-    over_rows(x_ref.shape[1], product)
-
-    @pl.when(step < last - HELD_BACK)
+        loads = []
+        for mid in range(mids):
+            for which, (source, held) in enumerate(((red_ref, red_held), (rup_ref, rup_held))):
+                loads.append(pltpu.make_async_copy(source.at[mid], held.at[mid], load_sem.at[2 * mid + which]))
+        each(loads, "start")
+        load_part.start()
+        each(expand_sum.over_cores(), "start")
+        each(taps_sum.over_cores(), "start")
+        first_back(count, red_held, sums_ref, prm_ref, rup_held, rupsums_ref, back_ref, loads)
+
+    weight_turn = (step >= EARLY) & (step < EARLY + members)
+
+    @pl.when(weight_turn)
     def _():
-        send(step).start()
-
-    weight_grad_block(x_ref[0], back_ref, wpart_ref, other)
-
-    @pl.when(step == last)
+        weight_grad_block(x_ref[0], back_ref, wpart_ref, lax.rem(me + 1 + weight_step, members))
+
+    @pl.when(jnp.logical_not(weight_turn))
+    def _():
+        def product(start, size):
+            part = pl.ds(start, size)
+            total = dot(back_ref[part], w_ref[0], ((1,), (1,)))
+            grad_ref[grad_step, part] = (up_ref[0, part] + total).astype(BF16)
+
+        over_rows(x_ref.shape[1], product)
+
+        @pl.when(grad_step < last - HELD_BACK)
+        def _():
+            send(grad_step).start()
+
+    @pl.when(step == EARLY)
+    def _():
+        load_part.wait()
+        for part in parts[:2]:
+            each(part.over_cores(), "wait")
+            part.add_cores()
+            each(part.over_x(), "start")
+
+    @pl.when(step == EARLY + members - 1)
+    def _():
+        each(reduce_sum.over_cores(), "start")
+        for part in parts[:2]:
+            each(part.over_x(), "wait")
+            part.add_x()
+            each(part.over_pair(), "start")
+
+    @pl.when(step == EARLY + members)
+    def _():
+        each(reduce_sum.over_cores(), "wait")
+        reduce_sum.add_cores()
+        each(reduce_sum.over_x(), "start")
+
+    @pl.when(step == 2 * members - 1)
     def _():
         own = pltpu.make_async_copy(grad_ref.at[last], recv_ref.at[me], gsend.at[last])
         own.start()
-        each(reduce_sum.over_batch(), "start")
-        for part in parts:
-            each(part.over_batch(), "wait")
-            part.add_batch()
-            each(part.over_pair(), "start")
-        for part in parts:
+        for part in parts[:2]:
             each(part.over_pair(), "wait")
             part.add_pair()
             each(part.over_line(), "start")
+        each(reduce_sum.over_x(), "wait")
+        reduce_sum.add_x()
+        each(reduce_sum.over_pair(), "start")
+        each(reduce_sum.over_pair(), "wait")
+        reduce_sum.add_pair()
+        each(reduce_sum.over_line(), "start")
         for index in range(last - HELD_BACK, last):
             send(index).start()
         for part in parts:
             each(part.over_line(), "wait")
             part.add_line()
-            each(part.share(), "start")
+            each(part.share_x() + part.keep(), "start")
+        for part in parts:
+            each(part.share_x(), "wait")
+            each(part.share_cores(), "start")
         own.wait()
         each(pieces(), "wait")
         for index in range(last):
             send(index).wait()
         for part in parts:
-            each(part.share(), "wait")
+            each(part.share_cores() + part.keep(), "wait")
 
 
 def closing(
@@ -1086,7 +1136,12 @@
     def keep(*dims):
         return pl.BlockSpec(dims, lambda j: (0,) * len(dims), pipeline_mode=once)
 
-    turn_block = functools.partial(turned_block, members)
+    def turn_block(which, *dims):
+        def index(j):
+            return (lax.rem(lax.axis_index("group") + 1 + closing_steps(j, members)[which], members),) + (0,) * len(dims)
+
+        return pl.BlockSpec((1,) + dims, index)
+
     anywhere = pl.BlockSpec(memory_space=pl.ANY)
     dma = pltpu.SemaphoreType.DMA
     wdims = (blocks, BLK, mids * BLK)
@@ -1101,19 +1156,25 @@
     ]
     for dims in (wdims, tpart.shape, wdims):
         scratch += reduce_scratch(dims, batches, members)
+    scratch += [
+        pltpu.VMEM((mids, pixels, BLK), F32),
+        pltpu.VMEM((mids, pixels, BLK), F32),
+        pltpu.VMEM(wdims, BF16),
+        dma((2 * mids + 1,)),
+    ]
     return pl.pallas_call(
         functools.partial(closing_kernel, count, batches, members, low, size),
-        grid=(blocks,),
+        grid=(2 * blocks,),
         in_specs=[
-            keep(mids, pixels, BLK),
+            anywhere,
             keep(mids, 2, BLK),
             keep(mids, 2, BLK),
-            keep(mids, pixels, BLK),
+            anywhere,
             keep(mids, 2, BLK),
-            turn_block(pixels, BLK),
-            turn_block(pixels, BLK),
-            turn_block(BLK, mids * BLK),
-            keep(*wdims),
+            turn_block(1, pixels, BLK),
+            turn_block(0, pixels, BLK),
+            turn_block(0, BLK, mids * BLK),
+            anywhere,
             keep(*tpart.shape),
             anywhere,
             anywhere,
@@ -1132,23 +1193,69 @@
     )(reduced, sums, params, rup, rupsums, x, up, weight, epart, tpart, source, into)
 
 
-def turn_out_kernel(in_ref, out_ref):
-    for first in range(0, in_ref.shape[0], HALF):
-        out_ref[:, first : first + HALF] = in_ref[first : first + HALF].astype(out_ref.dtype).T
-
-
-def turn_out(values, dtype):
-    rows, channels = values.shape
-    size = next(part for part in (1792, 896, HALF) if rows % part == 0)
+def turn_out_kernel(first_ref, second_ref, first_out, second_out):
+    own = lax.broadcasted_iota(jnp.int32, (BLK, BLK), 0) == lax.broadcasted_iota(jnp.int32, (BLK, BLK), 1)
+    identity = jnp.where(own, 1.0, 0.0).astype(BF16)
+    half = pl.num_programs(0) // 2
+
+    def turn_part(in_ref, out_ref):
+        for low in range(0, in_ref.shape[0], HALF):
+            part = dot(identity, in_ref[low : low + HALF], ((1,), (1,)))
+            out_ref[:, low : low + HALF] = part.astype(out_ref.dtype)
+
+    @pl.when(pl.program_id(0) < half)
+    def _():
+        turn_part(first_ref, first_out)
+
+    @pl.when(pl.program_id(0) >= half)
+    def _():
+        turn_part(second_ref, second_out)
+
+
+def turn_out(first, second):
+    rows, channels = first.shape
+    parts = 2
+    size = rows // parts
+
+    def early(j):
+        return jnp.minimum(j, parts - 1)
+
+    def late(j):
+        return jnp.maximum(j - parts, 0)
+
     return call(
         turn_out_kernel,
-        (rows // size,),
-        [pl.BlockSpec((size, channels), lambda j: (j, 0))],
-        [pl.BlockSpec((channels, size), lambda j: (0, j))],
-        [shape((channels, rows), dtype)],
+        (2 * parts,),
+        [
+            pl.BlockSpec((size, channels), lambda j: (early(j), 0)),
+            pl.BlockSpec((size, channels), lambda j: (late(j), 0)),
+        ],
+        [
+            pl.BlockSpec((channels, size), lambda j: (0, early(j))),
+            pl.BlockSpec((channels, size), lambda j: (0, late(j))),
+        ],
+        [shape((channels, rows)), shape((channels, rows), BF16)],
         [],
-        rows * channels,
-    )(values)[0]
+        4 * rows * channels * BLK,
+    )(first, second)
+
+
+def own_kernel(reduce_ref, group_ref, expand_ref, *outs):
+    me = lax.axis_index("group")
+    half = pl.ds(pl.multiple_of((me % 2) * HALF, HALF), HALF)
+    for index, stats_ref in enumerate((reduce_ref, group_ref)):
+        for which in range(2):
+            outs[2 * index + 1 - which][...] = stats_ref[me // 2, which : which + 1, half]
+    for which in range(2):
+        outs[5 - which][...] = expand_ref[me, which : which + 1]
+
+
+def own_parts(reduce_stats, group_stats, expand_stats):
+    sizes = (HALF,) * 4 + (BLK,) * 2
+    outs = pl.pallas_call(own_kernel, out_shape=[shape((1, size)) for size in sizes])(
+        reduce_stats, group_stats, expand_stats
+    )
+    return tuple(out.reshape(-1) for out in outs)
 
 
 def pixel_masks(pixels):
@@ -1182,7 +1289,6 @@
     channels, row_pixels = block_input.shape
     pixels = row_pixels // members
     count = row_pixels * batches
-    local_mid = reduce_gain.shape[0]
     vectors = [reduce_gain, reduce_bias, group_gain, group_bias, expand_gain, expand_bias]
     taps = group_weight.reshape(-1, 9, GW, GW).transpose(1, 2, 0, 3).reshape(9 * GW, HALF)
     taps = jnp.pad(taps, ((0, TAP_ROWS - 9 * GW), (0, 0)))
@@ -1195,17 +1301,16 @@
     expand_params = packs[:, 4:].reshape(-1, 2, BLK)
 
     comm = functools.partial(Comm, batches, members)
-    beside = (64, 48)
-    sends = comm(1, grad_turned, 0, (336,) + beside)
+    sends = comm(1, grad_turned, 0, (208, 240))
     reduced, reduce_sums, grad = reduce_product(x, reduce_full, sends)
-    sends = comm(2, grad_turned, sends.high, (448,) + beside, grad)
+    sends = comm(2, grad_turned, sends.high, (336, 224), grad)
     grouped, group_sums, grad = conv(reduced, reduce_sums, reduce_params, taps_full, masks, count, sends)
-    sends = comm(3, grad_turned, sends.high, (pixels - sends.high - sum(beside),) + beside, grad)
+    sends = comm(3, grad_turned, sends.high, (pixels - sends.high - 224, 224), grad)
     expanded, act, expand_sums, grad = expand_product(grouped, group_sums, group_params, expand_full, count, sends)
-    sends = comm(4, None, 0, (224,) + beside, None, True)
+    sends = comm(4, None, 0, (224, 112), None, True)
     out, upstream, expand_stats, moved = output(expanded, expand_sums, expand_params, x, grad, count, sends)
-    sends = comm(5, out, sends.high, (304,) + beside, moved)
-    back, group_up, group_stats, moved = expand_back(
+    sends = comm(5, out, sends.high, (384, 96), moved)
+    expand_part, group_up, group_stats, moved = expand_back(
         expanded,
         expand_sums,
         expand_params,
@@ -1215,11 +1320,12 @@
         grouped,
         group_sums,
         group_params,
+        act,
         count,
         sends,
     )
-    sends = comm(6, out, sends.high, (560,) + beside, moved)
-    expand_part, reduce_up, taps_part, reduce_stats, moved = conv_back(
+    sends = comm(6, out, sends.high, (496, 112), moved)
+    reduce_up, taps_part, reduce_stats, moved = conv_back(
         reduced,
         reduce_sums,
         reduce_params,
@@ -1232,7 +1338,6 @@
         masks,
         count,
         sends,
-        (back, act),
     )
     inner, reduce_weight_grad, expand_weight_grad, taps_grad, moved = closing(
         reduced,
@@ -1253,8 +1358,7 @@
         batches,
         members,
     )
-    block_output = turn_out(moved.reshape(row_pixels, channels), BF16)
-    input_grad = turn_out(inner.reshape(row_pixels, channels), F32)
+    input_grad, block_output = turn_out(inner.reshape(row_pixels, channels), moved.reshape(row_pixels, channels))
     taps_grad = taps_grad[: 9 * GW].reshape(9, GW, -1, GW).transpose(2, 0, 3, 1)
     return (
         block_output,
@@ -1262,13 +1366,7 @@
         reduce_weight_grad,
         taps_grad.reshape(group_weight.shape),
         expand_weight_grad,
-        own_part(reduce_stats, 1, local_mid),
-        own_part(reduce_stats, 0, local_mid),
-        own_part(group_stats, 1, local_mid),
-        own_part(group_stats, 0, local_mid),
-        own_part(expand_stats, 1, channels),
-        own_part(expand_stats, 0, channels),
-    )
+    ) + own_parts(reduce_stats, group_stats, expand_stats)
 
 
 def modular(
@@ -1340,10 +1438,9 @@
     expand_sums = exchange(expand_sums, batches, members, 2)
     out, upstream, expand_stats = output(expanded, expand_sums, expand_params, x, grad, count, None)
     expand_stats = exchange(expand_stats, batches, members, 2)
-    back, group_up, group_stats = expand_back(
-        expanded, expand_sums, expand_params, upstream, expand_stats, expand_full, grouped, group_sums, group_params, count, None
+    expand_part, group_up, group_stats = expand_back(
+        expanded, expand_sums, expand_params, upstream, expand_stats, expand_full, grouped, group_sums, group_params, act, count, None
     )
-    expand_part = weight_grad(back, act)
     group_stats = exchange(group_stats, batches, members, 1)
     reduce_up, taps_part, reduce_stats = conv_back(
         reduced,

time: 734 us -> 709 us (0.966)
  Pallas kernels: 716 us -> 699 us
    pallas_call x8 -> x7, Pallas kernels: 367 us -> 356 us  [plain_call(): pl.pallas_call(kernel, grid=grid, in_specs=in_specs, out_specs=out_specs,...]
    pallas_call x1, Pallas kernels: 199 us -> 191 us  [closing(): pl.pallas_call(functools.partial(closing_kernel, count, batches, members,...]
where the time goes in v4:
time: 709 us; the launch traced here: 708 us
  Pallas kernels  699 us (99%)
  local copies, waits for them, and re-layouts  8.26 us (1%)
    pallas_call x7, Pallas kernels, plain_call(): pl.pallas_call(kernel, grid=grid, in_specs=in_specs, out_specs=out_specs,...  356 us
    pallas_call x1, Pallas kernels, closing(): pl.pallas_call(functools.partial(closing_kernel, count, batches, members,...  191 us
    pallas_call x1, Pallas kernels, opening(): pl.pallas_call(functools.partial(opening_kernel, batches, members), in_sp...  151 us

profile of v4, /device:TPU:25, one launch (start us, length us, event | category | flops | bytes accessed | tf_op | source)
XLA Modules:
  0.0 708.0 jit_solution(15726904218806459517)
XLA Ops:
  0.6 1.1 copy.33
  1.8 0.2 reshape.77
  1.9 0.6 pad.4.refs_4_
  2.6 150.7 %shard_map.203 = (bf16[8,1568,256]{2,1,0:T(8,128)(2,1)}, bf16[8,1568,256]{2,1,0:T(8,128)(2,1)}, bf16[4,2,256,1024]{3,2,1,0:T(8,128)(2,1)}, bf16[4,2,256,1024]{3,...) custom-call(bf16[256,12544]{1,0:T(8,128)(2,1)} %refs_0_.1, bf16[256,12544]{1,0:T(8,128)(2,1)} %refs_1_.1, ...), custom_call_target="tpu_custom_call" | custom-call | tf_op jit(solution)/shard_map/pallas_call | solution.py:882
  153.3 0.8 fusion
  154.1 0.6 reshape.83.refs_2_
  154.8 0.6 fusion.1
  155.4 61.6 %shard_map.204 = (f32[4,1568,256]{2,1,0:T(8,128)}, f32[4,2,256]{2,1,0:T(2,128)}, bf16[8,1568,256]{2,1,0:T(8,128)(2,1)}) custom-call(bf16[8,1568,256]{2,1,0:T(8,128)(2,1)} %get-tuple-element.52.refs_0_.refs_3_.refs_5_, bf16[8,256,1024]{2,1,0:T(8,128)(2,1)} %bitcast.25, bf16[8,1568,256]{2,1,0:T(8,128)(2,1)} %get-tuple-element.54.refs_2_.refs_5_.refs_4_), custom_call_target="tpu_custom_call" | custom-call | flops 6576668672 | bytes 20000000 | tf_op jit(solution)/shard_map/pallas_call | solution.py:266
  217.0 57.8 %shard_map.205 = (f32[4,1568,256]{2,1,0:T(8,128)}, f32[4,2,256]{2,1,0:T(2,128)}, bf16[8,1568,256]{2,1,0:T(8,128)(2,1)}) custom-call(f32[4,1568,256]{2,1,0:T(8,128)} %get-tuple-element.55.refs_0_, f32[4,2,256]{2,1,0:T(2,128)} %get-tuple-element.56.refs_1_, f32[4,2,256]{2,1,0:T(2,128)} %get-tuple-element.96.refs_2_, ...), custom_call_target="tpu_custom_call", output_to_operand_aliasing={{2}: (6, {})} | custom-call | flops 7398752256 | bytes 20000000 | tf_op jit(solution)/shard_map/pallas_call | solution.py:266
  274.8 58.3 %shard_map.206 = (f32[8,1568,256]{2,1,0:T(8,128)}, bf16[1568,1024]{1,0:T(8,128)(2,1)}, f32[8,2,256]{2,1,0:T(2,128)}, bf16[8,1568,256]{2,1,0:T(8,128)(2,1)}) custom-call(f32[4,1568,256]{2,1,0:T(8,128)} %get-tuple-element.60.refs_0_.refs_6_.refs_3_, f32[4,2,256]{2,1,0:T(2,128)} %get-tuple-element.61.refs_1_.refs_7_.refs_4_, ...), custom_call_target="tpu_custom_call", output_to_operand_aliasing={{3}: (5, {})} | custom-call | flops 6576668672 | bytes 20000000 | tf_op jit(solution)/shard_map/pallas_call | solution.py:266
  333.1 45.6 %shard_map.207 = (bf16[8,1568,256]{2,1,0:T(8,128)(2,1)}, f32[8,1568,256]{2,1,0:T(8,128)}, f32[8,2,256]{2,1,0:T(2,128)}, bf16[8,1568,256]{2,1,0:T(8,128)(2,1)}) custom-call(f32[8,1568,256]{2,1,0:T(8,128)} %get-tuple-element.64.refs_0_, f32[8,2,256]{2,1,0:T(2,128)} %get-tuple-element.65.refs_1_, f32[8,2,256]{2,1,0:T(2,128)} %reshape.83.refs_2_, ...), custom_call_target="tpu_custom_call" | custom-call | flops 64225280 | bytes 20000000 | tf_op jit(solution)/shard_map/pallas_call | solution.py:266
  378.7 53.9 %shard_map.208 = (bf16[8,256,1024]{2,1,0:T(8,128)(2,1)}, f32[4,1568,256]{2,1,0:T(8,128)}, f32[4,2,256]{2,1,0:T(2,128)}, bf16[8,1568,256]{2,1,0:T(8,128)(2,1)}) custom-call(f32[8,1568,256]{2,1,0:T(8,128)} %get-tuple-element.64.refs_0_, f32[8,2,256]{2,1,0:T(2,128)} %get-tuple-element.65.refs_1_, ...), custom_call_target="tpu_custom_call", output_to_operand_aliasing={{3}: (11, {})} | custom-call | flops 13153337344 | bytes 20000000 | tf_op jit(solution)/shard_map/pallas_call | solution.py:266
  432.7 63.4 %shard_map.209 = (f32[4,1568,256]{2,1,0:T(8,128)}, bf16[8,320,128]{2,1,0:T(8,128)(2,1)}, f32[4,2,256]{2,1,0:T(2,128)}, bf16[8,1568,256]{2,1,0:T(8,128)(2,1)}) custom-call(f32[4,1568,256]{2,1,0:T(8,128)} %get-tuple-element.55.refs_0_, f32[4,2,256]{2,1,0:T(2,128)} %get-tuple-element.56.refs_1_, ...), custom_call_target="tpu_custom_call", output_to_operand_aliasing={{3}: (11, {})} | custom-call | flops 14797504512 | bytes 20000000 | tf_op jit(solution)/shard_map/pallas_call | solution.py:266
  496.1 1.3 shard_map.212
  497.4 191.2 %shard_map.210 = (bf16[8,1568,256]{2,1,0:T(8,128)(2,1)}, f32[256,1024]{1,0:T(8,128)}, f32[256,1024]{1,0:T(8,128)}, f32[320,128]{1,0:T(8,128)}, bf16[8,1568,256]{2,1,0:T(8,128)(2,1)}) custom-call(f32[4,1568,256]{2,1,0:T(8,128)} %get-tuple-element.55.refs_0_, f32[4,2,256]{2,1,0:T(2,128)} %get-tuple-element.56.refs_1_, ...), custom_call_target="tpu_custom_call", output_to_operand_aliasing={{4}: (11, {})} | custom-call | tf_op jit(solution)/shard_map/pallas_call | solution.py:1165
  688.6 0.9 slice.19
  689.5 0.3 reshape.86
  689.8 1.1 copy.30
  690.9 0.0 copy-start.1
  690.9 0.0 copy-start
  690.9 15.2 %shard_map.211 = (f32[256,12544]{1,0:T(8,128)}, bf16[256,12544]{1,0:T(8,128)(2,1)}) custom-call(bf16[12544,256]{1,0:T(8,128)(2,1)} %bitcast.22, bf16[12544,256]{1,0:T(8,128)(2,1)} %bitcast.21), custom_call_target="tpu_custom_call" | custom-call | flops 3288334336 | bytes 20000000 | tf_op jit(solution)/shard_map/pallas_call | solution.py:266
  706.1 0.0 copy-done.1
  706.1 1.0 copy.42
  707.1 0.0 copy-done
  707.1 1.0 copy.43
  (2 shorter events, 0.0 us)
Async XLA Ops:
  690.9 15.2 %copy-start.1 = (f32[256,1024]{1,0:T(8,128)S(1)}, f32[256,1024]{1,0:T(8,128)}, u32[]{:S(2)}) copy-start(f32[256,1024]{1,0:T(8,128)} %get-tuple-element.110) | copy-start | bytes 3145732
  690.9 16.2 %copy-start = (f32[256,1024]{1,0:T(8,128)S(1)}, f32[256,1024]{1,0:T(8,128)}, u32[]{:S(2)}) copy-start(f32[256,1024]{1,0:T(8,128)} %get-tuple-element.112) | copy-start | bytes 3145732

commit v5 on v4

--- a/solution.py
+++ b/solution.py
@@ -60,8 +60,31 @@
     ref[slot, 1:2] += jnp.sum(second, 0, keepdims=True)
 
 
+PHASE_START = [0]
+
+
+def grid_step():
+    return pl.program_id(0) - PHASE_START[-1]
+
+
+def in_phase(start, steps, body):
+    step = pl.program_id(0)
+
+    @pl.when((step >= start) & (step < start + steps))
+    def _():
+        PHASE_START.append(start)
+        try:
+            body()
+        finally:
+            PHASE_START.pop()
+
+
+def phase_block(start, steps, *dims):
+    return pl.BlockSpec((1,) + dims, lambda j: (jnp.clip(j - start, 0, steps - 1),) + (0,) * len(dims))
+
+
 def clear_stats(ref):
-    @pl.when(pl.program_id(0) == 0)
+    @pl.when(grid_step() == 0)
     def _():
         ref[...] = jnp.zeros_like(ref)
 
@@ -297,7 +320,7 @@
 
 def reduce_kernel(x_ref, w_ref, out_ref, sum_ref):
     clear_stats(sum_ref)
-    slot = pl.program_id(0)
+    slot = grid_step()
 
     def body(start, size):
         rows = pl.ds(start, size)
@@ -391,7 +414,7 @@
 
     over_rows(pixels, enter)
     clear_stats(stat_ref)
-    slot = pl.program_id(0)
+    slot = grid_step()
 
     def body(start, size):
         total = conv_rows(stack_ref, mask_ref, dense_ref, start, size)
@@ -457,7 +480,7 @@
 
     over_rows(pixels, back)
     clear_stats(stat_ref)
-    slot = pl.program_id(0)
+    slot = grid_step()
 
     def body(start, size):
         rows = pl.ds(start, size)
@@ -518,7 +541,7 @@
 def expand_kernel(count, grp_ref, gsums_ref, gprm_ref, w_ref, out_ref, act_ref, sum_ref):
     mids, pixels, _ = grp_ref.shape
 
-    @pl.when(pl.program_id(0) == 0)
+    @pl.when(grid_step() == 0)
     def _():
         for mid in range(mids):
             coef = coefficients(gsums_ref[mid], gprm_ref[mid], count)
@@ -531,7 +554,7 @@
             over_rows(pixels, body)
 
     clear_stats(sum_ref)
-    slot = pl.program_id(0)
+    slot = grid_step()
 
     def product(start, size):
         rows = pl.ds(start, size)
@@ -565,7 +588,7 @@
 def output_kernel(count, members, exp_ref, sums_ref, prm_ref, x_ref, grad_ref, out_ref, up_ref, stat_ref):
     coef = coefficients(sums_ref[0], prm_ref[0], count)
     clear_stats(stat_ref)
-    slot = pl.program_id(0)
+    slot = grid_step()
     if members:
         slot = lax.rem(lax.axis_index("group") + 1 + slot, members)
 
@@ -616,7 +639,7 @@
     keep_ref,
 ):
     blocks, pixels, _ = keep_ref.shape
-    step = pl.program_id(0)
+    step = grid_step()
     clear_stats(stat_ref)
 
     @pl.when(step < blocks)
@@ -763,6 +786,344 @@
         scratch_shapes=stats_scratch(values.shape, batches, members),
         compiler_params=pltpu.CompilerParams(collective_id=collective_id, has_side_effects=True),
     )(values)
+
+
+class Sends:
+    def __init__(self, source, target, low, sizes, me, along, send, recv):
+        self.parts = []
+        for part, size in enumerate(sizes):
+            self.parts.append(
+                functools.partial(
+                    piece_copies, source, target, low, size, me, along, send.at[part], recv.at[part]
+                )
+            )
+            low += size
+
+    def start(self, part):
+        each(self.parts[part](), "start")
+
+    def wait(self):
+        for part in self.parts:
+            each(part(), "wait")
+
+
+def at_step(step, body):
+    pl.when(pl.program_id(0) == step)(body)
+
+
+def forward_kernel(count, batches, members, sizes, *refs):
+    x_any, wr_ref, prm_ref, taps_ref, masks_any, gprm_ref, we_ref, src_ref = refs[:8]
+    red_any, grp_any, act_any, exp_ref, sums_ref, gsums_ref, esums_ref, dst_ref = refs[8:16]
+    x_held, masks, red, grp, act, stack, dense, psend, precv, load, keep = refs[16:27]
+    stats = [refs[27 + 7 * index : 34 + 7 * index] for index in range(3)]
+    row, me, across, along = devices(batches, members)
+    mids, blocks = red.shape[0], x_held.shape[0]
+    second, third, end = mids, 2 * mids, 2 * mids + blocks
+    sends = Sends(src_ref, dst_ref, 0, sizes, me, along, psend, precv)
+    loads = [pltpu.make_async_copy(x_any, x_held, load.at[0]), pltpu.make_async_copy(masks_any, masks, load.at[1])]
+    kept = [
+        pltpu.make_async_copy(held, out, keep.at[index])
+        for index, (held, out) in enumerate(((red, red_any), (grp, grp_any), (act, act_any)))
+    ]
+
+    def begin():
+        greet(across + along)
+        sends.start(0)
+        each(loads, "start")
+        each(loads, "wait")
+
+    at_step(0, begin)
+
+    def product():
+        reduce_kernel(x_held, wr_ref, red.at[pl.ds(grid_step(), 1)], sums_ref)
+
+    in_phase(0, mids, product)
+
+    def exchange_first():
+        kept[0].start()
+        total_stats(sums_ref, across, along, *stats[0], beside=sends.parts[1]())
+        sends.start(2)
+
+    at_step(second - 1, exchange_first)
+
+    def conv_phase():
+        own = pl.ds(grid_step(), 1)
+        conv_kernel(
+            count, red.at[own], sums_ref.at[own], prm_ref, taps_ref, masks, grp.at[own], gsums_ref, stack, dense
+        )
+
+    in_phase(second, mids, conv_phase)
+
+    def exchange_second():
+        kept[1].start()
+        total_stats(gsums_ref, across, along, *stats[1], beside=sends.parts[3]())
+        sends.start(4)
+
+    at_step(third - 1, exchange_second)
+    in_phase(third, blocks, lambda: expand_kernel(count, grp, gsums_ref, gprm_ref, we_ref, exp_ref, act, esums_ref))
+
+    def finish():
+        kept[2].start()
+        total_stats(esums_ref, across, along, *stats[2], beside=sends.parts[5]())
+        each(kept, "wait")
+        sends.wait()
+
+    at_step(end - 1, finish)
+
+
+def forward(x, reduce_full, reduce_params, taps, masks, group_params, expand_full, source, sizes, count, batches, members):
+    blocks, pixels, _ = x.shape
+    mid_total = reduce_full.shape[2]
+    mids = mid_total // BLK
+    anywhere = pl.BlockSpec(memory_space=pl.ANY)
+    dma = pltpu.SemaphoreType.DMA
+    mid_dims, sum_dims = (mids, pixels, BLK), (mids, 2, BLK)
+    scratch = [
+        pltpu.VMEM(x.shape, BF16),
+        pltpu.VMEM(masks.shape, F32),
+        pltpu.VMEM(mid_dims, F32),
+        pltpu.VMEM(mid_dims, F32),
+        pltpu.VMEM((pixels, mid_total), BF16),
+        pltpu.VMEM((3, 2, pixels + 2 * PAD, HALF), F32),
+        pltpu.VMEM((9, BLK, BLK), BF16),
+        dma((len(sizes), members)),
+        dma((len(sizes), members - 1)),
+        dma((2,)),
+        dma((3,)),
+    ]
+    for dims in (sum_dims, sum_dims, (blocks, 2, BLK)):
+        scratch += stats_scratch(dims, batches, members)
+    return pl.pallas_call(
+        functools.partial(forward_kernel, count, batches, members, sizes),
+        grid=(2 * mids + blocks,),
+        in_specs=[
+            anywhere,
+            pl.BlockSpec((blocks, BLK, BLK), lambda j: (0, 0, jnp.minimum(j, mids - 1))),
+            phase_block(mids, mids, 2, BLK),
+            pl.BlockSpec((2,) + taps.shape[1:], lambda j: (jnp.clip(j - mids, 0, mids - 1), 0, 0)),
+            anywhere,
+            whole(*sum_dims),
+            phase_block(2 * mids, blocks, BLK, mid_total),
+            anywhere,
+        ],
+        out_specs=[
+            anywhere,
+            anywhere,
+            anywhere,
+            phase_block(2 * mids, blocks, pixels, BLK),
+            whole(*sum_dims),
+            whole(*sum_dims),
+            whole(blocks, 2, BLK),
+            anywhere,
+        ],
+        out_shape=[
+            shape(mid_dims),
+            shape(mid_dims),
+            shape((pixels, mid_total), BF16),
+            shape(x.shape),
+            shape(sum_dims),
+            shape(sum_dims),
+            shape((blocks, 2, BLK)),
+            shape(source.shape, BF16),
+        ],
+        scratch_shapes=scratch,
+        compiler_params=pltpu.CompilerParams(vmem_limit_bytes=VMEM_LIMIT, collective_id=1, has_side_effects=True),
+    )(x, reduce_full, reduce_params, taps, masks, group_params, expand_full, source)
+
+
+def backward_kernel(count, batches, members, low, sizes, *refs):
+    exp_ref, esums_ref, eprm_ref, up_ref, upsums_ref, we_ref, grp_ref, gsums_ref, gprm_ref = refs[:9]
+    red_ref, sums_ref, prm_ref, taps_ref, act_any, masks_any, src_ref, _ = refs[9:17]
+    epart_ref, rup_ref, tpart_ref, gstats_ref, rstats_ref, dst_ref = refs[17:23]
+    keep, gup, act, masks, stack, dense, back, psend, precv, load = refs[23:33]
+    stats = [refs[33 + 7 * index : 40 + 7 * index] for index in range(2)]
+    row, me, across, along = devices(batches, members)
+    blocks, mids = keep.shape[0], gup.shape[0]
+    middle, second, end = blocks, blocks + mids, blocks + 2 * mids
+    sends = Sends(src_ref, dst_ref, low, sizes, me, along, psend, precv)
+    loads = [pltpu.make_async_copy(act_any, act, load.at[0]), pltpu.make_async_copy(masks_any, masks, load.at[1])]
+
+    def begin():
+        greet(across + along)
+        sends.start(0)
+        each(loads, "start")
+        each(loads, "wait")
+
+    at_step(0, begin)
+
+    def expand_phase():
+        place = jnp.clip(grid_step() - middle, 0, mids - 1)
+        expand_back_kernel(
+            count,
+            exp_ref,
+            esums_ref,
+            eprm_ref,
+            up_ref,
+            upsums_ref,
+            we_ref,
+            grp_ref,
+            gsums_ref,
+            gprm_ref,
+            act,
+            epart_ref,
+            gup.at[pl.ds(place, 1)],
+            gstats_ref,
+            keep,
+        )
+
+    in_phase(0, second, expand_phase)
+
+    def exchange_first():
+        total_stats(gstats_ref, across, along, *stats[0], beside=sends.parts[1]())
+        sends.start(2)
+
+    at_step(second - 1, exchange_first)
+
+    def conv_phase():
+        own = pl.ds(grid_step(), 1)
+        conv_back_kernel(
+            count,
+            red_ref,
+            sums_ref,
+            prm_ref,
+            grp_ref,
+            gsums_ref,
+            gprm_ref,
+            gup.at[own],
+            gstats_ref.at[own],
+            taps_ref,
+            masks,
+            rup_ref,
+            tpart_ref,
+            rstats_ref,
+            stack,
+            dense,
+            back,
+        )
+
+    in_phase(second, mids, conv_phase)
+
+    def finish():
+        total_stats(rstats_ref, across, along, *stats[1], beside=sends.parts[3]())
+        sends.wait()
+
+    at_step(end - 1, finish)
+
+
+def backward(
+    expanded,
+    esums,
+    eparams,
+    up,
+    upsums,
+    expand_full,
+    grouped,
+    gsums,
+    gparams,
+    reduced,
+    sums,
+    params,
+    taps,
+    act,
+    masks,
+    source,
+    into,
+    low,
+    sizes,
+    count,
+    batches,
+    members,
+):
+    blocks, pixels, _ = expanded.shape
+    mids = grouped.shape[0]
+    mid_total = mids * BLK
+    anywhere = pl.BlockSpec(memory_space=pl.ANY)
+    dma = pltpu.SemaphoreType.DMA
+    second = blocks + mids
+
+    def both(*dims):
+        def index(j):
+            return (jnp.where(j < second, jnp.maximum(j - blocks, 0), j - second),) + (0,) * len(dims)
+
+        return pl.BlockSpec((1,) + dims, index)
+
+    first = functools.partial(phase_block, 0, blocks)
+    last = functools.partial(phase_block, second, mids)
+    pairs = pl.BlockSpec((2,) + taps.shape[1:], lambda j: (jnp.clip(j - second, 0, mids - 1), 0, 0))
+    scratch = [
+        pltpu.VMEM((blocks, pixels, BLK), BF16),
+        pltpu.VMEM((mids, pixels, BLK), F32),
+        pltpu.VMEM((pixels, mid_total), BF16),
+        pltpu.VMEM(masks.shape, F32),
+        pltpu.VMEM((3, 2, pixels + 2 * PAD, HALF), F32),
+        pltpu.VMEM((9, BLK, BLK), BF16),
+        pltpu.VMEM((3, pixels, BLK), BF16),
+        dma((len(sizes), members)),
+        dma((len(sizes), members - 1)),
+        dma((2,)),
+    ]
+    for _ in range(2):
+        scratch += stats_scratch((mids, 2, BLK), batches, members)
+    return pl.pallas_call(
+        functools.partial(backward_kernel, count, batches, members, low, sizes),
+        grid=(second + mids,),
+        in_specs=[
+            first(pixels, BLK),
+            first(2, BLK),
+            first(2, BLK),
+            first(pixels, BLK),
+            first(2, BLK),
+            pl.BlockSpec((blocks, BLK, BLK), lambda j: (0, 0, jnp.clip(j - blocks, 0, mids - 1))),
+            both(pixels, BLK),
+            both(2, BLK),
+            both(2, BLK),
+            last(pixels, BLK),
+            last(2, BLK),
+            last(2, BLK),
+            pairs,
+            anywhere,
+            anywhere,
+            anywhere,
+            anywhere,
+        ],
+        out_specs=[
+            first(BLK, mid_total),
+            last(pixels, BLK),
+            pairs,
+            whole(mids, 2, BLK),
+            whole(mids, 2, BLK),
+            anywhere,
+        ],
+        out_shape=[
+            shape((blocks, BLK, mid_total), BF16),
+            shape((mids, pixels, BLK)),
+            shape(taps.shape, BF16),
+            shape((mids, 2, BLK)),
+            shape((mids, 2, BLK)),
+            shape(source.shape, BF16),
+        ],
+        scratch_shapes=scratch,
+        input_output_aliases={16: 5},
+        compiler_params=pltpu.CompilerParams(vmem_limit_bytes=VMEM_LIMIT, collective_id=5, has_side_effects=True),
+    )(
+        expanded,
+        esums,
+        eparams,
+        up,
+        upsums,
+        expand_full,
+        grouped,
+        gsums,
+        gparams,
+        reduced,
+        sums,
+        params,
+        taps,
+        act,
+        masks,
+        source,
+        into,
+    )
 
 
 def turn(source_ref, target_ref, slot, chunk):
@@ -1300,17 +1661,25 @@
     reduce_params, group_params = vectors[:, :2], vectors[:, 2:]
     expand_params = packs[:, 4:].reshape(-1, 2, BLK)
 
-    comm = functools.partial(Comm, batches, members)
-    sends = comm(1, grad_turned, 0, (208, 240))
-    reduced, reduce_sums, grad = reduce_product(x, reduce_full, sends)
-    sends = comm(2, grad_turned, sends.high, (336, 224), grad)
-    grouped, group_sums, grad = conv(reduced, reduce_sums, reduce_params, taps_full, masks, count, sends)
-    sends = comm(3, grad_turned, sends.high, (pixels - sends.high - 224, 224), grad)
-    expanded, act, expand_sums, grad = expand_product(grouped, group_sums, group_params, expand_full, count, sends)
-    sends = comm(4, None, 0, (224, 112), None, True)
+    sizes = (208, 240, 304, 240, 304)
+    reduced, grouped, act, expanded, reduce_sums, group_sums, expand_sums, grad = forward(
+        x,
+        reduce_full,
+        reduce_params,
+        taps_full,
+        masks,
+        group_params,
+        expand_full,
+        grad_turned,
+        sizes + (pixels - sum(sizes),),
+        count,
+        batches,
+        members,
+    )
+    sends = Comm(batches, members, 4, None, 0, (176, 64), None, True)
     out, upstream, expand_stats, moved = output(expanded, expand_sums, expand_params, x, grad, count, sends)
-    sends = comm(5, out, sends.high, (384, 96), moved)
-    expand_part, group_up, group_stats, moved = expand_back(
+    sizes = (480, 144, 448, 112)
+    expand_part, reduce_up, taps_part, group_stats, reduce_stats, moved = backward(
         expanded,
         expand_sums,
         expand_params,
@@ -1320,25 +1689,21 @@
         grouped,
         group_sums,
         group_params,
-        act,
-        count,
-        sends,
-    )
-    sends = comm(6, out, sends.high, (496, 112), moved)
-    reduce_up, taps_part, reduce_stats, moved = conv_back(
         reduced,
         reduce_sums,
         reduce_params,
-        grouped,
-        group_sums,
-        group_params,
-        group_up,
-        group_stats,
         taps_full,
+        act,
         masks,
+        out,
+        moved,
+        sends.high,
+        sizes,
         count,
-        sends,
+        batches,
+        members,
     )
+    high = sends.high + sum(sizes)
     inner, reduce_weight_grad, expand_weight_grad, taps_grad, moved = closing(
         reduced,
         reduce_sums,
@@ -1352,8 +1717,8 @@
         taps_part,
         out,
         moved,
-        sends.high,
-        pixels - sends.high,
+        high,
+        pixels - high,
         count,
         batches,
         members,

time: 709 us -> 690 us (0.973)
  Pallas kernels: 699 us -> 681 us
    pallas_call x7 -> x2, Pallas kernels: 356 us -> 55.2 us  [plain_call(): pl.pallas_call(kernel, grid=grid, in_specs=in_specs, out_specs=out_specs,...]
    pallas_call x0 -> x2, Pallas kernels: none -> 282 us  [the longest x1 165 us: forward(): pl.pallas_call(functools.partial(forward_kernel, count, batches, members,...]
where the time goes in v5:
time: 690 us
  Pallas kernels  681 us (99%)
  local copies, waits for them, and re-layouts  8.26 us (1%)
    pallas_call x1, Pallas kernels, closing(): pl.pallas_call(functools.partial(closing_kernel, count, batches, members,...  192 us
    pallas_call x1, Pallas kernels, forward(): pl.pallas_call(functools.partial(forward_kernel, count, batches, members,...  165 us
    pallas_call x1, Pallas kernels, opening(): pl.pallas_call(functools.partial(opening_kernel, batches, members), in_sp...  151 us
    pallas_call x1, Pallas kernels, backward(): pl.pallas_call(functools.partial(backward_kernel, count, batches, members...  116 us
    pallas_call x2, Pallas kernels, plain_call(): pl.pallas_call(kernel, grid=grid, in_specs=in_specs, out_specs=out_specs,...  55.2 us

profile of v5, /device:TPU:25, one launch (start us, length us, event | category | flops | bytes accessed | tf_op | source)
XLA Modules:
  0.0 689.7 jit_solution(13074580091670065275)
XLA Ops:
  0.6 1.1 copy.30
  1.8 0.2 reshape.77
  1.9 0.6 pad.4.refs_4_
  2.6 150.7 %shard_map.203 = (bf16[8,1568,256]{2,1,0:T(8,128)(2,1)}, bf16[8,1568,256]{2,1,0:T(8,128)(2,1)}, bf16[4,2,256,1024]{3,2,1,0:T(8,128)(2,1)}, bf16[4,2,256,1024]{3,...) custom-call(bf16[256,12544]{1,0:T(8,128)(2,1)} %refs_0_.1, bf16[256,12544]{1,0:T(8,128)(2,1)} %refs_1_.1, ...), custom_call_target="tpu_custom_call" | custom-call | tf_op jit(solution)/shard_map/pallas_call | solution.py:1243
  153.3 0.8 fusion
  154.1 0.6 reshape.83.refs_2_
  154.8 0.6 fusion.1
  155.4 165.5 %shard_map.204 = (f32[4,1568,256]{2,1,0:T(8,128)}, f32[4,1568,256]{2,1,0:T(8,128)}, bf16[1568,1024]{1,0:T(8,128)(2,1)}, f32[8,1568,256]{2,1,0:T(8,128)}, f32[4,2...) custom-call(bf16[8,1568,256]{2,1,0:T(8,128)(2,1)} %get-tuple-element.48.refs_0_.refs, ...), custom_call_target="tpu_custom_call" | custom-call | tf_op jit(solution)/shard_map/pallas_call | solution.py:896
  320.9 40.0 %shard_map.205 = (bf16[8,1568,256]{2,1,0:T(8,128)(2,1)}, f32[8,1568,256]{2,1,0:T(8,128)}, f32[8,2,256]{2,1,0:T(2,128)}, bf16[8,1568,256]{2,1,0:T(8,128)(2,1)}) custom-call(f32[8,1568,256]{2,1,0:T(8,128)} %get-tuple-element.56.refs_0_, f32[8,2,256]{2,1,0:T(2,128)} %get-tuple-element.57.refs_1_, f32[8,2,256]{2,1,0:T(2,128)} %reshape.83.refs_2_, ...), custom_call_target="tpu_custom_call" | custom-call | flops 64225280 | bytes 20000000 | tf_op jit(solution)/shard_map/pallas_call | solution.py:289
  360.9 116.3 %shard_map.206 = (bf16[8,256,1024]{2,1,0:T(8,128)(2,1)}, f32[4,1568,256]{2,1,0:T(8,128)}, bf16[8,320,128]{2,1,0:T(8,128)(2,1)}, f32[4,2,256]{2,1,0:T(2,128)}, f3...) custom-call(f32[8,1568,256]{2,1,0:T(8,128)} %get-tuple-element.56.refs_0_, ...), custom_call_target="tpu_custom_call", output_to_operand_aliasing={{5}: (16, {})} | custom-call | tf_op jit(solution)/shard_map/pallas_call | solution.py:1067
  477.2 1.3 shard_map.209
  478.5 191.8 %shard_map.207 = (bf16[8,1568,256]{2,1,0:T(8,128)(2,1)}, f32[256,1024]{1,0:T(8,128)}, f32[256,1024]{1,0:T(8,128)}, f32[320,128]{1,0:T(8,128)}, bf16[8,1568,256]{2,1,0:T(8,128)(2,1)}) custom-call(f32[4,1568,256]{2,1,0:T(8,128)} %get-tuple-element.54.refs_9_.refs_0_, ...), custom_call_target="tpu_custom_call", output_to_operand_aliasing={{4}: (11, {})} | custom-call | tf_op jit(solution)/shard_map/pallas_call | solution.py:1526
  670.3 0.9 slice.19
  671.3 0.3 reshape.86
  671.6 1.1 copy.27
  672.6 0.0 copy-start.1
  672.6 0.0 copy-start
  672.6 15.2 %shard_map.208 = (f32[256,12544]{1,0:T(8,128)}, bf16[256,12544]{1,0:T(8,128)(2,1)}) custom-call(bf16[12544,256]{1,0:T(8,128)(2,1)} %bitcast.26, bf16[12544,256]{1,0:T(8,128)(2,1)} %bitcast.21), custom_call_target="tpu_custom_call" | custom-call | flops 3288334336 | bytes 20000000 | tf_op jit(solution)/shard_map/pallas_call | solution.py:289
  687.8 0.0 copy-done.1
  687.8 1.0 copy.36
  688.8 0.0 copy-done
  688.8 1.0 copy.37
  (2 shorter events, 0.0 us)
Async XLA Ops:
  672.6 15.2 %copy-start.1 = (f32[256,1024]{1,0:T(8,128)S(1)}, f32[256,1024]{1,0:T(8,128)}, u32[]{:S(2)}) copy-start(f32[256,1024]{1,0:T(8,128)} %get-tuple-element.102) | copy-start | bytes 3145732
  672.6 16.2 %copy-start = (f32[256,1024]{1,0:T(8,128)S(1)}, f32[256,1024]{1,0:T(8,128)}, u32[]{:S(2)}) copy-start(f32[256,1024]{1,0:T(8,128)} %get-tuple-element.104) | copy-start | bytes 3145732

commit v6 on v5

--- a/solution.py
+++ b/solution.py
@@ -1368,7 +1368,7 @@
     ]
 
 
-HELD_BACK = 2
+HELD_BACK = 4
 EARLY = 3
 
 
@@ -1460,6 +1460,7 @@
     def _():
         own = pltpu.make_async_copy(grad_ref.at[last], recv_ref.at[me], gsend.at[last])
         own.start()
+        send(last - HELD_BACK).start()
         for part in parts[:2]:
             each(part.over_pair(), "wait")
             part.add_pair()
@@ -1470,7 +1471,7 @@
         each(reduce_sum.over_pair(), "wait")
         reduce_sum.add_pair()
         each(reduce_sum.over_line(), "start")
-        for index in range(last - HELD_BACK, last):
+        for index in range(last - HELD_BACK + 1, last):
             send(index).start()
         for part in parts:
             each(part.over_line(), "wait")
@@ -1554,54 +1555,7 @@
     )(reduced, sums, params, rup, rupsums, x, up, weight, epart, tpart, source, into)
 
 
-def turn_out_kernel(first_ref, second_ref, first_out, second_out):
-    own = lax.broadcasted_iota(jnp.int32, (BLK, BLK), 0) == lax.broadcasted_iota(jnp.int32, (BLK, BLK), 1)
-    identity = jnp.where(own, 1.0, 0.0).astype(BF16)
-    half = pl.num_programs(0) // 2
-
-    def turn_part(in_ref, out_ref):
-        for low in range(0, in_ref.shape[0], HALF):
-            part = dot(identity, in_ref[low : low + HALF], ((1,), (1,)))
-            out_ref[:, low : low + HALF] = part.astype(out_ref.dtype)
-
-    @pl.when(pl.program_id(0) < half)
-    def _():
-        turn_part(first_ref, first_out)
-
-    @pl.when(pl.program_id(0) >= half)
-    def _():
-        turn_part(second_ref, second_out)
-
-
-def turn_out(first, second):
-    rows, channels = first.shape
-    parts = 2
-    size = rows // parts
-
-    def early(j):
-        return jnp.minimum(j, parts - 1)
-
-    def late(j):
-        return jnp.maximum(j - parts, 0)
-
-    return call(
-        turn_out_kernel,
-        (2 * parts,),
-        [
-            pl.BlockSpec((size, channels), lambda j: (early(j), 0)),
-            pl.BlockSpec((size, channels), lambda j: (late(j), 0)),
-        ],
-        [
-            pl.BlockSpec((channels, size), lambda j: (0, early(j))),
-            pl.BlockSpec((channels, size), lambda j: (0, late(j))),
-        ],
-        [shape((channels, rows)), shape((channels, rows), BF16)],
-        [],
-        4 * rows * channels * BLK,
-    )(first, second)
-
-
-def own_kernel(reduce_ref, group_ref, expand_ref, *outs):
+def own_parts(reduce_ref, group_ref, expand_ref, outs):
     me = lax.axis_index("group")
     half = pl.ds(pl.multiple_of((me % 2) * HALF, HALF), HALF)
     for index, stats_ref in enumerate((reduce_ref, group_ref)):
@@ -1611,12 +1565,58 @@
         outs[5 - which][...] = expand_ref[me, which : which + 1]
 
 
-def own_parts(reduce_stats, group_stats, expand_stats):
+def turn_out_kernel(first_ref, second_ref, reduce_ref, group_ref, expand_ref, first_out, second_out, *outs):
+    own = lax.broadcasted_iota(jnp.int32, (BLK, BLK), 0) == lax.broadcasted_iota(jnp.int32, (BLK, BLK), 1)
+    identity = jnp.where(own, 1.0, 0.0).astype(BF16)
+    half = pl.num_programs(0) // 2
+
+    @pl.when(pl.program_id(0) == 0)
+    def _():
+        own_parts(reduce_ref, group_ref, expand_ref, outs)
+
+    def turn_part(in_ref, out_ref):
+        for low in range(0, in_ref.shape[0], HALF):
+            part = dot(identity, in_ref[low : low + HALF], ((1,), (1,)))
+            out_ref[:, low : low + HALF] = part.astype(out_ref.dtype)
+
+    @pl.when(pl.program_id(0) < half)
+    def _():
+        turn_part(first_ref, first_out)
+
+    @pl.when(pl.program_id(0) >= half)
+    def _():
+        turn_part(second_ref, second_out)
+
+
+def turn_out(first, second, stats):
     sizes = (HALF,) * 4 + (BLK,) * 2
-    outs = pl.pallas_call(own_kernel, out_shape=[shape((1, size)) for size in sizes])(
-        reduce_stats, group_stats, expand_stats
-    )
-    return tuple(out.reshape(-1) for out in outs)
+    rows, channels = first.shape
+    parts = 2
+    size = rows // parts
+
+    def early(j):
+        return jnp.minimum(j, parts - 1)
+
+    def late(j):
+        return jnp.maximum(j - parts, 0)
+
+    return call(
+        turn_out_kernel,
+        (2 * parts,),
+        [
+            pl.BlockSpec((size, channels), lambda j: (early(j), 0)),
+            pl.BlockSpec((size, channels), lambda j: (late(j), 0)),
+        ]
+        + [whole(*part.shape) for part in stats],
+        [
+            pl.BlockSpec((channels, size), lambda j: (0, early(j))),
+            pl.BlockSpec((channels, size), lambda j: (0, late(j))),
+        ]
+        + [whole(1, width) for width in sizes],
+        [shape((channels, rows)), shape((channels, rows), BF16)] + [shape((1, width)) for width in sizes],
+        [],
+        4 * rows * channels * BLK,
+    )(first, second, *stats)
 
 
 def pixel_masks(pixels):
@@ -1676,9 +1676,9 @@
         batches,
         members,
     )
-    sends = Comm(batches, members, 4, None, 0, (176, 64), None, True)
+    sends = Comm(batches, members, 4, None, 0, (208, 112), None, True)
     out, upstream, expand_stats, moved = output(expanded, expand_sums, expand_params, x, grad, count, sends)
-    sizes = (480, 144, 448, 112)
+    sizes = (416, 144, 432, 112)
     expand_part, reduce_up, taps_part, group_stats, reduce_stats, moved = backward(
         expanded,
         expand_sums,
@@ -1723,7 +1723,11 @@
         batches,
         members,
     )
-    input_grad, block_output = turn_out(inner.reshape(row_pixels, channels), moved.reshape(row_pixels, channels))
+    input_grad, block_output, *sums = turn_out(
+        inner.reshape(row_pixels, channels),
+        moved.reshape(row_pixels, channels),
+        (reduce_stats, group_stats, expand_stats),
+    )
     taps_grad = taps_grad[: 9 * GW].reshape(9, GW, -1, GW).transpose(2, 0, 3, 1)
     return (
         block_output,
@@ -1731,7 +1735,7 @@
         reduce_weight_grad,
         taps_grad.reshape(group_weight.shape),
         expand_weight_grad,
-    ) + own_parts(reduce_stats, group_stats, expand_stats)
+    ) + tuple(part.reshape(-1) for part in sums)
 
 
 def modular(

time: 690 us -> 687 us (level); the launches traced: 690 us -> 677 us
  Pallas kernels: 681 us -> 668 us
    pallas_call x1, Pallas kernels: 192 us -> 182 us  [closing(): pl.pallas_call(functools.partial(closing_kernel, count, batches, members,...]
    pallas_call x1, Pallas kernels: 116 us -> 109 us  [backward(): pl.pallas_call(functools.partial(backward_kernel, count, batches, members...]
where the time goes in v6:
time: 687 us; the launch traced here: 677 us
  Pallas kernels  668 us (97%)
  local copies, waits for them, and re-layouts  8.26 us (1%)
    pallas_call x1, Pallas kernels, closing(): pl.pallas_call(functools.partial(closing_kernel, count, batches, members,...  182 us
    pallas_call x1, Pallas kernels, forward(): pl.pallas_call(functools.partial(forward_kernel, count, batches, members,...  165 us
    pallas_call x1, Pallas kernels, opening(): pl.pallas_call(functools.partial(opening_kernel, batches, members), in_sp...  151 us
    pallas_call x1, Pallas kernels, backward(): pl.pallas_call(functools.partial(backward_kernel, count, batches, members...  109 us
    pallas_call x2, Pallas kernels, plain_call(): pl.pallas_call(kernel, grid=grid, in_specs=in_specs, out_specs=out_specs,...  61.1 us

profile of v6, /device:TPU:25, one launch (start us, length us, event | category | flops | bytes accessed | tf_op | source)
XLA Modules:
  0.0 677.3 jit_solution(2108385582342728667)
XLA Ops:
  0.6 1.1 copy.30
  1.8 0.2 reshape.77
  1.9 0.6 pad.4.refs_4_
  2.6 150.7 %shard_map.203 = (bf16[8,1568,256]{2,1,0:T(8,128)(2,1)}, bf16[8,1568,256]{2,1,0:T(8,128)(2,1)}, bf16[4,2,256,1024]{3,2,1,0:T(8,128)(2,1)}, bf16[4,2,256,1024]{3,...) custom-call(bf16[256,12544]{1,0:T(8,128)(2,1)} %refs_0_.1, bf16[256,12544]{1,0:T(8,128)(2,1)} %refs_1_.1, ...), custom_call_target="tpu_custom_call" | custom-call | tf_op jit(solution)/shard_map/pallas_call | solution.py:1243
  153.3 0.8 fusion
  154.1 0.6 reshape.83.refs_2_
  154.8 0.6 fusion.1
  155.4 165.4 %shard_map.204 = (f32[4,1568,256]{2,1,0:T(8,128)}, f32[4,1568,256]{2,1,0:T(8,128)}, bf16[1568,1024]{1,0:T(8,128)(2,1)}, f32[8,1568,256]{2,1,0:T(8,128)}, f32[4,2...) custom-call(bf16[8,1568,256]{2,1,0:T(8,128)(2,1)} %get-tuple-element.48.refs_0_.refs, ...), custom_call_target="tpu_custom_call" | custom-call | tf_op jit(solution)/shard_map/pallas_call | solution.py:896
  320.8 45.8 %shard_map.205 = (bf16[8,1568,256]{2,1,0:T(8,128)(2,1)}, f32[8,1568,256]{2,1,0:T(8,128)}, f32[8,2,256]{2,1,0:T(2,128)}, bf16[8,1568,256]{2,1,0:T(8,128)(2,1)}) custom-call(f32[8,1568,256]{2,1,0:T(8,128)} %get-tuple-element.56.refs_0_, f32[8,2,256]{2,1,0:T(2,128)} %get-tuple-element.57.refs_1_, f32[8,2,256]{2,1,0:T(2,128)} %reshape.83.refs_2_, ...), custom_call_target="tpu_custom_call" | custom-call | flops 64225280 | bytes 20000000 | tf_op jit(solution)/shard_map/pallas_call | solution.py:289
  366.7 109.2 %shard_map.206 = (bf16[8,256,1024]{2,1,0:T(8,128)(2,1)}, f32[4,1568,256]{2,1,0:T(8,128)}, bf16[8,320,128]{2,1,0:T(8,128)(2,1)}, f32[4,2,256]{2,1,0:T(2,128)}, f3...) custom-call(f32[8,1568,256]{2,1,0:T(8,128)} %get-tuple-element.56.refs_0_, ...), custom_call_target="tpu_custom_call", output_to_operand_aliasing={{5}: (16, {})} | custom-call | tf_op jit(solution)/shard_map/pallas_call | solution.py:1067
  475.9 181.9 %shard_map.207 = (bf16[8,1568,256]{2,1,0:T(8,128)(2,1)}, f32[256,1024]{1,0:T(8,128)}, f32[256,1024]{1,0:T(8,128)}, f32[320,128]{1,0:T(8,128)}, bf16[8,1568,256]{2,1,0:T(8,128)(2,1)}) custom-call(f32[4,1568,256]{2,1,0:T(8,128)} %get-tuple-element.54.refs_9_.refs_0_, ...), custom_call_target="tpu_custom_call", output_to_operand_aliasing={{4}: (11, {})} | custom-call | tf_op jit(solution)/shard_map/pallas_call | solution.py:1527
  657.8 0.9 slice.19
  658.7 0.3 reshape.86
  659.0 1.1 copy.27
  660.1 0.0 copy-start.1
  660.1 0.0 copy-start
  660.1 15.2 %shard_map.208 = (f32[256,12544]{1,0:T(8,128)}, bf16[256,12544]{1,0:T(8,128)(2,1)}, f32[1,128]{1,0:T(1,128)}, f32[1,128]{1,0:T(1,128)}, f32[1,128]{1,0:T(1,128)}...) custom-call(bf16[12544,256]{1,0:T(8,128)(2,1)} %bitcast.26, bf16[12544,256]{1,0:T(8,128)(2,1)} %bitcast.21, ...), custom_call_target="tpu_custom_call" | custom-call | flops 3288334336 | bytes 20000000 | tf_op jit(solution)/shard_map/pallas_call | solution.py:289
  675.3 0.0 copy-done.1
  675.3 1.0 copy.36
  676.3 0.0 copy-done
  676.3 1.0 copy.37
  (2 shorter events, 0.0 us)
Async XLA Ops:
  660.1 15.2 %copy-start.1 = (f32[256,1024]{1,0:T(8,128)S(1)}, f32[256,1024]{1,0:T(8,128)}, u32[]{:S(2)}) copy-start(f32[256,1024]{1,0:T(8,128)} %get-tuple-element.102) | copy-start | bytes 3145732
  660.1 16.2 %copy-start = (f32[256,1024]{1,0:T(8,128)S(1)}, f32[256,1024]{1,0:T(8,128)}, u32[]{:S(2)}) copy-start(f32[256,1024]{1,0:T(8,128)} %get-tuple-element.104) | copy-start | bytes 3145732

commit v7 on v6

--- a/solution.py
+++ b/solution.py
@@ -1661,7 +1661,7 @@
     reduce_params, group_params = vectors[:, :2], vectors[:, 2:]
     expand_params = packs[:, 4:].reshape(-1, 2, BLK)
 
-    sizes = (208, 240, 304, 240, 304)
+    sizes = (256, 240, 336, 240, 304)
     reduced, grouped, act, expanded, reduce_sums, group_sums, expand_sums, grad = forward(
         x,
         reduce_full,

time: 687 us -> 686 us (level)
  no operation moved by 1% of the time
where the time goes in v7:
time: 686 us; the launch traced here: 676 us
  Pallas kernels  667 us (97%)
  local copies, waits for them, and re-layouts  8.26 us (1%)
    pallas_call x1, Pallas kernels, closing(): pl.pallas_call(functools.partial(closing_kernel, count, batches, members,...  181 us
    pallas_call x1, Pallas kernels, forward(): pl.pallas_call(functools.partial(forward_kernel, count, batches, members,...  166 us
    pallas_call x1, Pallas kernels, opening(): pl.pallas_call(functools.partial(opening_kernel, batches, members), in_sp...  151 us
    pallas_call x1, Pallas kernels, backward(): pl.pallas_call(functools.partial(backward_kernel, count, batches, members...  109 us
    pallas_call x2, Pallas kernels, plain_call(): pl.pallas_call(kernel, grid=grid, in_specs=in_specs, out_specs=out_specs,...  59.9 us

profile of v7, /device:TPU:25, one launch (start us, length us, event | category | flops | bytes accessed | tf_op | source)
XLA Modules:
  0.0 676.0 jit_solution(13873667800284414514)
XLA Ops:
  0.6 1.1 copy.30
  1.8 0.2 reshape.77
  1.9 0.6 pad.4.refs_4_
  2.6 150.7 %shard_map.203 = (bf16[8,1568,256]{2,1,0:T(8,128)(2,1)}, bf16[8,1568,256]{2,1,0:T(8,128)(2,1)}, bf16[4,2,256,1024]{3,2,1,0:T(8,128)(2,1)}, bf16[4,2,256,1024]{3,...) custom-call(bf16[256,12544]{1,0:T(8,128)(2,1)} %refs_0_.1, bf16[256,12544]{1,0:T(8,128)(2,1)} %refs_1_.1, ...), custom_call_target="tpu_custom_call" | custom-call | tf_op jit(solution)/shard_map/pallas_call | solution.py:1243
  153.3 0.8 fusion
  154.1 0.6 reshape.83.refs_2_
  154.8 0.6 fusion.1
  155.4 166.0 %shard_map.204 = (f32[4,1568,256]{2,1,0:T(8,128)}, f32[4,1568,256]{2,1,0:T(8,128)}, bf16[1568,1024]{1,0:T(8,128)(2,1)}, f32[8,1568,256]{2,1,0:T(8,128)}, f32[4,2...) custom-call(bf16[8,1568,256]{2,1,0:T(8,128)(2,1)} %get-tuple-element.48.refs_0_.refs, ...), custom_call_target="tpu_custom_call" | custom-call | tf_op jit(solution)/shard_map/pallas_call | solution.py:896
  321.4 44.7 %shard_map.205 = (bf16[8,1568,256]{2,1,0:T(8,128)(2,1)}, f32[8,1568,256]{2,1,0:T(8,128)}, f32[8,2,256]{2,1,0:T(2,128)}, bf16[8,1568,256]{2,1,0:T(8,128)(2,1)}) custom-call(f32[8,1568,256]{2,1,0:T(8,128)} %get-tuple-element.56.refs_0_, f32[8,2,256]{2,1,0:T(2,128)} %get-tuple-element.57.refs_1_, f32[8,2,256]{2,1,0:T(2,128)} %reshape.83.refs_2_, ...), custom_call_target="tpu_custom_call" | custom-call | flops 64225280 | bytes 20000000 | tf_op jit(solution)/shard_map/pallas_call | solution.py:289
  366.1 109.4 %shard_map.206 = (bf16[8,256,1024]{2,1,0:T(8,128)(2,1)}, f32[4,1568,256]{2,1,0:T(8,128)}, bf16[8,320,128]{2,1,0:T(8,128)(2,1)}, f32[4,2,256]{2,1,0:T(2,128)}, f3...) custom-call(f32[8,1568,256]{2,1,0:T(8,128)} %get-tuple-element.56.refs_0_, ...), custom_call_target="tpu_custom_call", output_to_operand_aliasing={{5}: (16, {})} | custom-call | tf_op jit(solution)/shard_map/pallas_call | solution.py:1067
  475.5 181.1 %shard_map.207 = (bf16[8,1568,256]{2,1,0:T(8,128)(2,1)}, f32[256,1024]{1,0:T(8,128)}, f32[256,1024]{1,0:T(8,128)}, f32[320,128]{1,0:T(8,128)}, bf16[8,1568,256]{2,1,0:T(8,128)(2,1)}) custom-call(f32[4,1568,256]{2,1,0:T(8,128)} %get-tuple-element.54.refs_9_.refs_0_, ...), custom_call_target="tpu_custom_call", output_to_operand_aliasing={{4}: (11, {})} | custom-call | tf_op jit(solution)/shard_map/pallas_call | solution.py:1527
  656.5 0.9 slice.19
  657.4 0.3 reshape.86
  657.7 1.1 copy.27
  658.8 0.0 copy-start.1
  658.8 0.0 copy-start
  658.8 15.2 %shard_map.208 = (f32[256,12544]{1,0:T(8,128)}, bf16[256,12544]{1,0:T(8,128)(2,1)}, f32[1,128]{1,0:T(1,128)}, f32[1,128]{1,0:T(1,128)}, f32[1,128]{1,0:T(1,128)}...) custom-call(bf16[12544,256]{1,0:T(8,128)(2,1)} %bitcast.26, bf16[12544,256]{1,0:T(8,128)(2,1)} %bitcast.21, ...), custom_call_target="tpu_custom_call" | custom-call | flops 3288334336 | bytes 20000000 | tf_op jit(solution)/shard_map/pallas_call | solution.py:289
  674.0 0.0 copy-done.1
  674.1 1.0 copy.36
  675.0 0.0 copy-done
  675.0 1.0 copy.37
  (2 shorter events, 0.0 us)
Async XLA Ops:
  658.8 15.2 %copy-start.1 = (f32[256,1024]{1,0:T(8,128)S(1)}, f32[256,1024]{1,0:T(8,128)}, u32[]{:S(2)}) copy-start(f32[256,1024]{1,0:T(8,128)} %get-tuple-element.102) | copy-start | bytes 3145732
  658.8 16.2 %copy-start = (f32[256,1024]{1,0:T(8,128)S(1)}, f32[256,1024]{1,0:T(8,128)}, u32[]{:S(2)}) copy-start(f32[256,1024]{1,0:T(8,128)} %get-tuple-element.104) | copy-start | bytes 3145732
